TPU v7x, 256 devices: a whole 4x4x8 slice. The times are simulated.
256 devices in a mesh: dp: 32 (over x, z_hi, core), seq: 8 (over z_lo, y).
Axes of the slice: x: 4, y: 4, z: 8 (z_hi: 4, z_lo: 2; z = z_hi * 2 + z_lo), core: 2. Of those that a mesh axis runs over, the one named last changes fastest.
Arguments:
- query_rows: bfloat16 [32, 1024, 3072], P('dp', 'seq'), may hold values from -5 to 5
- key_rows: bfloat16 [32, 1024, 3072], P('dp', 'seq'), may hold values from -5 to 5
- value_rows: bfloat16 [32, 1024, 3072], P('dp', 'seq'), may hold values from -6 to 6
- query_tangent: bfloat16 [32, 1024, 3072], P('dp', 'seq'), may hold values from -6 to 6
- key_tangent: bfloat16 [32, 1024, 3072], P('dp', 'seq'), may hold values from -6 to 6
- value_tangent: bfloat16 [32, 1024, 3072], P('dp', 'seq'), may hold values from -6 to 6
- out_weight: bfloat16 [3072, 3072], P('dp'), may hold values from -0.109375 to 0.109375
- gate_scale: float32 [32, 3072], P('dp'), may hold values from -8 to 8
- gate_tangent: float32 [32, 3072], P('dp'), may hold values from -8 to 8
Outputs:
- gated_output: bfloat16 [32, 1024, 3072], P('dp', 'seq')
- output_tangent: bfloat16 [32, 1024, 3072], P('dp', 'seq')
All inputs are finite; a program needn't handle non-finite values.
Results may differ from a plain program's by a relative error of at most 0.008.
Values may be sent and summed in bfloat16 or wider, within the bound.
No kernel may reach another device: no remote copies, remote signals or barrier semaphores. Data moves between devices by JAX's collectives and lax.ppermute only.
A program may use at most 128 MiB of HBM per device.

v0:
```python
import math

import jax
import jax.numpy as jnp
from jax import lax
from jax.experimental import pallas as pl
from jax.experimental.pallas import tpu as pltpu
from jax.sharding import PartitionSpec as P

HEAD_DIM = 128
MIB = 1024 * 1024


def flat(x, z, core, y):
    dp = (x % 4) * 8 + ((z % 8) // 2) * 2 + core
    return dp * 8 + (z % 2) * 4 + y % 4


def moves(target):
    return [
        (flat(x, z, core, y), flat(*target(x, z, core, y)))
        for x in range(4)
        for z in range(8)
        for core in range(2)
        for y in range(4)
    ]


AXES = ("dp", "seq")
NEXT_X = moves(lambda x, z, core, y: (x + 1, z, core, y))
LAST_X = moves(lambda x, z, core, y: (x - 1, z, core, y))
OUTER_Z = moves(lambda x, z, core, y: (x, z + 1 if z % 2 else z - 1, core, y))
INNER_Z = moves(lambda x, z, core, y: (x, z - 1 if z % 2 else z + 1, core, y))
OTHER_CORE = moves(lambda x, z, core, y: (x, z, 1 - core, y))
PLANES = [[x * 8 + pair * 2 + core for x in range(4) for core in range(2)] for pair in range(4)]


def pack_kernel(*refs):
    ins, outs = refs[:6], refs[6:]
    pieces = outs[0].shape[0]
    width = sum(out_ref.shape[3] for out_ref in outs)
    first = 0
    for out_ref in outs:
        share = out_ref.shape[3]
        for piece in range(pieces):
            columns = slice(piece * width + first, piece * width + first + share)
            for at, ref in enumerate(ins):
                out_ref[piece, at] = ref[0, :, columns]
        first += share


def pack(arrays, pieces, shares, block=32):
    rows = arrays[0].shape[1]
    columns = arrays[0].shape[2]
    shapes = [(pieces, len(arrays), rows, share) for share in shares]
    return pl.pallas_call(
        pack_kernel,
        grid=(rows // block,),
        in_specs=[pl.BlockSpec((1, block, columns), lambda i: (0, i, 0)) for _ in arrays],
        out_specs=[
            pl.BlockSpec((pieces, len(arrays), block, share), lambda i: (0, 0, i, 0))
            for share in shares
        ],
        out_shape=[jax.ShapeDtypeStruct(shape, arrays[0].dtype) for shape in shapes],
        cost_estimate=pl.CostEstimate(
            flops=0, bytes_accessed=4 * len(arrays) * rows * columns, transcendentals=0
        ),
        name="pack",
    )(*arrays)


def dot_rows(a, b):
    return lax.dot_general(a, b, (((1,), (1,)), ((), ())), preferred_element_type=jnp.float32)


def attend_kernel(in_ref, *refs):
    out_ref = refs[-1]
    pieces, _, rows, _ = in_ref.shape
    factor = 1.0 / math.sqrt(HEAD_DIM)
    tokens = pieces * rows

    def part(at):
        return in_ref[:, at].reshape(tokens, HEAD_DIM)

    key, value = part(1), part(2)
    keys = jnp.concatenate((key, part(4)), axis=1)
    values = jnp.concatenate((value, part(5)), axis=1)
    step = 2
    for block in range(0, pieces, step):
        which = slice(block, block + step)
        query = in_ref[which, 0].reshape(step * rows, HEAD_DIM)
        query_tan = in_ref[which, 3].reshape(step * rows, HEAD_DIM)
        scores = dot_rows(query, key)
        tangent = dot_rows(jnp.concatenate((query_tan, query), axis=1), keys)
        row_max = jnp.max(scores, axis=1, keepdims=True)
        powers = jnp.exp((scores - row_max) * factor)
        product = powers * tangent
        total = jnp.sum(powers, axis=1, keepdims=True)
        product_sum = jnp.sum(product, axis=1, keepdims=True)
        both = jnp.dot(powers.astype(jnp.bfloat16), values, preferred_element_type=jnp.float32)
        third = jnp.dot(product.astype(jnp.bfloat16), value, preferred_element_type=jnp.float32)
        inverse = 1.0 / total
        attended = both[:, :HEAD_DIM] * inverse
        mean = product_sum * (inverse * factor)
        heads_tan = third * (inverse * factor) + both[:, HEAD_DIM:] * inverse - mean * attended
        out_ref[which, 0] = attended.astype(jnp.bfloat16).reshape(step, rows, HEAD_DIM)
        out_ref[which, 1] = heads_tan.astype(jnp.bfloat16).reshape(step, rows, HEAD_DIM)


def attend(received, first, width, others=None):
    pieces, count, rows, share = received.shape
    heads = share // HEAD_DIM
    tokens = rows * pieces
    kept = [] if others is None else [others]
    return pl.pallas_call(
        attend_kernel,
        grid=(heads,),
        in_specs=[pl.BlockSpec((pieces, count, rows, HEAD_DIM), lambda h: (0, 0, 0, h))]
        + [pl.BlockSpec(memory_space=pl.ANY)] * len(kept),
        out_specs=pl.BlockSpec((pieces, 2, rows, HEAD_DIM), lambda h: (0, 0, 0, h + first)),
        out_shape=jax.ShapeDtypeStruct((pieces, 2, rows, width), jnp.bfloat16),
        input_output_aliases={1: 0} if kept else {},
        compiler_params=pltpu.CompilerParams(vmem_limit_bytes=32 * MIB),
        cost_estimate=pl.CostEstimate(
            flops=heads * 12 * tokens * tokens * HEAD_DIM,
            bytes_accessed=heads * (count + 2) * tokens * HEAD_DIM * 2,
            transcendentals=heads * tokens * tokens,
        ),
        name="attend",
    )(received, *kept)


BLOCK = 512


def project_kernel(place_ref, *refs):
    x_ref, scale_ref, tan_ref, gated_ref, out_tan_ref, all_ref, held_ref, sem = refs[-8:]
    weights = refs[:-8]
    blocks, depth, _ = held_ref.shape
    height = depth // place_ref.shape[0]
    for n in range(blocks):
        at = 0
        for weight in weights:
            for first in range(0, weight.shape[0], height):
                place = pl.ds(pl.multiple_of(place_ref[at] * height, height), height)
                pltpu.make_async_copy(
                    weight.at[pl.ds(first, height), n * BLOCK : (n + 1) * BLOCK],
                    held_ref.at[n, place, :],
                    sem.at[n],
                ).start()
                at += 1
    pieces, _, rows, width = x_ref.shape
    for piece in range(pieces):
        columns = slice(piece * width, (piece + 1) * width)
        all_ref[:rows, columns] = x_ref[piece, 0]
        all_ref[rows:, columns] = x_ref[piece, 1]
    for n in range(blocks):
        pltpu.make_async_copy(held_ref.at[n], held_ref.at[n], sem.at[n]).wait()
        projected = jnp.dot(all_ref[...], held_ref[n], preferred_element_type=jnp.float32)
        primal, tangent = projected[:rows], projected[rows:]
        columns = slice(n * BLOCK, (n + 1) * BLOCK)
        scale = scale_ref[:, columns]
        gated_ref[0, :, columns] = (scale * primal).astype(jnp.bfloat16)
        out_tan_ref[0, :, columns] = (tan_ref[:, columns] * primal + scale * tangent).astype(
            jnp.bfloat16
        )


def project(weights, places, x, gate_scale, gate_tangent):
    columns = weights[0].shape[1]
    depth = sum(weight.shape[0] for weight in weights)
    rows = x.shape[2]
    out = jax.ShapeDtypeStruct((1, rows, columns), jnp.bfloat16)
    in_vmem = pl.BlockSpec(memory_space=pltpu.VMEM)
    return pl.pallas_call(
        project_kernel,
        in_specs=[pl.BlockSpec(memory_space=pltpu.SMEM)]
        + [pl.BlockSpec(memory_space=pl.ANY)] * len(weights)
        + [in_vmem] * 3,
        out_specs=[in_vmem] * 2,
        out_shape=[out, out],
        scratch_shapes=[
            pltpu.VMEM((2 * rows, depth), jnp.bfloat16),
            pltpu.VMEM((columns // BLOCK, depth, BLOCK), jnp.bfloat16),
            pltpu.SemaphoreType.DMA((columns // BLOCK,)),
        ],
        compiler_params=pltpu.CompilerParams(vmem_limit_bytes=60 * MIB),
        cost_estimate=pl.CostEstimate(
            flops=4 * rows * depth * columns,
            bytes_accessed=2 * depth * columns,
            transcendentals=0,
        ),
        name="project",
    )(places, *weights, x, gate_scale, gate_tangent)


def send(value, moves_of, *after):
    if after:
        value = lax.optimization_barrier((value,) + after)[0]
    return lax.ppermute(value, AXES, moves_of)


def gather_plane(shard):
    return lax.all_gather(shard, "dp", axis=0, tiled=True, axis_index_groups=PLANES)


def on_device(
    query_rows,
    key_rows,
    value_rows,
    query_tangent,
    key_tangent,
    value_tangent,
    out_weight,
    gate_scale,
    gate_tangent,
):
    dp, seq = lax.axis_index("dp"), lax.axis_index("seq")
    x, z_pair, core, toward = dp // 8, dp // 2 % 4, dp % 2, seq // 4 * 2 - 1
    arrays = (query_rows, key_rows, value_rows, query_tangent, key_tangent, value_tangent)

    groups = lax.axis_size("seq")
    width = query_rows.shape[2] // groups
    z = [out_weight, send(out_weight, OUTER_Z)]
    weights = [gather_plane(z[0])]
    sent = pack(arrays, groups, (HEAD_DIM, width - HEAD_DIM))
    received = lax.all_to_all(sent[0], "seq", 0, 0, tiled=True)
    z.append(send(z[1], INNER_Z, sent[0]))
    along = lax.optimization_barrier((jnp.concatenate((z[1], z[2])), received))[0]
    weights.append(gather_plane(along))
    z.append(send(z[2], OUTER_Z, received))
    before, later = send(z[3], NEXT_X), send(z[3], LAST_X)
    far = send(before, NEXT_X)
    last_sent = lax.optimization_barrier((sent[1], received))[0]
    last_received = lax.all_to_all(last_sent, "seq", 0, 0, tiled=True)
    results = attend(received, 0, width)
    last_received = lax.optimization_barrier((last_received, before, later))[0]
    results = attend(last_received, 1, width, results)
    results = lax.all_to_all(results, "seq", 0, 0, tiled=True)

    places = [s // 2 * 8 + z_pair * 2 + s % 2 for s in range(8)]
    for s in range(8):
        for pairs in (toward, -toward):
            places.append(s // 2 * 8 + (z_pair + pairs) % 4 * 2 + s % 2)
    for block, steps in ((z[3], 0), (before, -1), (later, 1), (far, 2)):
        place = (x + steps) % 4 * 8 + (z_pair + 2) % 4 * 2
        weights += [block, send(block, OTHER_CORE)]
        places += [place + core, place + 1 - core]
    gated, tangent = project(
        weights, jnp.stack(places).astype(jnp.int32), results, gate_scale, gate_tangent
    )
    return (gated, tangent)


def solution(mesh):
    rows = P("dp", "seq", None)
    placed = (rows,) * 6 + (P("dp", None),) * 3
    return jax.shard_map(
        on_device,
        mesh=mesh,
        in_specs=placed,
        out_specs=(rows, rows),
        check_vma=False,
    )
```

profile of v0, /device:TPU:1, one launch (start us, length us, event | category | flops | bytes accessed | tf_op | source)
XLA Modules:
  0.0 157.3 jit_solution(15452288323566453527)
XLA Ops:
  7.2 0.0 all-gather.3.cloned.1.call-start
  7.2 0.7 all-gather.3.cloned.1.call-update
  7.9 5.2 %pack.1 = (bf16[8,6,128,128]{3,2,1,0:T(8,128)(2,1)}, bf16[8,6,128,256]{3,2,1,0:T(8,128)(2,1)}) custom-call(bf16[1,128,3072]{2,1,0:T(8,128)(2,1)} %refs_0_.1, bf16[1,128,3072]{2,1,0:T(8,128)(2,1)} %refs_1_.1, bf16[1,128,3072]{2,1,0:T(8,128)(2,1)} %refs_2_.1, bf16[1,128,3072]{2,1,0:T(8,128)(2,1)} %refs_3_.1, bf16[1,128,3072]{2,1,0:T(8,128)(2,1)} %refs_4_.1, ...), custom_call_target="tpu_custom_call" | custom-call | bytes 9437184 | tf_op jit(solution)/shard_map/pack/pallas_call | solution.py:56
  13.1 6.5 %all-to-all-start = ((bf16[8,6,128,128]{3,2,1,0:T(8,128)(2,1)}), bf16[8,6,128,128]{3,2,1,0:T(8,128)(2,1)S(1)}, u32[]{:S(2)}, u32[]{:S(2)}) async-start(bf16[8,6,128,128]{3,2,1,0:T(8,128)(2,1)} %get-tuple-element.9), calls=%async_computation | async-start | bytes 3145728 | tf_op jit(solution)/shard_map/all_to_all | solution.py:227
  19.7 5.4 %collective-permute-start = (bf16[96,3072]{1,0:T(8,128)(2,1)S(1)}, bf16[96,3072]{1,0:T(8,128)(2,1)S(1)}, u32[]{:S(2)}, u32[]{:S(2)}) collective-permute-start(bf16[96,3072]{1,0:T(8,128)(2,1)S(1)} %copy-done.11), channel_id=1, source_target_pairs={{0,52},{1,53},{2,54},{3,55},{8,60},{9,61},{10,62},{11,63},{4,16},{... | collective-permute-start | bytes 1769480 | tf_op jit(solution)/shard_map/ppermute | solution.py:200
  25.1 12.5 %collective-permute-done = bf16[96,3072]{1,0:T(8,128)(2,1)S(1)} collective-permute-done((bf16[96,3072]{1,0:T(8,128)(2,1)S(1)}, bf16[96,3072]{1,0:T(8,128)(2,1)S(1)}, u32[]{:S(2)}, u32[]{:S(2)}) %collective-permute-start) | collective-permute-done | bytes 589856 | tf_op jit(solution)/shard_map/ppermute | solution.py:200
  37.7 13.1 %collective-permute-done.1 = bf16[96,3072]{1,0:T(8,128)(2,1)S(1)} collective-permute-done((bf16[96,3072]{1,0:T(8,128)(2,1)S(1)}, bf16[96,3072]{1,0:T(8,128)(2,1)S(1)}, u32[]{:S(2)}, u32[]{:S(2)}) %collective-permute-start.1) | collective-permute-done | bytes 589856 | tf_op jit(solution)/shard_map/ppermute | solution.py:200
  50.7 1.2 pad_maximum_fusion
  51.9 1.2 copy-done
  53.2 4.0 %all-to-all-start.1 = ((bf16[8,6,128,256]{3,2,1,0:T(8,128)(2,1)}), bf16[8,6,128,256]{3,2,1,0:T(8,128)(2,1)S(1)}, u32[]{:S(2)}, u32[]{:S(2)}) async-start(bf16[8,6,128,256]{3,2,1,0:T(8,128)(2,1)} %get-tuple-element.14), calls=%async_computation.1 | async-start | bytes 6291456 | tf_op jit(solution)/shard_map/all_to_all | solution.py:235
  57.1 5.5 %collective-permute-start.2 = (bf16[96,3072]{1,0:T(8,128)(2,1)}, bf16[96,3072]{1,0:T(8,128)(2,1)S(1)}, u32[]{:S(2)}, u32[]{:S(2)}) collective-permute-start(bf16[96,3072]{1,0:T(8,128)(2,1)} %copy-done.12), channel_id=1, source_target_pairs={{0,52},{1,53},{2,54},{3,55},{8,60},{9,61},{10,62},{11,63},{4,16},{... | collective-permute-start | bytes 1769480 | tf_op jit(solution)/shard_map/ppermute | solution.py:200
  62.7 11.7 %collective-permute-done.2.refs_2_ = bf16[96,3072]{1,0:T(8,128)(2,1)S(1)} collective-permute-done((bf16[96,3072]{1,0:T(8,128)(2,1)}, bf16[96,3072]{1,0:T(8,128)(2,1)S(1)}, u32[]{:S(2)}, u32[]{:S(2)}) %collective-permute-start.2) | collective-permute-done | bytes 589856 | tf_op jit(solution)/shard_map/ppermute | solution.py:200
  74.4 1.0 collective-permute-start.4
  75.4 1.6 %collective-permute-start.6 = (bf16[96,3072]{1,0:T(8,128)(2,1)S(1)}, bf16[96,3072]{1,0:T(8,128)(2,1)}, u32[]{:S(2)}, u32[]{:S(2)}) collective-permute-start(bf16[96,3072]{1,0:T(8,128)(2,1)S(1)} %collective-permute-done.2.refs_2_), channel_id=1, source_target_pairs={{0,192},{1,193},{2,194},{3,195},{8,200},{9,201},{10,202},{11,203},... | collective-permute-start | bytes 1769480 | tf_op jit(solution)/shard_map/ppermute | solution.py:200
  77.0 1.4 copy-done.1
  78.5 3.2 %attend.2.refs_0_ = bf16[8,2,128,384]{3,2,1,0:T(8,128)(2,1)S(1)} custom-call(bf16[8,6,128,128]{3,2,1,0:T(8,128)(2,1)S(1)} %copy-done.1), custom_call_target="tpu_custom_call" | custom-call | flops 1610612736 | bytes 2097152 | tf_op jit(solution)/shard_map/attend/pallas_call | solution.py:115
  81.7 1.2 copy-done.2
  82.9 19.7 %collective-permute-done.4.refs_4_ = bf16[96,3072]{1,0:T(8,128)(2,1)S(1)} collective-permute-done((bf16[96,3072]{1,0:T(8,128)(2,1)S(1)}, bf16[96,3072]{1,0:T(8,128)(2,1)S(1)}, u32[]{:S(2)}, u32[]{:S(2)}) %collective-permute-start.4) | collective-permute-done | bytes 589856 | tf_op jit(solution)/shard_map/ppermute | solution.py:200
  102.5 0.8 copy-done.8
  103.4 1.4 copy-done.3
  104.8 6.9 %attend.3 = bf16[8,2,128,384]{3,2,1,0:T(8,128)(2,1)S(1)} custom-call(bf16[8,6,128,256]{3,2,1,0:T(8,128)(2,1)S(1)} %all-to-all-done.1.in_ref, bf16[8,2,128,384]{3,2,1,0:T(8,128)(2,1)S(1)} %copy-done.3), custom_call_target="tpu_custom_call", output_to_operand_aliasing={{}: (1, {})} | custom-call | flops 3221225472 | bytes 4194304 | tf_op jit(solution)/shard_map/attend/pallas_call | solution.py:115
  111.7 1.1 copy-done.4
  112.9 4.1 %all-to-all-start.2 = ((bf16[8,2,128,384]{3,2,1,0:T(8,128)(2,1)}), bf16[8,2,128,384]{3,2,1,0:T(8,128)(2,1)S(1)}, u32[]{:S(2)}, u32[]{:S(2)}) async-start(bf16[8,2,128,384]{3,2,1,0:T(8,128)(2,1)} %copy-done.4), calls=%async_computation.2 | async-start | bytes 3145728 | tf_op jit(solution)/shard_map/all_to_all | solution.py:239
  117.0 0.2 collective-permute-start.8
  117.2 4.6 %collective-permute-start.3 = (bf16[96,3072]{1,0:T(8,128)(2,1)S(1)}, bf16[96,3072]{1,0:T(8,128)(2,1)}, u32[]{:S(2)}, u32[]{:S(2)}) collective-permute-start(bf16[96,3072]{1,0:T(8,128)(2,1)S(1)} %copy-done.7), channel_id=1, source_target_pairs={{0,8},{1,9},{2,10},{3,11},{8,0},{9,1},{10,2},{11,3},{4,12},{5,13},... | collective-permute-start | bytes 1769480 | tf_op jit(solution)/shard_map/ppermute | solution.py:200
  121.8 0.5 collective-permute-start.7
  122.3 12.9 %collective-permute-done.8.refs_8_ = bf16[96,3072]{1,0:T(8,128)(2,1)S(1)} collective-permute-done((bf16[96,3072]{1,0:T(8,128)(2,1)S(1)}, bf16[96,3072]{1,0:T(8,128)(2,1)S(1)}, u32[]{:S(2)}, u32[]{:S(2)}) %collective-permute-start.8) | collective-permute-done | bytes 589856 | tf_op jit(solution)/shard_map/ppermute | solution.py:200
  135.2 1.8 %collective-permute-start.9 = (bf16[96,3072]{1,0:T(8,128)(2,1)S(1)}, bf16[96,3072]{1,0:T(8,128)(2,1)}, u32[]{:S(2)}, u32[]{:S(2)}) collective-permute-start(bf16[96,3072]{1,0:T(8,128)(2,1)S(1)} %collective-permute-done.8.refs_8_), channel_id=1, source_target_pairs={{0,8},{1,9},{2,10},{3,11},{8,0},{9,1},{10,2},{11,3},{4,12},{5,13},... | collective-permute-start | bytes 1769480 | tf_op jit(solution)/shard_map/ppermute | solution.py:200
  137.1 0.7 stack.131.place_ref
  137.8 1.0 collective-permute-done.9.refs_9_
  138.9 1.1 copy-done.5
  140.0 10.4 %project.1 = (bf16[1,128,3072]{2,1,0:T(8,128)(2,1)}, bf16[1,128,3072]{2,1,0:T(8,128)(2,1)}) custom-call(s32[32]{0:T(128)} %stack.131.place_ref, bf16[768,3072]{1,0:T(8,128)(2,1)} %all-gather.3.cloned.1.call-done.refs_0_, bf16[1536,3072]{1,0:T(8,128)(2,1)} %all-gather.5.cloned.1.call-done.refs_1_, bf16[96,3072]{1,0:T(8,128)(2,1)} %copy-done.6, ...), custom_call_target="tpu_custom_call" | custom-call | flops 4831838208 | bytes 18874368 | tf_op jit(solution)/shard_map/project/pallas_call | solution.py:175
  (32 shorter events, 0.1 us)
Async XLA Ops:
  7.2 131.7 %all-gather.3.cloned.1.call-start = ((), (), s32[]{:S(2)}) async-start(), calls=%async_computation.3 | async-start | bytes 5308416 | tf_op jit(solution)/shard_map/all_gather | solution.py:204
  13.1 6.6 %copy-start.11 = (bf16[96,3072]{1,0:T(8,128)(2,1)S(1)}, bf16[96,3072]{1,0:T(8,128)(2,1)}, u32[]{:S(2)}) copy-start(bf16[96,3072]{1,0:T(8,128)(2,1)} %param.15) | copy-start | bytes 1769476
  13.1 38.8 %all-to-all-start = ((bf16[8,6,128,128]{3,2,1,0:T(8,128)(2,1)}), bf16[8,6,128,128]{3,2,1,0:T(8,128)(2,1)S(1)}, u32[]{:S(2)}, u32[]{:S(2)}) async-start(bf16[8,6,128,128]{3,2,1,0:T(8,128)(2,1)} %get-tuple-element.9), calls=%async_computation | async-start | bytes 3145728 | tf_op jit(solution)/shard_map/all_to_all | solution.py:227
  19.6 119.2 %all-gather.5.cloned.1.call-start = ((), (), s32[]{:S(2)}) async-start(), calls=%async_computation.4 | async-start | bytes 10616832 | tf_op jit(solution)/shard_map/all_gather | solution.py:204
  19.7 18.0 %collective-permute-start = (bf16[96,3072]{1,0:T(8,128)(2,1)S(1)}, bf16[96,3072]{1,0:T(8,128)(2,1)S(1)}, u32[]{:S(2)}, u32[]{:S(2)}) collective-permute-start(bf16[96,3072]{1,0:T(8,128)(2,1)S(1)} %copy-done.11), channel_id=1, source_target_pairs={{0,52},{1,53},{2,54},{3,55},{8,60},{9,61},{10,62},{11,63},{4,16},{... | collective-permute-start | bytes 1769480 | tf_op jit(solution)/shard_map/ppermute | solution.py:200
  37.7 13.1 %collective-permute-start.1 = (bf16[96,3072]{1,0:T(8,128)(2,1)S(1)}, bf16[96,3072]{1,0:T(8,128)(2,1)S(1)}, u32[]{:S(2)}, u32[]{:S(2)}) collective-permute-start(bf16[96,3072]{1,0:T(8,128)(2,1)S(1)} %collective-permute-done), channel_id=1, source_target_pairs={{0,4},{1,5},{2,6},{3,7},{8,12},{9,13},{10,14},{11,15},{4,0},{5,1},... | collective-permute-start | bytes 1769480 | tf_op jit(solution)/shard_map/ppermute | solution.py:200
  50.7 2.4 %copy-start.12 = (bf16[96,3072]{1,0:T(8,128)(2,1)}, bf16[96,3072]{1,0:T(8,128)(2,1)S(1)}, u32[]{:S(2)}) copy-start(bf16[96,3072]{1,0:T(8,128)(2,1)S(1)} %collective-permute-done.1) | copy-start | bytes 1769476
  51.9 1.2 copy-start
  53.2 50.2 %all-to-all-start.1 = ((bf16[8,6,128,256]{3,2,1,0:T(8,128)(2,1)}), bf16[8,6,128,256]{3,2,1,0:T(8,128)(2,1)S(1)}, u32[]{:S(2)}, u32[]{:S(2)}) async-start(bf16[8,6,128,256]{3,2,1,0:T(8,128)(2,1)} %get-tuple-element.14), calls=%async_computation.1 | async-start | bytes 6291456 | tf_op jit(solution)/shard_map/all_to_all | solution.py:235
  57.1 17.2 %collective-permute-start.2 = (bf16[96,3072]{1,0:T(8,128)(2,1)}, bf16[96,3072]{1,0:T(8,128)(2,1)S(1)}, u32[]{:S(2)}, u32[]{:S(2)}) collective-permute-start(bf16[96,3072]{1,0:T(8,128)(2,1)} %copy-done.12), channel_id=1, source_target_pairs={{0,52},{1,53},{2,54},{3,55},{8,60},{9,61},{10,62},{11,63},{4,16},{... | collective-permute-start | bytes 1769480 | tf_op jit(solution)/shard_map/ppermute | solution.py:200
  74.4 7.3 %copy-start.6 = (bf16[96,3072]{1,0:T(8,128)(2,1)}, bf16[96,3072]{1,0:T(8,128)(2,1)S(1)}, u32[]{:S(2)}) copy-start(bf16[96,3072]{1,0:T(8,128)(2,1)S(1)} %collective-permute-done.2.refs_2_) | copy-start | bytes 1769476
  74.4 28.2 %collective-permute-start.4 = (bf16[96,3072]{1,0:T(8,128)(2,1)S(1)}, bf16[96,3072]{1,0:T(8,128)(2,1)S(1)}, u32[]{:S(2)}, u32[]{:S(2)}) collective-permute-start(bf16[96,3072]{1,0:T(8,128)(2,1)S(1)} %collective-permute-done.2.refs_2_), channel_id=1, source_target_pairs={{0,64},{1,65},{2,66},{3,67},{8,72},{9,73},{10,74},{11,75},{4,68},{... | collective-permute-start | bytes 1769480 | tf_op jit(solution)/shard_map/ppermute | solution.py:200
  75.4 28.0 %collective-permute-start.6 = (bf16[96,3072]{1,0:T(8,128)(2,1)S(1)}, bf16[96,3072]{1,0:T(8,128)(2,1)}, u32[]{:S(2)}, u32[]{:S(2)}) collective-permute-start(bf16[96,3072]{1,0:T(8,128)(2,1)S(1)} %collective-permute-done.2.refs_2_), channel_id=1, source_target_pairs={{0,192},{1,193},{2,194},{3,195},{8,200},{9,201},{10,202},{11,203},... | collective-permute-start | bytes 1769480 | tf_op jit(solution)/shard_map/ppermute | solution.py:200
  77.0 1.4 copy-start.1
  81.7 1.2 copy-start.2
  102.5 0.8 copy-start.8
  103.4 1.4 copy-start.3
  111.7 1.2 copy-start.4
  112.8 4.1 %copy-start.9 = (bf16[96,3072]{1,0:T(8,128)(2,1)S(1)}, bf16[96,3072]{1,0:T(8,128)(2,1)}, u32[]{:S(2)}) copy-start(bf16[96,3072]{1,0:T(8,128)(2,1)} %copy-done.8) | copy-start | bytes 1769476
  112.9 4.3 %copy-start.7 = (bf16[96,3072]{1,0:T(8,128)(2,1)S(1)}, bf16[96,3072]{1,0:T(8,128)(2,1)}, u32[]{:S(2)}) copy-start(bf16[96,3072]{1,0:T(8,128)(2,1)} %copy-done.6) | copy-start | bytes 1769476
  112.9 26.0 %all-to-all-start.2 = ((bf16[8,2,128,384]{3,2,1,0:T(8,128)(2,1)}), bf16[8,2,128,384]{3,2,1,0:T(8,128)(2,1)S(1)}, u32[]{:S(2)}, u32[]{:S(2)}) async-start(bf16[8,2,128,384]{3,2,1,0:T(8,128)(2,1)} %copy-done.4), calls=%async_computation.2 | async-start | bytes 3145728 | tf_op jit(solution)/shard_map/all_to_all | solution.py:239
  117.0 18.2 %collective-permute-start.8 = (bf16[96,3072]{1,0:T(8,128)(2,1)S(1)}, bf16[96,3072]{1,0:T(8,128)(2,1)S(1)}, u32[]{:S(2)}, u32[]{:S(2)}) collective-permute-start(bf16[96,3072]{1,0:T(8,128)(2,1)S(1)} %copy-done.9), channel_id=1, source_target_pairs={{0,64},{1,65},{2,66},{3,67},{8,72},{9,73},{10,74},{11,75},{4,68},{... | collective-permute-start | bytes 1769480 | tf_op jit(solution)/shard_map/ppermute | solution.py:200
  117.2 20.6 %collective-permute-start.3 = (bf16[96,3072]{1,0:T(8,128)(2,1)S(1)}, bf16[96,3072]{1,0:T(8,128)(2,1)}, u32[]{:S(2)}, u32[]{:S(2)}) collective-permute-start(bf16[96,3072]{1,0:T(8,128)(2,1)S(1)} %copy-done.7), channel_id=1, source_target_pairs={{0,8},{1,9},{2,10},{3,11},{8,0},{9,1},{10,2},{11,3},{4,12},{5,13},... | collective-permute-start | bytes 1769480 | tf_op jit(solution)/shard_map/ppermute | solution.py:200
  121.8 16.0 %collective-permute-start.5 = (bf16[96,3072]{1,0:T(8,128)(2,1)S(1)}, bf16[96,3072]{1,0:T(8,128)(2,1)}, u32[]{:S(2)}, u32[]{:S(2)}) collective-permute-start(bf16[96,3072]{1,0:T(8,128)(2,1)S(1)} %copy-done.9), channel_id=1, source_target_pairs={{0,8},{1,9},{2,10},{3,11},{8,0},{9,1},{10,2},{11,3},{4,12},{5,13},... | collective-permute-start | bytes 1769480 | tf_op jit(solution)/shard_map/ppermute | solution.py:200
  121.8 16.0 %collective-permute-start.7 = (bf16[96,3072]{1,0:T(8,128)(2,1)}, bf16[96,3072]{1,0:T(8,128)(2,1)}, u32[]{:S(2)}, u32[]{:S(2)}) collective-permute-start(bf16[96,3072]{1,0:T(8,128)(2,1)} %collective-permute-done.6.refs_6_), channel_id=1, source_target_pairs={{0,8},{1,9},{2,10},{3,11},{8,0},{9,1},{10,2},{11,3},{4,12},{5,13},... | collective-permute-start | bytes 1769480 | tf_op jit(solution)/shard_map/ppermute | solution.py:200
  135.2 3.6 %copy-start.10 = (bf16[96,3072]{1,0:T(8,128)(2,1)}, bf16[96,3072]{1,0:T(8,128)(2,1)S(1)}, u32[]{:S(2)}) copy-start(bf16[96,3072]{1,0:T(8,128)(2,1)S(1)} %collective-permute-done.8.refs_8_) | copy-start | bytes 1769476
  135.2 3.6 %collective-permute-start.9 = (bf16[96,3072]{1,0:T(8,128)(2,1)S(1)}, bf16[96,3072]{1,0:T(8,128)(2,1)}, u32[]{:S(2)}, u32[]{:S(2)}) collective-permute-start(bf16[96,3072]{1,0:T(8,128)(2,1)S(1)} %collective-permute-done.8.refs_8_), channel_id=1, source_target_pairs={{0,8},{1,9},{2,10},{3,11},{8,0},{9,1},{10,2},{11,3},{4,12},{5,13},... | collective-permute-start | bytes 1769480 | tf_op jit(solution)/shard_map/ppermute | solution.py:200
  138.8 1.2 copy-start.5
Sparse Core Ops, SparseCore 0:
  9.8 41.0 all-gather.2
  53.3 74.5 all-gather.4
where the time goes:
time: 158 us; the launch traced here: 157 us
  waiting for transfers between devices  71.6 us (45%)
  starting transfers between devices  35.5 us (22%)
  Pallas kernels  25.8 us (16%)
  between operations  14.2 us (9%)
  local copies, waits for them, and re-layouts  9.01 us (6%)
    ppermute x10, waiting for transfers between devices, send(): return lax.ppermute(value, AXES, moves_of)  70.9 us
    ppermute x10, starting transfers between devices, send(): return lax.ppermute(value, AXES, moves_of)  20.8 us
    pallas_call x1, Pallas kernels, project(): pl.pallas_call(project_kernel, in_specs=[pl.BlockSpec(memory_space=pltpu....  10.4 us
    pallas_call x2, Pallas kernels, attend(): pl.pallas_call(attend_kernel, grid=(heads,), in_specs=[pl.BlockSpec((piec...  10.1 us
    unnamed x26, local copies, waits for them, and re-layouts  8.3 us
    all_to_all x1, starting transfers between devices, on_device(): received = lax.all_to_all(sent[0], 'seq', 0, 0, tiled=True)  6.51 us
    pallas_call x1, Pallas kernels, pack(): pl.pallas_call(pack_kernel, grid=(rows // block,), in_specs=[pl.BlockSpec...  5.23 us
    all_to_all x1, starting transfers between devices, on_device(): results = lax.all_to_all(results, 'seq', 0, 0, tiled=True)  4.1 us
  transfers between devices with their start and end apart: 15, of which 6 were waited for; matrix products, arithmetic and copies ran while one was open for 1% of the time, Pallas kernels for 10%

commit v1 on v0

--- a/solution.py
+++ b/solution.py
@@ -32,36 +32,25 @@
 OUTER_Z = moves(lambda x, z, core, y: (x, z + 1 if z % 2 else z - 1, core, y))
 INNER_Z = moves(lambda x, z, core, y: (x, z - 1 if z % 2 else z + 1, core, y))
 OTHER_CORE = moves(lambda x, z, core, y: (x, z, 1 - core, y))
-PLANES = [[x * 8 + pair * 2 + core for x in range(4) for core in range(2)] for pair in range(4)]
 
 
 def pack_kernel(*refs):
-    ins, outs = refs[:6], refs[6:]
-    pieces = outs[0].shape[0]
-    width = sum(out_ref.shape[3] for out_ref in outs)
-    first = 0
-    for out_ref in outs:
-        share = out_ref.shape[3]
-        for piece in range(pieces):
-            columns = slice(piece * width + first, piece * width + first + share)
-            for at, ref in enumerate(ins):
-                out_ref[piece, at] = ref[0, :, columns]
-        first += share
-
-
-def pack(arrays, pieces, shares, block=32):
-    rows = arrays[0].shape[1]
-    columns = arrays[0].shape[2]
-    shapes = [(pieces, len(arrays), rows, share) for share in shares]
+    ins, out_ref = refs[:-1], refs[-1]
+    pieces, _, _, width = out_ref.shape
+    for piece in range(pieces):
+        for at, ref in enumerate(ins):
+            out_ref[piece, at] = ref[0, :, piece * width : (piece + 1) * width]
+
+
+def pack(arrays, pieces, block=32):
+    _, rows, columns = arrays[0].shape
+    width = columns // pieces
     return pl.pallas_call(
         pack_kernel,
         grid=(rows // block,),
         in_specs=[pl.BlockSpec((1, block, columns), lambda i: (0, i, 0)) for _ in arrays],
-        out_specs=[
-            pl.BlockSpec((pieces, len(arrays), block, share), lambda i: (0, 0, i, 0))
-            for share in shares
-        ],
-        out_shape=[jax.ShapeDtypeStruct(shape, arrays[0].dtype) for shape in shapes],
+        out_specs=pl.BlockSpec((pieces, len(arrays), block, width), lambda i: (0, 0, i, 0)),
+        out_shape=jax.ShapeDtypeStruct((pieces, len(arrays), rows, width), arrays[0].dtype),
         cost_estimate=pl.CostEstimate(
             flops=0, bytes_accessed=4 * len(arrays) * rows * columns, transcendentals=0
         ),
@@ -107,15 +96,14 @@
         out_ref[which, 1] = heads_tan.astype(jnp.bfloat16).reshape(step, rows, HEAD_DIM)
 
 
-def attend(received, first, width, others=None):
-    pieces, count, rows, share = received.shape
-    heads = share // HEAD_DIM
+def attend(received, first, heads, others=None):
+    pieces, count, rows, width = received.shape
     tokens = rows * pieces
     kept = [] if others is None else [others]
     return pl.pallas_call(
         attend_kernel,
         grid=(heads,),
-        in_specs=[pl.BlockSpec((pieces, count, rows, HEAD_DIM), lambda h: (0, 0, 0, h))]
+        in_specs=[pl.BlockSpec((pieces, count, rows, HEAD_DIM), lambda h: (0, 0, 0, h + first))]
         + [pl.BlockSpec(memory_space=pl.ANY)] * len(kept),
         out_specs=pl.BlockSpec((pieces, 2, rows, HEAD_DIM), lambda h: (0, 0, 0, h + first)),
         out_shape=jax.ShapeDtypeStruct((pieces, 2, rows, width), jnp.bfloat16),
@@ -200,10 +188,6 @@
     return lax.ppermute(value, AXES, moves_of)
 
 
-def gather_plane(shard):
-    return lax.all_gather(shard, "dp", axis=0, tiled=True, axis_index_groups=PLANES)
-
-
 def on_device(
     query_rows,
     key_rows,
@@ -219,33 +203,42 @@
     x, z_pair, core, toward = dp // 8, dp // 2 % 4, dp % 2, seq // 4 * 2 - 1
     arrays = (query_rows, key_rows, value_rows, query_tangent, key_tangent, value_tangent)
 
-    groups = lax.axis_size("seq")
-    width = query_rows.shape[2] // groups
-    z = [out_weight, send(out_weight, OUTER_Z)]
-    weights = [gather_plane(z[0])]
-    sent = pack(arrays, groups, (HEAD_DIM, width - HEAD_DIM))
-    received = lax.all_to_all(sent[0], "seq", 0, 0, tiled=True)
-    z.append(send(z[1], INNER_Z, sent[0]))
-    along = lax.optimization_barrier((jnp.concatenate((z[1], z[2])), received))[0]
-    weights.append(gather_plane(along))
-    z.append(send(z[2], OUTER_Z, received))
-    before, later = send(z[3], NEXT_X), send(z[3], LAST_X)
-    far = send(before, NEXT_X)
-    last_sent = lax.optimization_barrier((sent[1], received))[0]
-    last_received = lax.all_to_all(last_sent, "seq", 0, 0, tiled=True)
-    results = attend(received, 0, width)
-    last_received = lax.optimization_barrier((last_received, before, later))[0]
-    results = attend(last_received, 1, width, results)
+    sent = pack(arrays, lax.axis_size("seq"))
+    received = lax.all_to_all(sent, "seq", 0, 0, tiled=True)
+
+    z, before, later, far = {0: out_weight}, {}, {}, {}
+    z[1] = send(z[0], OUTER_Z)
+    before[0] = send(z[0], NEXT_X)
+    later[0] = send(z[0], LAST_X)
+    z[2] = send(z[1], INNER_Z, sent)
+    far[0] = send(before[0], NEXT_X, sent)
+    later[1] = send(z[1], LAST_X, later[0], sent)
+    before[1] = send(z[1], NEXT_X, before[0])
+    far[1] = send(later[1], LAST_X)
+    z[3] = send(z[2], OUTER_Z)
+    before[2] = send(z[2], NEXT_X, far[0])
+    later[2] = send(z[2], LAST_X, later[1])
+    far[2] = send(before[2], NEXT_X, before[1])
+    later[3] = send(z[3], LAST_X, far[1])
+    before[3] = send(z[3], NEXT_X, before[2])
+    far[3] = send(later[3], LAST_X, later[2])
+
+    freed = (before[1], far[1], far[2], before[3])
+    weights, swapped, places = [], {}, []
+    for at, pairs in enumerate((0, toward, -toward, 2)):
+        for block, steps in ((z[at], 0), (before[at], -1), (later[at], 1), (far[at], 2)):
+            place = (x + steps) % 4 * 8 + (z_pair + pairs) % 4 * 2
+            swapped[at, steps] = send(block, OTHER_CORE, freed[at])
+            weights += [block, swapped[at, steps]]
+            places += [place + core, place + 1 - core]
+
+    early = [swapped[at, steps] for at in (0, 1) for steps in (0, -1, 1, 2)]
+    received = lax.optimization_barrier((received, z[3], before[2], later[2], *early))[0]
+    results = attend(received, 0, 2)
+    received = lax.optimization_barrier((received, far[2], later[3]))[0]
+    results = attend(received, 2, 1, results)
     results = lax.all_to_all(results, "seq", 0, 0, tiled=True)
 
-    places = [s // 2 * 8 + z_pair * 2 + s % 2 for s in range(8)]
-    for s in range(8):
-        for pairs in (toward, -toward):
-            places.append(s // 2 * 8 + (z_pair + pairs) % 4 * 2 + s % 2)
-    for block, steps in ((z[3], 0), (before, -1), (later, 1), (far, 2)):
-        place = (x + steps) % 4 * 8 + (z_pair + 2) % 4 * 2
-        weights += [block, send(block, OTHER_CORE)]
-        places += [place + core, place + 1 - core]
     gated, tangent = project(
         weights, jnp.stack(places).astype(jnp.int32), results, gate_scale, gate_tangent
     )

time: 158 us -> 174 us (1.10)
  starting transfers between devices: 35.5 us -> 52 us
  waiting for transfers between devices: 71.6 us -> 86.2 us
  between operations: 14.2 us -> 1.01 us
  local copies, waits for them, and re-layouts: 9.01 us -> 4.71 us
  Pallas kernels: 25.8 us -> 29.3 us
    ppermute x10 -> x31, starting transfers between devices: 20.8 us -> 41.7 us  [send(): return lax.ppermute(value, AXES, moves_of)]
    ppermute x10 -> x31, waiting for transfers between devices: 70.9 us -> 86.2 us  [send(): return lax.ppermute(value, AXES, moves_of)]
    unnamed x26 -> x54, local copies, waits for them, and re-layouts: 8.3 us -> 4.07 us
    all_to_all x2 -> x1, starting transfers between devices: 10.5 us -> 6.51 us  [on_device(): received = lax.all_to_all(sent, 'seq', 0, 0, tiled=True)]
    pallas_call x2, Pallas kernels: 10.1 us -> 13.8 us  [attend(): pl.pallas_call(attend_kernel, grid=(heads,), in_specs=[pl.BlockSpec((piec...]
  transfers between devices with their start and end apart: 15 -> 33, of which waited for: 6 -> 12; matrix products, arithmetic and copies ran while one was open for 1% -> 0% of each run, Pallas kernels for 10% -> 5%
where the time goes in v1:
time: 174 us; the launch traced here: 173 us
  waiting for transfers between devices  86.2 us (50%)
  starting transfers between devices  52 us (30%)
  Pallas kernels  29.3 us (17%)
  local copies, waits for them, and re-layouts  4.71 us (3%)
    ppermute x31, waiting for transfers between devices, send(): return lax.ppermute(value, AXES, moves_of)  86.2 us
    ppermute x31, starting transfers between devices, send(): return lax.ppermute(value, AXES, moves_of)  41.7 us
    pallas_call x2, Pallas kernels, attend(): pl.pallas_call(attend_kernel, grid=(heads,), in_specs=[pl.BlockSpec((piec...  13.8 us
    pallas_call x1, Pallas kernels, project(): pl.pallas_call(project_kernel, in_specs=[pl.BlockSpec(memory_space=pltpu....  10.4 us
    all_to_all x1, starting transfers between devices, on_device(): received = lax.all_to_all(sent, 'seq', 0, 0, tiled=True)  6.51 us
    pallas_call x1, Pallas kernels, pack(): pl.pallas_call(pack_kernel, grid=(rows // block,), in_specs=[pl.BlockSpec...  5.13 us
    unnamed x54, local copies, waits for them, and re-layouts  4.07 us
    all_to_all x1, starting transfers between devices, on_device(): results = lax.all_to_all(results, 'seq', 0, 0, tiled=True)  3.79 us
  transfers between devices with their start and end apart: 33, of which 12 were waited for; matrix products, arithmetic and copies ran while one was open for 0% of the time, Pallas kernels for 5%

profile of v1, /device:TPU:1, one launch (start us, length us, event | category | flops | bytes accessed | tf_op | source)
XLA Modules:
  0.0 173.3 jit_solution(12236461679580535295)
XLA Ops:
  0.6 5.1 %pack.1 = bf16[8,6,128,384]{3,2,1,0:T(8,128)(2,1)} custom-call(bf16[1,128,3072]{2,1,0:T(8,128)(2,1)} %refs_0_.2, bf16[1,128,3072]{2,1,0:T(8,128)(2,1)} %refs_1_.1, bf16[1,128,3072]{2,1,0:T(8,128)(2,1)} %refs_2_.1, bf16[1,128,3072]{2,1,0:T(8,128)(2,1)} %refs_3_.1, bf16[1,128,3072]{2,1,0:T(8,128)(2,1)} %refs_4_.1, bf16[1,128,3072]{2,1,0:T(8,128)(2,1)} %refs_5_.1), custom_call_target="tpu_custom_call" | custom-call | bytes 9437184 | tf_op jit(solution)/shard_map/pack/pallas_call | solution.py:48
  5.8 6.5 %all-to-all-start = ((bf16[8,6,128,384]{3,2,1,0:T(8,128)(2,1)}), bf16[8,6,128,384]{3,2,1,0:T(8,128)(2,1)}, u32[]{:S(2)}, u32[]{:S(2)}) async-start(bf16[8,6,128,384]{3,2,1,0:T(8,128)(2,1)} %pack.1), calls=%async_computation | async-start | bytes 9437184 | tf_op jit(solution)/shard_map/all_to_all | solution.py:207
  12.3 5.4 %collective-permute-start = (bf16[96,3072]{1,0:T(8,128)(2,1)S(1)}, bf16[96,3072]{1,0:T(8,128)(2,1)S(1)}, u32[]{:S(2)}, u32[]{:S(2)}) collective-permute-start(bf16[96,3072]{1,0:T(8,128)(2,1)S(1)} %copy-done.1), channel_id=1, source_target_pairs={{0,52},{1,53},{2,54},{3,55},{8,60},{9,61},{10,62},{11,63},{4,16},{... | collective-permute-start | bytes 1769480 | tf_op jit(solution)/shard_map/ppermute | solution.py:188
  17.7 2.5 %collective-permute-start.5 = (bf16[96,3072]{1,0:T(8,128)(2,1)S(1)}, bf16[96,3072]{1,0:T(8,128)(2,1)S(1)}, u32[]{:S(2)}, u32[]{:S(2)}) collective-permute-start(bf16[96,3072]{1,0:T(8,128)(2,1)S(1)} %copy-done.1), channel_id=1, source_target_pairs={{0,192},{1,193},{2,194},{3,195},{8,200},{9,201},{10,202},{11,203},... | collective-permute-start | bytes 1769480 | tf_op jit(solution)/shard_map/ppermute | solution.py:188
  20.2 10.0 %collective-permute-done.refs_8_ = bf16[96,3072]{1,0:T(8,128)(2,1)S(1)} collective-permute-done((bf16[96,3072]{1,0:T(8,128)(2,1)S(1)}, bf16[96,3072]{1,0:T(8,128)(2,1)S(1)}, u32[]{:S(2)}, u32[]{:S(2)}) %collective-permute-start) | collective-permute-done | bytes 589856 | tf_op jit(solution)/shard_map/ppermute | solution.py:188
  30.2 1.1 collective-permute-done.5.refs_4_
  31.3 3.5 %collective-permute-start.9 = (bf16[96,3072]{1,0:T(8,128)(2,1)S(1)}, bf16[96,3072]{1,0:T(8,128)(2,1)S(1)}, u32[]{:S(2)}, u32[]{:S(2)}) collective-permute-start(bf16[96,3072]{1,0:T(8,128)(2,1)S(1)} %collective-permute-done.refs_8_), channel_id=1, source_target_pairs={{0,192},{1,193},{2,194},{3,195},{8,200},{9,201},{10,202},{11,203},... | collective-permute-start | bytes 1769480 | tf_op jit(solution)/shard_map/ppermute | solution.py:188
  35.0 10.1 %collective-permute-done.9.refs_12_ = bf16[96,3072]{1,0:T(8,128)(2,1)S(1)} collective-permute-done((bf16[96,3072]{1,0:T(8,128)(2,1)S(1)}, bf16[96,3072]{1,0:T(8,128)(2,1)S(1)}, u32[]{:S(2)}, u32[]{:S(2)}) %collective-permute-start.9) | collective-permute-done | bytes 589856 | tf_op jit(solution)/shard_map/ppermute | solution.py:188
  45.1 3.5 %collective-permute-start.10 = (bf16[96,3072]{1,0:T(8,128)(2,1)S(1)}, bf16[96,3072]{1,0:T(8,128)(2,1)S(1)}, u32[]{:S(2)}, u32[]{:S(2)}) collective-permute-start(bf16[96,3072]{1,0:T(8,128)(2,1)S(1)} %collective-permute-done.9.refs_12_), channel_id=1, source_target_pairs={{0,192},{1,193},{2,194},{3,195},{8,200},{9,201},{10,202},{11,203},... | collective-permute-start | bytes 1769480 | tf_op jit(solution)/shard_map/ppermute | solution.py:188
  48.6 28.0 %collective-permute-done.15.refs_16_ = bf16[96,3072]{1,0:T(8,128)(2,1)S(1)} collective-permute-done((bf16[96,3072]{1,0:T(8,128)(2,1)S(1)}, bf16[96,3072]{1,0:T(8,128)(2,1)S(1)}, u32[]{:S(2)}, u32[]{:S(2)}) %collective-permute-start.15) | collective-permute-done | bytes 589856 | tf_op jit(solution)/shard_map/ppermute | solution.py:188
  76.6 2.9 %collective-permute-start.20 = (bf16[96,3072]{1,0:T(8,128)(2,1)S(1)}, bf16[96,3072]{1,0:T(8,128)(2,1)S(1)}, u32[]{:S(2)}, u32[]{:S(2)}) collective-permute-start(bf16[96,3072]{1,0:T(8,128)(2,1)S(1)} %collective-permute-done.15.refs_16_), channel_id=1, source_target_pairs={{0,192},{1,193},{2,194},{3,195},{8,200},{9,201},{10,202},{11,203},... | collective-permute-start | bytes 1769480 | tf_op jit(solution)/shard_map/ppermute | solution.py:188
  79.6 2.2 %collective-permute-start.8 = (bf16[96,3072]{1,0:T(8,128)(2,1)S(1)}, bf16[96,3072]{1,0:T(8,128)(2,1)S(1)}, u32[]{:S(2)}, u32[]{:S(2)}) collective-permute-start(bf16[96,3072]{1,0:T(8,128)(2,1)S(1)} %collective-permute-done.7.refs_6_), channel_id=1, source_target_pairs={{0,8},{1,9},{2,10},{3,11},{8,0},{9,1},{10,2},{11,3},{4,12},{5,13},... | collective-permute-start | bytes 1769480 | tf_op jit(solution)/shard_map/ppermute | solution.py:188
  82.3 8.1 %collective-permute-done.20.refs_20_ = bf16[96,3072]{1,0:T(8,128)(2,1)S(1)} collective-permute-done((bf16[96,3072]{1,0:T(8,128)(2,1)S(1)}, bf16[96,3072]{1,0:T(8,128)(2,1)S(1)}, u32[]{:S(2)}, u32[]{:S(2)}) %collective-permute-start.20) | collective-permute-done | bytes 589856 | tf_op jit(solution)/shard_map/ppermute | solution.py:188
  90.3 4.5 %collective-permute-start.23 = (bf16[96,3072]{1,0:T(8,128)(2,1)S(1)}, bf16[96,3072]{1,0:T(8,128)(2,1)}, u32[]{:S(2)}, u32[]{:S(2)}) collective-permute-start(bf16[96,3072]{1,0:T(8,128)(2,1)S(1)} %collective-permute-done.15.refs_16_), channel_id=1, source_target_pairs={{0,52},{1,53},{2,54},{3,55},{8,60},{9,61},{10,62},{11,63},{4,16},{... | collective-permute-start | bytes 1769480 | tf_op jit(solution)/shard_map/ppermute | solution.py:188
  94.8 2.7 %collective-permute-start.3 = (bf16[96,3072]{1,0:T(8,128)(2,1)S(1)}, bf16[96,3072]{1,0:T(8,128)(2,1)S(1)}, u32[]{:S(2)}, u32[]{:S(2)}) collective-permute-start(bf16[96,3072]{1,0:T(8,128)(2,1)S(1)} %copy-done.1), channel_id=1, source_target_pairs={{0,8},{1,9},{2,10},{3,11},{8,0},{9,1},{10,2},{11,3},{4,12},{5,13},... | collective-permute-start | bytes 1769480 | tf_op jit(solution)/shard_map/ppermute | solution.py:188
  98.2 7.9 %collective-permute-done.23.refs_24_ = bf16[96,3072]{1,0:T(8,128)(2,1)} collective-permute-done((bf16[96,3072]{1,0:T(8,128)(2,1)S(1)}, bf16[96,3072]{1,0:T(8,128)(2,1)}, u32[]{:S(2)}, u32[]{:S(2)}) %collective-permute-start.23) | collective-permute-done | bytes 589856 | tf_op jit(solution)/shard_map/ppermute | solution.py:188
  106.1 3.1 %collective-permute-start.14 = (bf16[96,3072]{1,0:T(8,128)(2,1)S(1)}, bf16[96,3072]{1,0:T(8,128)(2,1)}, u32[]{:S(2)}, u32[]{:S(2)}) collective-permute-start(bf16[96,3072]{1,0:T(8,128)(2,1)S(1)} %collective-permute-done.10.refs_14_), channel_id=1, source_target_pairs={{0,8},{1,9},{2,10},{3,11},{8,0},{9,1},{10,2},{11,3},{4,12},{5,13},... | collective-permute-start | bytes 1769480 | tf_op jit(solution)/shard_map/ppermute | solution.py:188
  109.2 0.9 collective-permute-start.17
  110.2 2.6 %collective-permute-start.27 = (bf16[96,3072]{1,0:T(8,128)(2,1)}, bf16[96,3072]{1,0:T(8,128)(2,1)}, u32[]{:S(2)}, u32[]{:S(2)}) collective-permute-start(bf16[96,3072]{1,0:T(8,128)(2,1)} %collective-permute-done.23.refs_24_), channel_id=1, source_target_pairs={{0,192},{1,193},{2,194},{3,195},{8,200},{9,201},{10,202},{11,203},... | collective-permute-start | bytes 1769480 | tf_op jit(solution)/shard_map/ppermute | solution.py:188
  113.6 0.8 copy-done.21
  114.4 8.4 %attend.2.refs_0_ = bf16[8,2,128,384]{3,2,1,0:T(8,128)(2,1)} custom-call(bf16[8,6,128,384]{3,2,1,0:T(8,128)(2,1)} %all-to-all-done.in_ref), custom_call_target="tpu_custom_call" | custom-call | flops 3221225472 | bytes 4194304 | tf_op jit(solution)/shard_map/attend/pallas_call | solution.py:103
  122.9 3.5 %collective-permute-done.17.refs_22_ = bf16[96,3072]{1,0:T(8,128)(2,1)} collective-permute-done((bf16[96,3072]{1,0:T(8,128)(2,1)S(1)}, bf16[96,3072]{1,0:T(8,128)(2,1)}, u32[]{:S(2)}, u32[]{:S(2)}) %collective-permute-start.17) | collective-permute-done | bytes 589856 | tf_op jit(solution)/shard_map/ppermute | solution.py:188
  126.3 5.3 %attend.3 = bf16[8,2,128,384]{3,2,1,0:T(8,128)(2,1)} custom-call(bf16[8,6,128,384]{3,2,1,0:T(8,128)(2,1)} %all-to-all-done.in_ref, bf16[8,2,128,384]{3,2,1,0:T(8,128)(2,1)} %attend.2.refs_0_), custom_call_target="tpu_custom_call", output_to_operand_aliasing={{}: (1, {})} | custom-call | flops 1610612736 | bytes 2097152 | tf_op jit(solution)/shard_map/attend/pallas_call | solution.py:103
  131.7 3.8 %all-to-all-start.1 = ((bf16[8,2,128,384]{3,2,1,0:T(8,128)(2,1)}), bf16[8,2,128,384]{3,2,1,0:T(8,128)(2,1)S(1)}, u32[]{:S(2)}, u32[]{:S(2)}) async-start(bf16[8,2,128,384]{3,2,1,0:T(8,128)(2,1)} %attend.3), calls=%async_computation.1 | async-start | bytes 3145728 | tf_op jit(solution)/shard_map/all_to_all | solution.py:240
  135.5 0.9 collective-permute-start.24
  136.4 2.0 %collective-permute-start.29 = (bf16[96,3072]{1,0:T(8,128)(2,1)}, bf16[96,3072]{1,0:T(8,128)(2,1)}, u32[]{:S(2)}, u32[]{:S(2)}) collective-permute-start(bf16[96,3072]{1,0:T(8,128)(2,1)} %collective-permute-done.27.refs_28_), channel_id=1, source_target_pairs={{0,192},{1,193},{2,194},{3,195},{8,200},{9,201},{10,202},{11,203},... | collective-permute-start | bytes 1769480 | tf_op jit(solution)/shard_map/ppermute | solution.py:188
  138.4 12.8 %collective-permute-done.24.refs_26_ = bf16[96,3072]{1,0:T(8,128)(2,1)} collective-permute-done((bf16[96,3072]{1,0:T(8,128)(2,1)}, bf16[96,3072]{1,0:T(8,128)(2,1)}, u32[]{:S(2)}, u32[]{:S(2)}) %collective-permute-start.24) | collective-permute-done | bytes 589856 | tf_op jit(solution)/shard_map/ppermute | solution.py:188
  151.2 1.7 collective-permute-start.28
  153.9 1.6 collective-permute-done.28.refs_29_
  156.0 2.0 %collective-permute-done.19.refs_19_ = bf16[96,3072]{1,0:T(8,128)(2,1)S(1)} collective-permute-done((bf16[96,3072]{1,0:T(8,128)(2,1)S(1)}, bf16[96,3072]{1,0:T(8,128)(2,1)S(1)}, u32[]{:S(2)}, u32[]{:S(2)}) %collective-permute-start.19) | collective-permute-done | bytes 589856 | tf_op jit(solution)/shard_map/ppermute | solution.py:188
  161.5 1.2 copy-done
  162.7 10.4 %project.1 = (bf16[1,128,3072]{2,1,0:T(8,128)(2,1)}, bf16[1,128,3072]{2,1,0:T(8,128)(2,1)}) custom-call(s32[32]{0:T(128)} %stack.131.place_ref, bf16[96,3072]{1,0:T(8,128)(2,1)} %refs_0_.3, bf16[96,3072]{1,0:T(8,128)(2,1)} %copy-done.18, bf16[96,3072]{1,0:T(8,128)(2,1)} %copy-done.4, bf16[96,3072]{1,0:T(8,128)(2,1)} %copy-done.16, ...), custom_call_target="tpu_custom_call" | custom-call | flops 4831838208 | bytes 18874368 | tf_op jit(solution)/shard_map/project/pallas_call | solution.py:163
  (93 shorter events, 7.1 us)
Async XLA Ops:
  5.8 108.7 %all-to-all-start = ((bf16[8,6,128,384]{3,2,1,0:T(8,128)(2,1)}), bf16[8,6,128,384]{3,2,1,0:T(8,128)(2,1)}, u32[]{:S(2)}, u32[]{:S(2)}) async-start(bf16[8,6,128,384]{3,2,1,0:T(8,128)(2,1)} %pack.1), calls=%async_computation | async-start | bytes 9437184 | tf_op jit(solution)/shard_map/all_to_all | solution.py:207
  12.3 17.9 %collective-permute-start = (bf16[96,3072]{1,0:T(8,128)(2,1)S(1)}, bf16[96,3072]{1,0:T(8,128)(2,1)S(1)}, u32[]{:S(2)}, u32[]{:S(2)}) collective-permute-start(bf16[96,3072]{1,0:T(8,128)(2,1)S(1)} %copy-done.1), channel_id=1, source_target_pairs={{0,52},{1,53},{2,54},{3,55},{8,60},{9,61},{10,62},{11,63},{4,16},{... | collective-permute-start | bytes 1769480 | tf_op jit(solution)/shard_map/ppermute | solution.py:188
  17.7 13.6 %collective-permute-start.5 = (bf16[96,3072]{1,0:T(8,128)(2,1)S(1)}, bf16[96,3072]{1,0:T(8,128)(2,1)S(1)}, u32[]{:S(2)}, u32[]{:S(2)}) collective-permute-start(bf16[96,3072]{1,0:T(8,128)(2,1)S(1)} %copy-done.1), channel_id=1, source_target_pairs={{0,192},{1,193},{2,194},{3,195},{8,200},{9,201},{10,202},{11,203},... | collective-permute-start | bytes 1769480 | tf_op jit(solution)/shard_map/ppermute | solution.py:188
  20.2 14.6 %collective-permute-start.1 = (bf16[96,3072]{1,0:T(8,128)(2,1)S(1)}, bf16[96,3072]{1,0:T(8,128)(2,1)S(1)}, u32[]{:S(2)}, u32[]{:S(2)}) collective-permute-start(bf16[96,3072]{1,0:T(8,128)(2,1)S(1)} %copy-done.1), channel_id=1, source_target_pairs={{0,64},{1,65},{2,66},{3,67},{8,72},{9,73},{10,74},{11,75},{4,68},{... | collective-permute-start | bytes 1769480 | tf_op jit(solution)/shard_map/ppermute | solution.py:188
  31.3 13.8 %collective-permute-start.9 = (bf16[96,3072]{1,0:T(8,128)(2,1)S(1)}, bf16[96,3072]{1,0:T(8,128)(2,1)S(1)}, u32[]{:S(2)}, u32[]{:S(2)}) collective-permute-start(bf16[96,3072]{1,0:T(8,128)(2,1)S(1)} %collective-permute-done.refs_8_), channel_id=1, source_target_pairs={{0,192},{1,193},{2,194},{3,195},{8,200},{9,201},{10,202},{11,203},... | collective-permute-start | bytes 1769480 | tf_op jit(solution)/shard_map/ppermute | solution.py:188
  34.8 41.8 %collective-permute-start.15 = (bf16[96,3072]{1,0:T(8,128)(2,1)S(1)}, bf16[96,3072]{1,0:T(8,128)(2,1)S(1)}, u32[]{:S(2)}, u32[]{:S(2)}) collective-permute-start(bf16[96,3072]{1,0:T(8,128)(2,1)S(1)} %collective-permute-done.refs_8_), channel_id=1, source_target_pairs={{0,4},{1,5},{2,6},{3,7},{8,12},{9,13},{10,14},{11,15},{4,0},{5,1},... | collective-permute-start | bytes 1769480 | tf_op jit(solution)/shard_map/ppermute | solution.py:188
  34.8 44.7 %collective-permute-start.7 = (bf16[96,3072]{1,0:T(8,128)(2,1)S(1)}, bf16[96,3072]{1,0:T(8,128)(2,1)S(1)}, u32[]{:S(2)}, u32[]{:S(2)}) collective-permute-start(bf16[96,3072]{1,0:T(8,128)(2,1)S(1)} %collective-permute-done.1.refs_2_), channel_id=1, source_target_pairs={{0,64},{1,65},{2,66},{3,67},{8,72},{9,73},{10,74},{11,75},{4,68},{... | collective-permute-start | bytes 1769480 | tf_op jit(solution)/shard_map/ppermute | solution.py:188
  34.9 44.7 %collective-permute-start.2 = (bf16[96,3072]{1,0:T(8,128)(2,1)S(1)}, bf16[96,3072]{1,0:T(8,128)(2,1)S(1)}, u32[]{:S(2)}, u32[]{:S(2)}) collective-permute-start(bf16[96,3072]{1,0:T(8,128)(2,1)S(1)} %collective-permute-done.refs_8_), channel_id=1, source_target_pairs={{0,64},{1,65},{2,66},{3,67},{8,72},{9,73},{10,74},{11,75},{4,68},{... | collective-permute-start | bytes 1769480 | tf_op jit(solution)/shard_map/ppermute | solution.py:188
  45.1 36.8 %collective-permute-start.10 = (bf16[96,3072]{1,0:T(8,128)(2,1)S(1)}, bf16[96,3072]{1,0:T(8,128)(2,1)S(1)}, u32[]{:S(2)}, u32[]{:S(2)}) collective-permute-start(bf16[96,3072]{1,0:T(8,128)(2,1)S(1)} %collective-permute-done.9.refs_12_), channel_id=1, source_target_pairs={{0,192},{1,193},{2,194},{3,195},{8,200},{9,201},{10,202},{11,203},... | collective-permute-start | bytes 1769480 | tf_op jit(solution)/shard_map/ppermute | solution.py:188
  76.6 13.7 %collective-permute-start.20 = (bf16[96,3072]{1,0:T(8,128)(2,1)S(1)}, bf16[96,3072]{1,0:T(8,128)(2,1)S(1)}, u32[]{:S(2)}, u32[]{:S(2)}) collective-permute-start(bf16[96,3072]{1,0:T(8,128)(2,1)S(1)} %collective-permute-done.15.refs_16_), channel_id=1, source_target_pairs={{0,192},{1,193},{2,194},{3,195},{8,200},{9,201},{10,202},{11,203},... | collective-permute-start | bytes 1769480 | tf_op jit(solution)/shard_map/ppermute | solution.py:188
  79.5 15.3 %collective-permute-start.16 = (bf16[96,3072]{1,0:T(8,128)(2,1)S(1)}, bf16[96,3072]{1,0:T(8,128)(2,1)S(1)}, u32[]{:S(2)}, u32[]{:S(2)}) collective-permute-start(bf16[96,3072]{1,0:T(8,128)(2,1)S(1)} %collective-permute-done.15.refs_16_), channel_id=1, source_target_pairs={{0,64},{1,65},{2,66},{3,67},{8,72},{9,73},{10,74},{11,75},{4,68},{... | collective-permute-start | bytes 1769480 | tf_op jit(solution)/shard_map/ppermute | solution.py:188
  79.6 18.0 %collective-permute-start.8 = (bf16[96,3072]{1,0:T(8,128)(2,1)S(1)}, bf16[96,3072]{1,0:T(8,128)(2,1)S(1)}, u32[]{:S(2)}, u32[]{:S(2)}) collective-permute-start(bf16[96,3072]{1,0:T(8,128)(2,1)S(1)} %collective-permute-done.7.refs_6_), channel_id=1, source_target_pairs={{0,8},{1,9},{2,10},{3,11},{8,0},{9,1},{10,2},{11,3},{4,12},{5,13},... | collective-permute-start | bytes 1769480 | tf_op jit(solution)/shard_map/ppermute | solution.py:188
  81.7 15.9 %collective-permute-start.4 = (bf16[96,3072]{1,0:T(8,128)(2,1)S(1)}, bf16[96,3072]{1,0:T(8,128)(2,1)S(1)}, u32[]{:S(2)}, u32[]{:S(2)}) collective-permute-start(bf16[96,3072]{1,0:T(8,128)(2,1)S(1)} %collective-permute-done.1.refs_2_), channel_id=1, source_target_pairs={{0,8},{1,9},{2,10},{3,11},{8,0},{9,1},{10,2},{11,3},{4,12},{5,13},... | collective-permute-start | bytes 1769480 | tf_op jit(solution)/shard_map/ppermute | solution.py:188
  81.9 16.2 %collective-permute-start.6 = (bf16[96,3072]{1,0:T(8,128)(2,1)S(1)}, bf16[96,3072]{1,0:T(8,128)(2,1)S(1)}, u32[]{:S(2)}, u32[]{:S(2)}) collective-permute-start(bf16[96,3072]{1,0:T(8,128)(2,1)S(1)} %collective-permute-done.5.refs_4_), channel_id=1, source_target_pairs={{0,8},{1,9},{2,10},{3,11},{8,0},{9,1},{10,2},{11,3},{4,12},{5,13},... | collective-permute-start | bytes 1769480 | tf_op jit(solution)/shard_map/ppermute | solution.py:188
  90.3 15.8 %collective-permute-start.23 = (bf16[96,3072]{1,0:T(8,128)(2,1)S(1)}, bf16[96,3072]{1,0:T(8,128)(2,1)}, u32[]{:S(2)}, u32[]{:S(2)}) collective-permute-start(bf16[96,3072]{1,0:T(8,128)(2,1)S(1)} %collective-permute-done.15.refs_16_), channel_id=1, source_target_pairs={{0,52},{1,53},{2,54},{3,55},{8,60},{9,61},{10,62},{11,63},{4,16},{... | collective-permute-start | bytes 1769480 | tf_op jit(solution)/shard_map/ppermute | solution.py:188
  94.8 14.4 %collective-permute-start.3 = (bf16[96,3072]{1,0:T(8,128)(2,1)S(1)}, bf16[96,3072]{1,0:T(8,128)(2,1)S(1)}, u32[]{:S(2)}, u32[]{:S(2)}) collective-permute-start(bf16[96,3072]{1,0:T(8,128)(2,1)S(1)} %copy-done.1), channel_id=1, source_target_pairs={{0,8},{1,9},{2,10},{3,11},{8,0},{9,1},{10,2},{11,3},{4,12},{5,13},... | collective-permute-start | bytes 1769480 | tf_op jit(solution)/shard_map/ppermute | solution.py:188
  97.6 12.6 %collective-permute-start.12 = (bf16[96,3072]{1,0:T(8,128)(2,1)S(1)}, bf16[96,3072]{1,0:T(8,128)(2,1)S(1)}, u32[]{:S(2)}, u32[]{:S(2)}) collective-permute-start(bf16[96,3072]{1,0:T(8,128)(2,1)S(1)} %collective-permute-done.2.refs_10_), channel_id=1, source_target_pairs={{0,8},{1,9},{2,10},{3,11},{8,0},{9,1},{10,2},{11,3},{4,12},{5,13},... | collective-permute-start | bytes 1769480 | tf_op jit(solution)/shard_map/ppermute | solution.py:188
  97.7 15.1 %collective-permute-start.13 = (bf16[96,3072]{1,0:T(8,128)(2,1)S(1)}, bf16[96,3072]{1,0:T(8,128)(2,1)S(1)}, u32[]{:S(2)}, u32[]{:S(2)}) collective-permute-start(bf16[96,3072]{1,0:T(8,128)(2,1)S(1)} %collective-permute-done.9.refs_12_), channel_id=1, source_target_pairs={{0,8},{1,9},{2,10},{3,11},{8,0},{9,1},{10,2},{11,3},{4,12},{5,13},... | collective-permute-start | bytes 1769480 | tf_op jit(solution)/shard_map/ppermute | solution.py:188
  98.1 14.6 %collective-permute-start.11 = (bf16[96,3072]{1,0:T(8,128)(2,1)S(1)}, bf16[96,3072]{1,0:T(8,128)(2,1)S(1)}, u32[]{:S(2)}, u32[]{:S(2)}) collective-permute-start(bf16[96,3072]{1,0:T(8,128)(2,1)S(1)} %collective-permute-done.refs_8_), channel_id=1, source_target_pairs={{0,8},{1,9},{2,10},{3,11},{8,0},{9,1},{10,2},{11,3},{4,12},{5,13},... | collective-permute-start | bytes 1769480 | tf_op jit(solution)/shard_map/ppermute | solution.py:188
  106.1 8.3 %collective-permute-start.14 = (bf16[96,3072]{1,0:T(8,128)(2,1)S(1)}, bf16[96,3072]{1,0:T(8,128)(2,1)}, u32[]{:S(2)}, u32[]{:S(2)}) collective-permute-start(bf16[96,3072]{1,0:T(8,128)(2,1)S(1)} %collective-permute-done.10.refs_14_), channel_id=1, source_target_pairs={{0,8},{1,9},{2,10},{3,11},{8,0},{9,1},{10,2},{11,3},{4,12},{5,13},... | collective-permute-start | bytes 1769480 | tf_op jit(solution)/shard_map/ppermute | solution.py:188
  109.2 17.1 %collective-permute-start.17 = (bf16[96,3072]{1,0:T(8,128)(2,1)S(1)}, bf16[96,3072]{1,0:T(8,128)(2,1)}, u32[]{:S(2)}, u32[]{:S(2)}) collective-permute-start(bf16[96,3072]{1,0:T(8,128)(2,1)S(1)} %collective-permute-done.16.refs_18_), channel_id=1, source_target_pairs={{0,64},{1,65},{2,66},{3,67},{8,72},{9,73},{10,74},{11,75},{4,68},{... | collective-permute-start | bytes 1769480 | tf_op jit(solution)/shard_map/ppermute | solution.py:188
  110.2 16.2 %collective-permute-start.27 = (bf16[96,3072]{1,0:T(8,128)(2,1)}, bf16[96,3072]{1,0:T(8,128)(2,1)}, u32[]{:S(2)}, u32[]{:S(2)}) collective-permute-start(bf16[96,3072]{1,0:T(8,128)(2,1)} %collective-permute-done.23.refs_24_), channel_id=1, source_target_pairs={{0,192},{1,193},{2,194},{3,195},{8,200},{9,201},{10,202},{11,203},... | collective-permute-start | bytes 1769480 | tf_op jit(solution)/shard_map/ppermute | solution.py:188
  131.7 29.0 %all-to-all-start.1 = ((bf16[8,2,128,384]{3,2,1,0:T(8,128)(2,1)}), bf16[8,2,128,384]{3,2,1,0:T(8,128)(2,1)S(1)}, u32[]{:S(2)}, u32[]{:S(2)}) async-start(bf16[8,2,128,384]{3,2,1,0:T(8,128)(2,1)} %attend.3), calls=%async_computation.1 | async-start | bytes 3145728 | tf_op jit(solution)/shard_map/all_to_all | solution.py:240
  135.5 15.7 %collective-permute-start.24 = (bf16[96,3072]{1,0:T(8,128)(2,1)}, bf16[96,3072]{1,0:T(8,128)(2,1)}, u32[]{:S(2)}, u32[]{:S(2)}) collective-permute-start(bf16[96,3072]{1,0:T(8,128)(2,1)} %collective-permute-done.23.refs_24_), channel_id=1, source_target_pairs={{0,64},{1,65},{2,66},{3,67},{8,72},{9,73},{10,74},{11,75},{4,68},{... | collective-permute-start | bytes 1769480 | tf_op jit(solution)/shard_map/ppermute | solution.py:188
  136.4 17.1 %collective-permute-start.29 = (bf16[96,3072]{1,0:T(8,128)(2,1)}, bf16[96,3072]{1,0:T(8,128)(2,1)}, u32[]{:S(2)}, u32[]{:S(2)}) collective-permute-start(bf16[96,3072]{1,0:T(8,128)(2,1)} %collective-permute-done.27.refs_28_), channel_id=1, source_target_pairs={{0,192},{1,193},{2,194},{3,195},{8,200},{9,201},{10,202},{11,203},... | collective-permute-start | bytes 1769480 | tf_op jit(solution)/shard_map/ppermute | solution.py:188
  151.2 4.3 %collective-permute-start.28 = (bf16[96,3072]{1,0:T(8,128)(2,1)}, bf16[96,3072]{1,0:T(8,128)(2,1)S(1)}, u32[]{:S(2)}, u32[]{:S(2)}) collective-permute-start(bf16[96,3072]{1,0:T(8,128)(2,1)} %collective-permute-done.27.refs_28_), channel_id=1, source_target_pairs={{0,8},{1,9},{2,10},{3,11},{8,0},{9,1},{10,2},{11,3},{4,12},{5,13},... | collective-permute-start | bytes 1769480 | tf_op jit(solution)/shard_map/ppermute | solution.py:188
  152.9 3.0 %collective-permute-start.21 = (bf16[96,3072]{1,0:T(8,128)(2,1)S(1)}, bf16[96,3072]{1,0:T(8,128)(2,1)S(1)}, u32[]{:S(2)}, u32[]{:S(2)}) collective-permute-start(bf16[96,3072]{1,0:T(8,128)(2,1)S(1)} %copy-done.12), channel_id=1, source_target_pairs={{0,8},{1,9},{2,10},{3,11},{8,0},{9,1},{10,2},{11,3},{4,12},{5,13},... | collective-permute-start | bytes 1769480 | tf_op jit(solution)/shard_map/ppermute | solution.py:188
  152.9 5.1 %collective-permute-start.19 = (bf16[96,3072]{1,0:T(8,128)(2,1)S(1)}, bf16[96,3072]{1,0:T(8,128)(2,1)S(1)}, u32[]{:S(2)}, u32[]{:S(2)}) collective-permute-start(bf16[96,3072]{1,0:T(8,128)(2,1)S(1)} %copy-done.14), channel_id=1, source_target_pairs={{0,8},{1,9},{2,10},{3,11},{8,0},{9,1},{10,2},{11,3},{4,12},{5,13},... | collective-permute-start | bytes 1769480 | tf_op jit(solution)/shard_map/ppermute | solution.py:188
  153.4 6.1 %collective-permute-start.25 = (bf16[96,3072]{1,0:T(8,128)(2,1)}, bf16[96,3072]{1,0:T(8,128)(2,1)}, u32[]{:S(2)}, u32[]{:S(2)}) collective-permute-start(bf16[96,3072]{1,0:T(8,128)(2,1)} %collective-permute-done.23.refs_24_), channel_id=1, source_target_pairs={{0,8},{1,9},{2,10},{3,11},{8,0},{9,1},{10,2},{11,3},{4,12},{5,13},... | collective-permute-start | bytes 1769480 | tf_op jit(solution)/shard_map/ppermute | solution.py:188
  153.5 6.0 %collective-permute-start.18 = (bf16[96,3072]{1,0:T(8,128)(2,1)S(1)}, bf16[96,3072]{1,0:T(8,128)(2,1)}, u32[]{:S(2)}, u32[]{:S(2)}) collective-permute-start(bf16[96,3072]{1,0:T(8,128)(2,1)S(1)} %copy-done.7), channel_id=1, source_target_pairs={{0,8},{1,9},{2,10},{3,11},{8,0},{9,1},{10,2},{11,3},{4,12},{5,13},... | collective-permute-start | bytes 1769480 | tf_op jit(solution)/shard_map/ppermute | solution.py:188
  155.5 4.4 %collective-permute-start.26 = (bf16[96,3072]{1,0:T(8,128)(2,1)}, bf16[96,3072]{1,0:T(8,128)(2,1)}, u32[]{:S(2)}, u32[]{:S(2)}) collective-permute-start(bf16[96,3072]{1,0:T(8,128)(2,1)} %collective-permute-done.24.refs_26_), channel_id=1, source_target_pairs={{0,8},{1,9},{2,10},{3,11},{8,0},{9,1},{10,2},{11,3},{4,12},{5,13},... | collective-permute-start | bytes 1769480 | tf_op jit(solution)/shard_map/ppermute | solution.py:188
  155.9 4.0 %collective-permute-start.22 = (bf16[96,3072]{1,0:T(8,128)(2,1)}, bf16[96,3072]{1,0:T(8,128)(2,1)S(1)}, u32[]{:S(2)}, u32[]{:S(2)}) collective-permute-start(bf16[96,3072]{1,0:T(8,128)(2,1)} %collective-permute-done.17.refs_22_), channel_id=1, source_target_pairs={{0,8},{1,9},{2,10},{3,11},{8,0},{9,1},{10,2},{11,3},{4,12},{5,13},... | collective-permute-start | bytes 1769480 | tf_op jit(solution)/shard_map/ppermute | solution.py:188
  (28 other events, 659.3 us)

commit v2 on v1

--- a/solution.py
+++ b/solution.py
@@ -30,7 +30,7 @@
 NEXT_X = moves(lambda x, z, core, y: (x + 1, z, core, y))
 LAST_X = moves(lambda x, z, core, y: (x - 1, z, core, y))
 OUTER_Z = moves(lambda x, z, core, y: (x, z + 1 if z % 2 else z - 1, core, y))
-INNER_Z = moves(lambda x, z, core, y: (x, z - 1 if z % 2 else z + 1, core, y))
+THROUGH_Z = moves(lambda x, z, core, y: (x, z + 2 if z % 2 else z - 2, core, y))
 OTHER_CORE = moves(lambda x, z, core, y: (x, z, 1 - core, y))
 
 
@@ -204,18 +204,18 @@
     arrays = (query_rows, key_rows, value_rows, query_tangent, key_tangent, value_tangent)
 
     sent = pack(arrays, lax.axis_size("seq"))
-    received = lax.all_to_all(sent, "seq", 0, 0, tiled=True)
-
     z, before, later, far = {0: out_weight}, {}, {}, {}
-    z[1] = send(z[0], OUTER_Z)
+    z[1] = send(z[0], THROUGH_Z)
     before[0] = send(z[0], NEXT_X)
     later[0] = send(z[0], LAST_X)
-    z[2] = send(z[1], INNER_Z, sent)
-    far[0] = send(before[0], NEXT_X, sent)
-    later[1] = send(z[1], LAST_X, later[0], sent)
+    sent = lax.optimization_barrier((sent, z[1], before[0], later[0]))[0]
+    received = lax.all_to_all(sent, "seq", 0, 0, tiled=True)
+    z[2] = send(z[0], OUTER_Z, z[1])
+    far[0] = send(before[0], NEXT_X)
+    later[1] = send(z[1], LAST_X)
     before[1] = send(z[1], NEXT_X, before[0])
-    far[1] = send(later[1], LAST_X)
-    z[3] = send(z[2], OUTER_Z)
+    far[1] = send(later[1], LAST_X, later[0])
+    z[3] = send(z[1], OUTER_Z)
     before[2] = send(z[2], NEXT_X, far[0])
     later[2] = send(z[2], LAST_X, later[1])
     far[2] = send(before[2], NEXT_X, before[1])
@@ -225,7 +225,7 @@
 
     freed = (before[1], far[1], far[2], before[3])
     weights, swapped, places = [], {}, []
-    for at, pairs in enumerate((0, toward, -toward, 2)):
+    for at, pairs in enumerate((0, -toward, toward, 2)):
         for block, steps in ((z[at], 0), (before[at], -1), (later[at], 1), (far[at], 2)):
             place = (x + steps) % 4 * 8 + (z_pair + pairs) % 4 * 2
             swapped[at, steps] = send(block, OTHER_CORE, freed[at])

time: 174 us -> 142 us (0.82)
  waiting for transfers between devices: 86.2 us -> 65.1 us
  starting transfers between devices: 52 us -> 42.1 us
    ppermute x31, waiting for transfers between devices: 86.2 us -> 62.5 us  [send(): return lax.ppermute(value, AXES, moves_of)]
    ppermute x31, starting transfers between devices: 41.7 us -> 33 us  [send(): return lax.ppermute(value, AXES, moves_of)]
    all_to_all x1, waiting for transfers between devices: 0.01 us -> 2.54 us  [on_device(): received = lax.all_to_all(sent, 'seq', 0, 0, tiled=True)]
    all_to_all x1, starting transfers between devices: 6.51 us -> 4.62 us  [on_device(): received = lax.all_to_all(sent, 'seq', 0, 0, tiled=True)]
    unnamed x54 -> x50, local copies, waits for them, and re-layouts: 4.07 us -> 3.56 us
  transfers between devices with their start and end apart: 33 -> 33, of which waited for: 12 -> 14; matrix products, arithmetic and copies ran while one was open for 0% -> 0% of each run, Pallas kernels for 5% -> 10%
where the time goes in v2:
time: 142 us
  waiting for transfers between devices  65.1 us (46%)
  starting transfers between devices  42.1 us (30%)
  Pallas kernels  29.5 us (21%)
  local copies, waits for them, and re-layouts  4.16 us (3%)
    ppermute x31, waiting for transfers between devices, send(): return lax.ppermute(value, AXES, moves_of)  62.5 us
    ppermute x31, starting transfers between devices, send(): return lax.ppermute(value, AXES, moves_of)  33 us
    pallas_call x2, Pallas kernels, attend(): pl.pallas_call(attend_kernel, grid=(heads,), in_specs=[pl.BlockSpec((piec...  13.9 us
    pallas_call x1, Pallas kernels, project(): pl.pallas_call(project_kernel, in_specs=[pl.BlockSpec(memory_space=pltpu....  10.4 us
    pallas_call x1, Pallas kernels, pack(): pl.pallas_call(pack_kernel, grid=(rows // block,), in_specs=[pl.BlockSpec...  5.13 us
    all_to_all x1, starting transfers between devices, on_device(): received = lax.all_to_all(sent, 'seq', 0, 0, tiled=True)  4.62 us
    all_to_all x1, starting transfers between devices, on_device(): results = lax.all_to_all(results, 'seq', 0, 0, tiled=True)  4.45 us
    unnamed x50, local copies, waits for them, and re-layouts  3.56 us
  transfers between devices with their start and end apart: 33, of which 14 were waited for; matrix products, arithmetic and copies ran while one was open for 0% of the time, Pallas kernels for 10%

profile of v2, /device:TPU:1, one launch (start us, length us, event | category | flops | bytes accessed | tf_op | source)
XLA Modules:
  0.0 141.8 jit_solution(11464741063948247269)
XLA Ops:
  0.6 6.9 %collective-permute-start = (bf16[96,3072]{1,0:T(8,128)(2,1)}, bf16[96,3072]{1,0:T(8,128)(2,1)S(1)}, u32[]{:S(2)}, u32[]{:S(2)}) collective-permute-start(bf16[96,3072]{1,0:T(8,128)(2,1)} %refs_0_.3), channel_id=1, source_target_pairs={{0,48},{1,49},{2,50},{3,51},{8,56},{9,57},{10,58},{11,59},{4,20},{... | collective-permute-start | bytes 1769480 | tf_op jit(solution)/shard_map/ppermute | solution.py:188
  7.6 2.5 %collective-permute-start.5 = (bf16[96,3072]{1,0:T(8,128)(2,1)}, bf16[96,3072]{1,0:T(8,128)(2,1)S(1)}, u32[]{:S(2)}, u32[]{:S(2)}) collective-permute-start(bf16[96,3072]{1,0:T(8,128)(2,1)} %refs_0_.3), channel_id=1, source_target_pairs={{0,192},{1,193},{2,194},{3,195},{8,200},{9,201},{10,202},{11,203},... | collective-permute-start | bytes 1769480 | tf_op jit(solution)/shard_map/ppermute | solution.py:188
  10.0 5.1 %pack.1 = bf16[8,6,128,384]{3,2,1,0:T(8,128)(2,1)} custom-call(bf16[1,128,3072]{2,1,0:T(8,128)(2,1)} %refs_0_.2, bf16[1,128,3072]{2,1,0:T(8,128)(2,1)} %refs_1_.1, bf16[1,128,3072]{2,1,0:T(8,128)(2,1)} %refs_2_.1, bf16[1,128,3072]{2,1,0:T(8,128)(2,1)} %refs_3_.1, bf16[1,128,3072]{2,1,0:T(8,128)(2,1)} %refs_4_.1, bf16[1,128,3072]{2,1,0:T(8,128)(2,1)} %refs_5_.1), custom_call_target="tpu_custom_call" | custom-call | bytes 9437184 | tf_op jit(solution)/shard_map/pack/pallas_call | solution.py:48
  15.2 4.7 %collective-permute-done.refs_8_ = bf16[96,3072]{1,0:T(8,128)(2,1)S(1)} collective-permute-done((bf16[96,3072]{1,0:T(8,128)(2,1)}, bf16[96,3072]{1,0:T(8,128)(2,1)S(1)}, u32[]{:S(2)}, u32[]{:S(2)}) %collective-permute-start) | collective-permute-done | bytes 589856 | tf_op jit(solution)/shard_map/ppermute | solution.py:188
  19.9 2.2 %collective-permute-done.5.refs_4_ = bf16[96,3072]{1,0:T(8,128)(2,1)S(1)} collective-permute-done((bf16[96,3072]{1,0:T(8,128)(2,1)}, bf16[96,3072]{1,0:T(8,128)(2,1)S(1)}, u32[]{:S(2)}, u32[]{:S(2)}) %collective-permute-start.5) | collective-permute-done | bytes 589856 | tf_op jit(solution)/shard_map/ppermute | solution.py:188
  22.0 3.0 %collective-permute-done.1.refs_2_ = bf16[96,3072]{1,0:T(8,128)(2,1)S(1)} collective-permute-done((bf16[96,3072]{1,0:T(8,128)(2,1)}, bf16[96,3072]{1,0:T(8,128)(2,1)S(1)}, u32[]{:S(2)}, u32[]{:S(2)}) %collective-permute-start.1) | collective-permute-done | bytes 589856 | tf_op jit(solution)/shard_map/ppermute | solution.py:188
  25.0 4.6 %all-to-all-start = ((bf16[8,6,128,384]{3,2,1,0:T(8,128)(2,1)}), bf16[8,6,128,384]{3,2,1,0:T(8,128)(2,1)}, u32[]{:S(2)}, u32[]{:S(2)}) async-start(bf16[8,6,128,384]{3,2,1,0:T(8,128)(2,1)} %pack.1), calls=%async_computation | async-start | bytes 9437184 | tf_op jit(solution)/shard_map/all_to_all | solution.py:212
  30.1 1.2 collective-permute-start.2
  31.3 1.3 collective-permute-start.15
  32.5 1.4 collective-permute-start.23
  33.9 8.6 %collective-permute-done.9.refs_12_ = bf16[96,3072]{1,0:T(8,128)(2,1)S(1)} collective-permute-done((bf16[96,3072]{1,0:T(8,128)(2,1)S(1)}, bf16[96,3072]{1,0:T(8,128)(2,1)S(1)}, u32[]{:S(2)}, u32[]{:S(2)}) %collective-permute-start.9) | collective-permute-done | bytes 589856 | tf_op jit(solution)/shard_map/ppermute | solution.py:188
  42.5 1.8 %collective-permute-start.10 = (bf16[96,3072]{1,0:T(8,128)(2,1)S(1)}, bf16[96,3072]{1,0:T(8,128)(2,1)S(1)}, u32[]{:S(2)}, u32[]{:S(2)}) collective-permute-start(bf16[96,3072]{1,0:T(8,128)(2,1)S(1)} %collective-permute-done.9.refs_12_), channel_id=1, source_target_pairs={{0,192},{1,193},{2,194},{3,195},{8,200},{9,201},{10,202},{11,203},... | collective-permute-start | bytes 1769480 | tf_op jit(solution)/shard_map/ppermute | solution.py:188
  44.3 12.4 %collective-permute-done.7.refs_6_ = bf16[96,3072]{1,0:T(8,128)(2,1)S(1)} collective-permute-done((bf16[96,3072]{1,0:T(8,128)(2,1)S(1)}, bf16[96,3072]{1,0:T(8,128)(2,1)S(1)}, u32[]{:S(2)}, u32[]{:S(2)}) %collective-permute-start.7) | collective-permute-done | bytes 589856 | tf_op jit(solution)/shard_map/ppermute | solution.py:188
  56.7 3.0 %collective-permute-start.8 = (bf16[96,3072]{1,0:T(8,128)(2,1)S(1)}, bf16[96,3072]{1,0:T(8,128)(2,1)S(1)}, u32[]{:S(2)}, u32[]{:S(2)}) collective-permute-start(bf16[96,3072]{1,0:T(8,128)(2,1)S(1)} %collective-permute-done.7.refs_6_), channel_id=1, source_target_pairs={{0,8},{1,9},{2,10},{3,11},{8,0},{9,1},{10,2},{11,3},{4,12},{5,13},... | collective-permute-start | bytes 1769480 | tf_op jit(solution)/shard_map/ppermute | solution.py:188
  59.9 1.1 collective-permute-start.6
  62.3 12.3 %collective-permute-done.20.refs_20_ = bf16[96,3072]{1,0:T(8,128)(2,1)S(1)} collective-permute-done((bf16[96,3072]{1,0:T(8,128)(2,1)S(1)}, bf16[96,3072]{1,0:T(8,128)(2,1)S(1)}, u32[]{:S(2)}, u32[]{:S(2)}) %collective-permute-start.20) | collective-permute-done | bytes 589856 | tf_op jit(solution)/shard_map/ppermute | solution.py:188
  76.2 1.0 collective-permute-done.16.refs_18_
  77.2 0.9 collective-permute-start.14
  78.1 2.7 %collective-permute-start.27 = (bf16[96,3072]{1,0:T(8,128)(2,1)}, bf16[96,3072]{1,0:T(8,128)(2,1)}, u32[]{:S(2)}, u32[]{:S(2)}) collective-permute-start(bf16[96,3072]{1,0:T(8,128)(2,1)} %collective-permute-done.23.refs_24_), channel_id=1, source_target_pairs={{0,192},{1,193},{2,194},{3,195},{8,200},{9,201},{10,202},{11,203},... | collective-permute-start | bytes 1769480 | tf_op jit(solution)/shard_map/ppermute | solution.py:188
  81.6 2.5 %all-to-all-done.in_ref = bf16[8,6,128,384]{3,2,1,0:T(8,128)(2,1)} async-done(((bf16[8,6,128,384]{3,2,1,0:T(8,128)(2,1)}), bf16[8,6,128,384]{3,2,1,0:T(8,128)(2,1)}, u32[]{:S(2)}, u32[]{:S(2)}) %all-to-all-start) | async-done | bytes 4718624 | tf_op jit(solution)/shard_map/all_to_all | solution.py:212
  84.1 8.4 %attend.2.refs_0_ = bf16[8,2,128,384]{3,2,1,0:T(8,128)(2,1)} custom-call(bf16[8,6,128,384]{3,2,1,0:T(8,128)(2,1)} %all-to-all-done.in_ref), custom_call_target="tpu_custom_call" | custom-call | flops 3221225472 | bytes 4194304 | tf_op jit(solution)/shard_map/attend/pallas_call | solution.py:103
  92.6 1.8 %collective-permute-done.17.refs_22_ = bf16[96,3072]{1,0:T(8,128)(2,1)S(1)} collective-permute-done((bf16[96,3072]{1,0:T(8,128)(2,1)}, bf16[96,3072]{1,0:T(8,128)(2,1)S(1)}, u32[]{:S(2)}, u32[]{:S(2)}) %collective-permute-start.17) | collective-permute-done | bytes 589856 | tf_op jit(solution)/shard_map/ppermute | solution.py:188
  94.4 5.5 %attend.3 = bf16[8,2,128,384]{3,2,1,0:T(8,128)(2,1)} custom-call(bf16[8,6,128,384]{3,2,1,0:T(8,128)(2,1)} %all-to-all-done.in_ref, bf16[8,2,128,384]{3,2,1,0:T(8,128)(2,1)} %attend.2.refs_0_), custom_call_target="tpu_custom_call", output_to_operand_aliasing={{}: (1, {})} | custom-call | flops 1610612736 | bytes 2097152 | tf_op jit(solution)/shard_map/attend/pallas_call | solution.py:103
  99.9 4.4 %all-to-all-start.1 = ((bf16[8,2,128,384]{3,2,1,0:T(8,128)(2,1)}), bf16[8,2,128,384]{3,2,1,0:T(8,128)(2,1)S(1)}, u32[]{:S(2)}, u32[]{:S(2)}) async-start(bf16[8,2,128,384]{3,2,1,0:T(8,128)(2,1)} %attend.3), calls=%async_computation.1 | async-start | bytes 3145728 | tf_op jit(solution)/shard_map/all_to_all | solution.py:240
  104.3 2.7 %collective-permute-start.29 = (bf16[96,3072]{1,0:T(8,128)(2,1)}, bf16[96,3072]{1,0:T(8,128)(2,1)}, u32[]{:S(2)}, u32[]{:S(2)}) collective-permute-start(bf16[96,3072]{1,0:T(8,128)(2,1)} %collective-permute-done.27.refs_28_), channel_id=1, source_target_pairs={{0,192},{1,193},{2,194},{3,195},{8,200},{9,201},{10,202},{11,203},... | collective-permute-start | bytes 1769480 | tf_op jit(solution)/shard_map/ppermute | solution.py:188
  107.0 12.5 %collective-permute-done.24.refs_26_ = bf16[96,3072]{1,0:T(8,128)(2,1)} collective-permute-done((bf16[96,3072]{1,0:T(8,128)(2,1)}, bf16[96,3072]{1,0:T(8,128)(2,1)}, u32[]{:S(2)}, u32[]{:S(2)}) %collective-permute-start.24) | collective-permute-done | bytes 589856 | tf_op jit(solution)/shard_map/ppermute | solution.py:188
  119.5 2.1 %collective-permute-start.28 = (bf16[96,3072]{1,0:T(8,128)(2,1)}, bf16[96,3072]{1,0:T(8,128)(2,1)S(1)}, u32[]{:S(2)}, u32[]{:S(2)}) collective-permute-start(bf16[96,3072]{1,0:T(8,128)(2,1)} %collective-permute-done.27.refs_28_), channel_id=1, source_target_pairs={{0,8},{1,9},{2,10},{3,11},{8,0},{9,1},{10,2},{11,3},{4,12},{5,13},... | collective-permute-start | bytes 1769480 | tf_op jit(solution)/shard_map/ppermute | solution.py:188
  122.6 1.6 %collective-permute-done.28.refs_29_ = bf16[96,3072]{1,0:T(8,128)(2,1)S(1)} collective-permute-done((bf16[96,3072]{1,0:T(8,128)(2,1)}, bf16[96,3072]{1,0:T(8,128)(2,1)S(1)}, u32[]{:S(2)}, u32[]{:S(2)}) %collective-permute-start.28) | collective-permute-done | bytes 589856 | tf_op jit(solution)/shard_map/ppermute | solution.py:188
  125.9 0.9 collective-permute-done.19.refs_19_
  128.7 1.3 collective-permute-done.30.refs_31_
  130.0 1.2 copy-done
  131.2 10.4 %project.1 = (bf16[1,128,3072]{2,1,0:T(8,128)(2,1)}, bf16[1,128,3072]{2,1,0:T(8,128)(2,1)}) custom-call(s32[32]{0:T(128)} %stack.131.place_ref, bf16[96,3072]{1,0:T(8,128)(2,1)} %refs_0_.3, bf16[96,3072]{1,0:T(8,128)(2,1)} %copy-done.16, bf16[96,3072]{1,0:T(8,128)(2,1)} %copy-done.4, bf16[96,3072]{1,0:T(8,128)(2,1)} %copy-done.14, ...), custom_call_target="tpu_custom_call" | custom-call | flops 4831838208 | bytes 18874368 | tf_op jit(solution)/shard_map/project/pallas_call | solution.py:163
  (89 shorter events, 8.9 us)
Async XLA Ops:
  0.6 19.2 %collective-permute-start = (bf16[96,3072]{1,0:T(8,128)(2,1)}, bf16[96,3072]{1,0:T(8,128)(2,1)S(1)}, u32[]{:S(2)}, u32[]{:S(2)}) collective-permute-start(bf16[96,3072]{1,0:T(8,128)(2,1)} %refs_0_.3), channel_id=1, source_target_pairs={{0,48},{1,49},{2,50},{3,51},{8,56},{9,57},{10,58},{11,59},{4,20},{... | collective-permute-start | bytes 1769480 | tf_op jit(solution)/shard_map/ppermute | solution.py:188
  7.6 14.5 %collective-permute-start.5 = (bf16[96,3072]{1,0:T(8,128)(2,1)}, bf16[96,3072]{1,0:T(8,128)(2,1)S(1)}, u32[]{:S(2)}, u32[]{:S(2)}) collective-permute-start(bf16[96,3072]{1,0:T(8,128)(2,1)} %refs_0_.3), channel_id=1, source_target_pairs={{0,192},{1,193},{2,194},{3,195},{8,200},{9,201},{10,202},{11,203},... | collective-permute-start | bytes 1769480 | tf_op jit(solution)/shard_map/ppermute | solution.py:188
  10.0 15.0 %collective-permute-start.1 = (bf16[96,3072]{1,0:T(8,128)(2,1)}, bf16[96,3072]{1,0:T(8,128)(2,1)S(1)}, u32[]{:S(2)}, u32[]{:S(2)}) collective-permute-start(bf16[96,3072]{1,0:T(8,128)(2,1)} %refs_0_.3), channel_id=1, source_target_pairs={{0,64},{1,65},{2,66},{3,67},{8,72},{9,73},{10,74},{11,75},{4,68},{... | collective-permute-start | bytes 1769480 | tf_op jit(solution)/shard_map/ppermute | solution.py:188
  25.0 59.1 %all-to-all-start = ((bf16[8,6,128,384]{3,2,1,0:T(8,128)(2,1)}), bf16[8,6,128,384]{3,2,1,0:T(8,128)(2,1)}, u32[]{:S(2)}, u32[]{:S(2)}) async-start(bf16[8,6,128,384]{3,2,1,0:T(8,128)(2,1)} %pack.1), calls=%async_computation | async-start | bytes 9437184 | tf_op jit(solution)/shard_map/all_to_all | solution.py:212
  29.7 12.8 %collective-permute-start.9 = (bf16[96,3072]{1,0:T(8,128)(2,1)S(1)}, bf16[96,3072]{1,0:T(8,128)(2,1)S(1)}, u32[]{:S(2)}, u32[]{:S(2)}) collective-permute-start(bf16[96,3072]{1,0:T(8,128)(2,1)S(1)} %collective-permute-done.refs_8_), channel_id=1, source_target_pairs={{0,192},{1,193},{2,194},{3,195},{8,200},{9,201},{10,202},{11,203},... | collective-permute-start | bytes 1769480 | tf_op jit(solution)/shard_map/ppermute | solution.py:188
  30.1 14.3 %collective-permute-start.2 = (bf16[96,3072]{1,0:T(8,128)(2,1)S(1)}, bf16[96,3072]{1,0:T(8,128)(2,1)S(1)}, u32[]{:S(2)}, u32[]{:S(2)}) collective-permute-start(bf16[96,3072]{1,0:T(8,128)(2,1)S(1)} %collective-permute-done.refs_8_), channel_id=1, source_target_pairs={{0,64},{1,65},{2,66},{3,67},{8,72},{9,73},{10,74},{11,75},{4,68},{... | collective-permute-start | bytes 1769480 | tf_op jit(solution)/shard_map/ppermute | solution.py:188
  31.2 25.5 %collective-permute-start.7 = (bf16[96,3072]{1,0:T(8,128)(2,1)S(1)}, bf16[96,3072]{1,0:T(8,128)(2,1)S(1)}, u32[]{:S(2)}, u32[]{:S(2)}) collective-permute-start(bf16[96,3072]{1,0:T(8,128)(2,1)S(1)} %collective-permute-done.1.refs_2_), channel_id=1, source_target_pairs={{0,64},{1,65},{2,66},{3,67},{8,72},{9,73},{10,74},{11,75},{4,68},{... | collective-permute-start | bytes 1769480 | tf_op jit(solution)/shard_map/ppermute | solution.py:188
  31.3 28.4 %collective-permute-start.15 = (bf16[96,3072]{1,0:T(8,128)(2,1)S(1)}, bf16[96,3072]{1,0:T(8,128)(2,1)S(1)}, u32[]{:S(2)}, u32[]{:S(2)}) collective-permute-start(bf16[96,3072]{1,0:T(8,128)(2,1)S(1)} %copy-done.1), channel_id=1, source_target_pairs={{0,52},{1,53},{2,54},{3,55},{8,60},{9,61},{10,62},{11,63},{4,16},{... | collective-permute-start | bytes 1769480 | tf_op jit(solution)/shard_map/ppermute | solution.py:188
  32.5 27.3 %collective-permute-start.23 = (bf16[96,3072]{1,0:T(8,128)(2,1)S(1)}, bf16[96,3072]{1,0:T(8,128)(2,1)}, u32[]{:S(2)}, u32[]{:S(2)}) collective-permute-start(bf16[96,3072]{1,0:T(8,128)(2,1)S(1)} %collective-permute-done.refs_8_), channel_id=1, source_target_pairs={{0,52},{1,53},{2,54},{3,55},{8,60},{9,61},{10,62},{11,63},{4,16},{... | collective-permute-start | bytes 1769480 | tf_op jit(solution)/shard_map/ppermute | solution.py:188
  42.5 18.4 %collective-permute-start.10 = (bf16[96,3072]{1,0:T(8,128)(2,1)S(1)}, bf16[96,3072]{1,0:T(8,128)(2,1)S(1)}, u32[]{:S(2)}, u32[]{:S(2)}) collective-permute-start(bf16[96,3072]{1,0:T(8,128)(2,1)S(1)} %collective-permute-done.9.refs_12_), channel_id=1, source_target_pairs={{0,192},{1,193},{2,194},{3,195},{8,200},{9,201},{10,202},{11,203},... | collective-permute-start | bytes 1769480 | tf_op jit(solution)/shard_map/ppermute | solution.py:188
  56.7 5.0 %collective-permute-start.8 = (bf16[96,3072]{1,0:T(8,128)(2,1)S(1)}, bf16[96,3072]{1,0:T(8,128)(2,1)S(1)}, u32[]{:S(2)}, u32[]{:S(2)}) collective-permute-start(bf16[96,3072]{1,0:T(8,128)(2,1)S(1)} %collective-permute-done.7.refs_6_), channel_id=1, source_target_pairs={{0,8},{1,9},{2,10},{3,11},{8,0},{9,1},{10,2},{11,3},{4,12},{5,13},... | collective-permute-start | bytes 1769480 | tf_op jit(solution)/shard_map/ppermute | solution.py:188
  59.7 15.0 %collective-permute-start.20 = (bf16[96,3072]{1,0:T(8,128)(2,1)S(1)}, bf16[96,3072]{1,0:T(8,128)(2,1)S(1)}, u32[]{:S(2)}, u32[]{:S(2)}) collective-permute-start(bf16[96,3072]{1,0:T(8,128)(2,1)S(1)} %collective-permute-done.15.refs_16_), channel_id=1, source_target_pairs={{0,192},{1,193},{2,194},{3,195},{8,200},{9,201},{10,202},{11,203},... | collective-permute-start | bytes 1769480 | tf_op jit(solution)/shard_map/ppermute | solution.py:188
  59.7 15.7 %collective-permute-start.4 = (bf16[96,3072]{1,0:T(8,128)(2,1)S(1)}, bf16[96,3072]{1,0:T(8,128)(2,1)S(1)}, u32[]{:S(2)}, u32[]{:S(2)}) collective-permute-start(bf16[96,3072]{1,0:T(8,128)(2,1)S(1)} %collective-permute-done.1.refs_2_), channel_id=1, source_target_pairs={{0,8},{1,9},{2,10},{3,11},{8,0},{9,1},{10,2},{11,3},{4,12},{5,13},... | collective-permute-start | bytes 1769480 | tf_op jit(solution)/shard_map/ppermute | solution.py:188
  59.9 15.7 %collective-permute-start.6 = (bf16[96,3072]{1,0:T(8,128)(2,1)S(1)}, bf16[96,3072]{1,0:T(8,128)(2,1)S(1)}, u32[]{:S(2)}, u32[]{:S(2)}) collective-permute-start(bf16[96,3072]{1,0:T(8,128)(2,1)S(1)} %collective-permute-done.5.refs_4_), channel_id=1, source_target_pairs={{0,8},{1,9},{2,10},{3,11},{8,0},{9,1},{10,2},{11,3},{4,12},{5,13},... | collective-permute-start | bytes 1769480 | tf_op jit(solution)/shard_map/ppermute | solution.py:188
  61.0 16.2 %collective-permute-start.16 = (bf16[96,3072]{1,0:T(8,128)(2,1)S(1)}, bf16[96,3072]{1,0:T(8,128)(2,1)}, u32[]{:S(2)}, u32[]{:S(2)}) collective-permute-start(bf16[96,3072]{1,0:T(8,128)(2,1)S(1)} %collective-permute-done.15.refs_16_), channel_id=1, source_target_pairs={{0,64},{1,65},{2,66},{3,67},{8,72},{9,73},{10,74},{11,75},{4,68},{... | collective-permute-start | bytes 1769480 | tf_op jit(solution)/shard_map/ppermute | solution.py:188
  61.7 16.4 %collective-permute-start.3 = (bf16[96,3072]{1,0:T(8,128)(2,1)S(1)}, bf16[96,3072]{1,0:T(8,128)(2,1)S(1)}, u32[]{:S(2)}, u32[]{:S(2)}) collective-permute-start(bf16[96,3072]{1,0:T(8,128)(2,1)S(1)} %copy-done.1), channel_id=1, source_target_pairs={{0,8},{1,9},{2,10},{3,11},{8,0},{9,1},{10,2},{11,3},{4,12},{5,13},... | collective-permute-start | bytes 1769480 | tf_op jit(solution)/shard_map/ppermute | solution.py:188
  74.7 3.4 %collective-permute-start.12 = (bf16[96,3072]{1,0:T(8,128)(2,1)S(1)}, bf16[96,3072]{1,0:T(8,128)(2,1)S(1)}, u32[]{:S(2)}, u32[]{:S(2)}) collective-permute-start(bf16[96,3072]{1,0:T(8,128)(2,1)S(1)} %collective-permute-done.2.refs_10_), channel_id=1, source_target_pairs={{0,8},{1,9},{2,10},{3,11},{8,0},{9,1},{10,2},{11,3},{4,12},{5,13},... | collective-permute-start | bytes 1769480 | tf_op jit(solution)/shard_map/ppermute | solution.py:188
  75.4 5.3 %collective-permute-start.13 = (bf16[96,3072]{1,0:T(8,128)(2,1)S(1)}, bf16[96,3072]{1,0:T(8,128)(2,1)S(1)}, u32[]{:S(2)}, u32[]{:S(2)}) collective-permute-start(bf16[96,3072]{1,0:T(8,128)(2,1)S(1)} %collective-permute-done.9.refs_12_), channel_id=1, source_target_pairs={{0,8},{1,9},{2,10},{3,11},{8,0},{9,1},{10,2},{11,3},{4,12},{5,13},... | collective-permute-start | bytes 1769480 | tf_op jit(solution)/shard_map/ppermute | solution.py:188
  75.5 5.2 %collective-permute-start.11 = (bf16[96,3072]{1,0:T(8,128)(2,1)S(1)}, bf16[96,3072]{1,0:T(8,128)(2,1)S(1)}, u32[]{:S(2)}, u32[]{:S(2)}) collective-permute-start(bf16[96,3072]{1,0:T(8,128)(2,1)S(1)} %collective-permute-done.refs_8_), channel_id=1, source_target_pairs={{0,8},{1,9},{2,10},{3,11},{8,0},{9,1},{10,2},{11,3},{4,12},{5,13},... | collective-permute-start | bytes 1769480 | tf_op jit(solution)/shard_map/ppermute | solution.py:188
  77.2 4.4 %collective-permute-start.14 = (bf16[96,3072]{1,0:T(8,128)(2,1)S(1)}, bf16[96,3072]{1,0:T(8,128)(2,1)}, u32[]{:S(2)}, u32[]{:S(2)}) collective-permute-start(bf16[96,3072]{1,0:T(8,128)(2,1)S(1)} %collective-permute-done.10.refs_14_), channel_id=1, source_target_pairs={{0,8},{1,9},{2,10},{3,11},{8,0},{9,1},{10,2},{11,3},{4,12},{5,13},... | collective-permute-start | bytes 1769480 | tf_op jit(solution)/shard_map/ppermute | solution.py:188
  78.0 16.3 %collective-permute-start.17 = (bf16[96,3072]{1,0:T(8,128)(2,1)}, bf16[96,3072]{1,0:T(8,128)(2,1)S(1)}, u32[]{:S(2)}, u32[]{:S(2)}) collective-permute-start(bf16[96,3072]{1,0:T(8,128)(2,1)} %collective-permute-done.16.refs_18_), channel_id=1, source_target_pairs={{0,64},{1,65},{2,66},{3,67},{8,72},{9,73},{10,74},{11,75},{4,68},{... | collective-permute-start | bytes 1769480 | tf_op jit(solution)/shard_map/ppermute | solution.py:188
  78.1 16.3 %collective-permute-start.27 = (bf16[96,3072]{1,0:T(8,128)(2,1)}, bf16[96,3072]{1,0:T(8,128)(2,1)}, u32[]{:S(2)}, u32[]{:S(2)}) collective-permute-start(bf16[96,3072]{1,0:T(8,128)(2,1)} %collective-permute-done.23.refs_24_), channel_id=1, source_target_pairs={{0,192},{1,193},{2,194},{3,195},{8,200},{9,201},{10,202},{11,203},... | collective-permute-start | bytes 1769480 | tf_op jit(solution)/shard_map/ppermute | solution.py:188
  99.9 30.2 %all-to-all-start.1 = ((bf16[8,2,128,384]{3,2,1,0:T(8,128)(2,1)}), bf16[8,2,128,384]{3,2,1,0:T(8,128)(2,1)S(1)}, u32[]{:S(2)}, u32[]{:S(2)}) async-start(bf16[8,2,128,384]{3,2,1,0:T(8,128)(2,1)} %attend.3), calls=%async_computation.1 | async-start | bytes 3145728 | tf_op jit(solution)/shard_map/all_to_all | solution.py:240
  104.3 15.2 %collective-permute-start.24 = (bf16[96,3072]{1,0:T(8,128)(2,1)}, bf16[96,3072]{1,0:T(8,128)(2,1)}, u32[]{:S(2)}, u32[]{:S(2)}) collective-permute-start(bf16[96,3072]{1,0:T(8,128)(2,1)} %collective-permute-done.23.refs_24_), channel_id=1, source_target_pairs={{0,64},{1,65},{2,66},{3,67},{8,72},{9,73},{10,74},{11,75},{4,68},{... | collective-permute-start | bytes 1769480 | tf_op jit(solution)/shard_map/ppermute | solution.py:188
  104.3 17.8 %collective-permute-start.29 = (bf16[96,3072]{1,0:T(8,128)(2,1)}, bf16[96,3072]{1,0:T(8,128)(2,1)}, u32[]{:S(2)}, u32[]{:S(2)}) collective-permute-start(bf16[96,3072]{1,0:T(8,128)(2,1)} %collective-permute-done.27.refs_28_), channel_id=1, source_target_pairs={{0,192},{1,193},{2,194},{3,195},{8,200},{9,201},{10,202},{11,203},... | collective-permute-start | bytes 1769480 | tf_op jit(solution)/shard_map/ppermute | solution.py:188
  119.5 4.7 %collective-permute-start.28 = (bf16[96,3072]{1,0:T(8,128)(2,1)}, bf16[96,3072]{1,0:T(8,128)(2,1)S(1)}, u32[]{:S(2)}, u32[]{:S(2)}) collective-permute-start(bf16[96,3072]{1,0:T(8,128)(2,1)} %collective-permute-done.27.refs_28_), channel_id=1, source_target_pairs={{0,8},{1,9},{2,10},{3,11},{8,0},{9,1},{10,2},{11,3},{4,12},{5,13},... | collective-permute-start | bytes 1769480 | tf_op jit(solution)/shard_map/ppermute | solution.py:188
  121.6 3.2 %collective-permute-start.21 = (bf16[96,3072]{1,0:T(8,128)(2,1)S(1)}, bf16[96,3072]{1,0:T(8,128)(2,1)S(1)}, u32[]{:S(2)}, u32[]{:S(2)}) collective-permute-start(bf16[96,3072]{1,0:T(8,128)(2,1)S(1)} %copy-done.13), channel_id=1, source_target_pairs={{0,8},{1,9},{2,10},{3,11},{8,0},{9,1},{10,2},{11,3},{4,12},{5,13},... | collective-permute-start | bytes 1769480 | tf_op jit(solution)/shard_map/ppermute | solution.py:188
  121.6 5.2 %collective-permute-start.19 = (bf16[96,3072]{1,0:T(8,128)(2,1)}, bf16[96,3072]{1,0:T(8,128)(2,1)S(1)}, u32[]{:S(2)}, u32[]{:S(2)}) collective-permute-start(bf16[96,3072]{1,0:T(8,128)(2,1)} %collective-permute-done.16.refs_18_), channel_id=1, source_target_pairs={{0,8},{1,9},{2,10},{3,11},{8,0},{9,1},{10,2},{11,3},{4,12},{5,13},... | collective-permute-start | bytes 1769480 | tf_op jit(solution)/shard_map/ppermute | solution.py:188
  122.1 6.5 %collective-permute-start.18 = (bf16[96,3072]{1,0:T(8,128)(2,1)S(1)}, bf16[96,3072]{1,0:T(8,128)(2,1)}, u32[]{:S(2)}, u32[]{:S(2)}) collective-permute-start(bf16[96,3072]{1,0:T(8,128)(2,1)S(1)} %copy-done.9), channel_id=1, source_target_pairs={{0,8},{1,9},{2,10},{3,11},{8,0},{9,1},{10,2},{11,3},{4,12},{5,13},... | collective-permute-start | bytes 1769480 | tf_op jit(solution)/shard_map/ppermute | solution.py:188
  122.1 6.5 %collective-permute-start.25 = (bf16[96,3072]{1,0:T(8,128)(2,1)}, bf16[96,3072]{1,0:T(8,128)(2,1)}, u32[]{:S(2)}, u32[]{:S(2)}) collective-permute-start(bf16[96,3072]{1,0:T(8,128)(2,1)} %collective-permute-done.23.refs_24_), channel_id=1, source_target_pairs={{0,8},{1,9},{2,10},{3,11},{8,0},{9,1},{10,2},{11,3},{4,12},{5,13},... | collective-permute-start | bytes 1769480 | tf_op jit(solution)/shard_map/ppermute | solution.py:188
  124.2 4.4 %collective-permute-start.22 = (bf16[96,3072]{1,0:T(8,128)(2,1)S(1)}, bf16[96,3072]{1,0:T(8,128)(2,1)}, u32[]{:S(2)}, u32[]{:S(2)}) collective-permute-start(bf16[96,3072]{1,0:T(8,128)(2,1)S(1)} %collective-permute-done.17.refs_22_), channel_id=1, source_target_pairs={{0,8},{1,9},{2,10},{3,11},{8,0},{9,1},{10,2},{11,3},{4,12},{5,13},... | collective-permute-start | bytes 1769480 | tf_op jit(solution)/shard_map/ppermute | solution.py:188
  125.0 3.6 %collective-permute-start.26 = (bf16[96,3072]{1,0:T(8,128)(2,1)}, bf16[96,3072]{1,0:T(8,128)(2,1)S(1)}, u32[]{:S(2)}, u32[]{:S(2)}) collective-permute-start(bf16[96,3072]{1,0:T(8,128)(2,1)} %collective-permute-done.24.refs_26_), channel_id=1, source_target_pairs={{0,8},{1,9},{2,10},{3,11},{8,0},{9,1},{10,2},{11,3},{4,12},{5,13},... | collective-permute-start | bytes 1769480 | tf_op jit(solution)/shard_map/ppermute | solution.py:188
  (26 other events, 430.2 us)

commit v3 on v2

--- a/solution.py
+++ b/solution.py
@@ -62,8 +62,7 @@
     return lax.dot_general(a, b, (((1,), (1,)), ((), ())), preferred_element_type=jnp.float32)
 
 
-def attend_kernel(in_ref, *refs):
-    out_ref = refs[-1]
+def attend_kernel(in_ref, out_ref):
     pieces, _, rows, _ = in_ref.shape
     factor = 1.0 / math.sqrt(HEAD_DIM)
     tokens = pieces * rows
@@ -96,26 +95,24 @@
         out_ref[which, 1] = heads_tan.astype(jnp.bfloat16).reshape(step, rows, HEAD_DIM)
 
 
-def attend(received, first, heads, others=None):
+def attend(received):
     pieces, count, rows, width = received.shape
+    heads = width // HEAD_DIM
     tokens = rows * pieces
-    kept = [] if others is None else [others]
     return pl.pallas_call(
         attend_kernel,
         grid=(heads,),
-        in_specs=[pl.BlockSpec((pieces, count, rows, HEAD_DIM), lambda h: (0, 0, 0, h + first))]
-        + [pl.BlockSpec(memory_space=pl.ANY)] * len(kept),
-        out_specs=pl.BlockSpec((pieces, 2, rows, HEAD_DIM), lambda h: (0, 0, 0, h + first)),
+        in_specs=[pl.BlockSpec((pieces, count, rows, HEAD_DIM), lambda h: (0, 0, 0, h))],
+        out_specs=pl.BlockSpec((pieces, 2, rows, HEAD_DIM), lambda h: (0, 0, 0, h)),
         out_shape=jax.ShapeDtypeStruct((pieces, 2, rows, width), jnp.bfloat16),
-        input_output_aliases={1: 0} if kept else {},
         compiler_params=pltpu.CompilerParams(vmem_limit_bytes=32 * MIB),
         cost_estimate=pl.CostEstimate(
             flops=heads * 12 * tokens * tokens * HEAD_DIM,
-            bytes_accessed=heads * (count + 2) * tokens * HEAD_DIM * 2,
+            bytes_accessed=(count + 2) * tokens * width * 2,
             transcendentals=heads * tokens * tokens,
         ),
         name="attend",
-    )(received, *kept)
+    )(received)
 
 
 BLOCK = 512
@@ -223,20 +220,20 @@
     before[3] = send(z[3], NEXT_X, before[2])
     far[3] = send(later[3], LAST_X, later[2])
 
-    freed = (before[1], far[1], far[2], before[3])
     weights, swapped, places = [], {}, []
     for at, pairs in enumerate((0, -toward, toward, 2)):
         for block, steps in ((z[at], 0), (before[at], -1), (later[at], 1), (far[at], 2)):
             place = (x + steps) % 4 * 8 + (z_pair + pairs) % 4 * 2
-            swapped[at, steps] = send(block, OTHER_CORE, freed[at])
+            after = [before[1], far[1], before[2], far[2]][at]
+            swapped[at, steps] = send(block, OTHER_CORE, after)
             weights += [block, swapped[at, steps]]
             places += [place + core, place + 1 - core]
 
     early = [swapped[at, steps] for at in (0, 1) for steps in (0, -1, 1, 2)]
+    during = [swapped[2, steps] for steps in (0, -1, 1)]
     received = lax.optimization_barrier((received, z[3], before[2], later[2], *early))[0]
-    results = attend(received, 0, 2)
-    received = lax.optimization_barrier((received, far[2], later[3]))[0]
-    results = attend(received, 2, 1, results)
+    results = attend(received)
+    results = lax.optimization_barrier((results, far[2], later[3], *during))[0]
     results = lax.all_to_all(results, "seq", 0, 0, tiled=True)
 
     gated, tangent = project(

time: 142 us -> 136 us (0.958)
  Pallas kernels: 29.5 us -> 27.1 us
  waiting for transfers between devices: 65.1 us -> 63.2 us
    pallas_call x2 -> x1, Pallas kernels: 13.9 us -> 11.5 us  [attend(): pl.pallas_call(attend_kernel, grid=(heads,), in_specs=[pl.BlockSpec((piec...]
    all_to_all x1, waiting for transfers between devices: 2.54 us -> 0.78 us  [on_device(): received = lax.all_to_all(sent, 'seq', 0, 0, tiled=True)]
    unnamed x50 -> x42, local copies, waits for them, and re-layouts: 3.56 us -> 2.22 us
  transfers between devices with their start and end apart: 33 -> 33, of which waited for: 14 -> 18; matrix products, arithmetic and copies ran while one was open for 0% -> 0% of each run, Pallas kernels for 10% -> 12%
where the time goes in v3:
time: 136 us
  waiting for transfers between devices  63.2 us (46%)
  starting transfers between devices  41.8 us (31%)
  Pallas kernels  27.1 us (20%)
  local copies, waits for them, and re-layouts  2.82 us (2%)
    ppermute x31, waiting for transfers between devices, send(): return lax.ppermute(value, AXES, moves_of)  62.4 us
    ppermute x31, starting transfers between devices, send(): return lax.ppermute(value, AXES, moves_of)  32.4 us
    pallas_call x1, Pallas kernels, attend(): pl.pallas_call(attend_kernel, grid=(heads,), in_specs=[pl.BlockSpec((piec...  11.5 us
    pallas_call x1, Pallas kernels, project(): pl.pallas_call(project_kernel, in_specs=[pl.BlockSpec(memory_space=pltpu....  10.4 us
    pallas_call x1, Pallas kernels, pack(): pl.pallas_call(pack_kernel, grid=(rows // block,), in_specs=[pl.BlockSpec...  5.13 us
    all_to_all x1, starting transfers between devices, on_device(): results = lax.all_to_all(results, 'seq', 0, 0, tiled=True)  4.81 us
    all_to_all x1, starting transfers between devices, on_device(): received = lax.all_to_all(sent, 'seq', 0, 0, tiled=True)  4.6 us
  transfers between devices with their start and end apart: 33, of which 18 were waited for; matrix products, arithmetic and copies ran while one was open for 0% of the time, Pallas kernels for 12%

profile of v3, /device:TPU:1, one launch (start us, length us, event | category | flops | bytes accessed | tf_op | source)
XLA Modules:
  0.0 136.0 jit_solution(16795832440151282007)
XLA Ops:
  0.6 6.9 %collective-permute-start = (bf16[96,3072]{1,0:T(8,128)(2,1)}, bf16[96,3072]{1,0:T(8,128)(2,1)S(1)}, u32[]{:S(2)}, u32[]{:S(2)}) collective-permute-start(bf16[96,3072]{1,0:T(8,128)(2,1)} %refs_0_.3), channel_id=1, source_target_pairs={{0,48},{1,49},{2,50},{3,51},{8,56},{9,57},{10,58},{11,59},{4,20},{... | collective-permute-start | bytes 1769480 | tf_op jit(solution)/shard_map/ppermute | solution.py:185
  7.6 2.5 %collective-permute-start.5 = (bf16[96,3072]{1,0:T(8,128)(2,1)}, bf16[96,3072]{1,0:T(8,128)(2,1)S(1)}, u32[]{:S(2)}, u32[]{:S(2)}) collective-permute-start(bf16[96,3072]{1,0:T(8,128)(2,1)} %refs_0_.3), channel_id=1, source_target_pairs={{0,192},{1,193},{2,194},{3,195},{8,200},{9,201},{10,202},{11,203},... | collective-permute-start | bytes 1769480 | tf_op jit(solution)/shard_map/ppermute | solution.py:185
  10.0 5.1 %pack.1 = bf16[8,6,128,384]{3,2,1,0:T(8,128)(2,1)} custom-call(bf16[1,128,3072]{2,1,0:T(8,128)(2,1)} %refs_0_.2, bf16[1,128,3072]{2,1,0:T(8,128)(2,1)} %refs_1_.1, bf16[1,128,3072]{2,1,0:T(8,128)(2,1)} %refs_2_.1, bf16[1,128,3072]{2,1,0:T(8,128)(2,1)} %refs_3_.1, bf16[1,128,3072]{2,1,0:T(8,128)(2,1)} %refs_4_.1, bf16[1,128,3072]{2,1,0:T(8,128)(2,1)} %refs_5_.1), custom_call_target="tpu_custom_call" | custom-call | bytes 9437184 | tf_op jit(solution)/shard_map/pack/pallas_call | solution.py:48
  15.2 4.7 %collective-permute-done.refs_8_ = bf16[96,3072]{1,0:T(8,128)(2,1)S(1)} collective-permute-done((bf16[96,3072]{1,0:T(8,128)(2,1)}, bf16[96,3072]{1,0:T(8,128)(2,1)S(1)}, u32[]{:S(2)}, u32[]{:S(2)}) %collective-permute-start) | collective-permute-done | bytes 589856 | tf_op jit(solution)/shard_map/ppermute | solution.py:185
  19.9 2.2 %collective-permute-done.5.refs_4_ = bf16[96,3072]{1,0:T(8,128)(2,1)S(1)} collective-permute-done((bf16[96,3072]{1,0:T(8,128)(2,1)}, bf16[96,3072]{1,0:T(8,128)(2,1)S(1)}, u32[]{:S(2)}, u32[]{:S(2)}) %collective-permute-start.5) | collective-permute-done | bytes 589856 | tf_op jit(solution)/shard_map/ppermute | solution.py:185
  22.0 3.0 %collective-permute-done.1.refs_2_ = bf16[96,3072]{1,0:T(8,128)(2,1)S(1)} collective-permute-done((bf16[96,3072]{1,0:T(8,128)(2,1)}, bf16[96,3072]{1,0:T(8,128)(2,1)S(1)}, u32[]{:S(2)}, u32[]{:S(2)}) %collective-permute-start.1) | collective-permute-done | bytes 589856 | tf_op jit(solution)/shard_map/ppermute | solution.py:185
  25.0 4.6 %all-to-all-start = ((bf16[8,6,128,384]{3,2,1,0:T(8,128)(2,1)}), bf16[8,6,128,384]{3,2,1,0:T(8,128)(2,1)}, u32[]{:S(2)}, u32[]{:S(2)}) async-start(bf16[8,6,128,384]{3,2,1,0:T(8,128)(2,1)} %pack.1), calls=%async_computation | async-start | bytes 9437184 | tf_op jit(solution)/shard_map/all_to_all | solution.py:209
  30.0 1.2 collective-permute-start.2
  31.2 1.3 collective-permute-start.15
  32.5 1.4 %collective-permute-start.23 = (bf16[96,3072]{1,0:T(8,128)(2,1)S(1)}, bf16[96,3072]{1,0:T(8,128)(2,1)}, u32[]{:S(2)}, u32[]{:S(2)}) collective-permute-start(bf16[96,3072]{1,0:T(8,128)(2,1)S(1)} %collective-permute-done.refs_8_), channel_id=1, source_target_pairs={{0,52},{1,53},{2,54},{3,55},{8,60},{9,61},{10,62},{11,63},{4,16},{... | collective-permute-start | bytes 1769480 | tf_op jit(solution)/shard_map/ppermute | solution.py:185
  33.9 8.6 %collective-permute-done.9.refs_12_ = bf16[96,3072]{1,0:T(8,128)(2,1)S(1)} collective-permute-done((bf16[96,3072]{1,0:T(8,128)(2,1)S(1)}, bf16[96,3072]{1,0:T(8,128)(2,1)S(1)}, u32[]{:S(2)}, u32[]{:S(2)}) %collective-permute-start.9) | collective-permute-done | bytes 589856 | tf_op jit(solution)/shard_map/ppermute | solution.py:185
  42.5 1.8 %collective-permute-start.10 = (bf16[96,3072]{1,0:T(8,128)(2,1)S(1)}, bf16[96,3072]{1,0:T(8,128)(2,1)S(1)}, u32[]{:S(2)}, u32[]{:S(2)}) collective-permute-start(bf16[96,3072]{1,0:T(8,128)(2,1)S(1)} %collective-permute-done.9.refs_12_), channel_id=1, source_target_pairs={{0,192},{1,193},{2,194},{3,195},{8,200},{9,201},{10,202},{11,203},... | collective-permute-start | bytes 1769480 | tf_op jit(solution)/shard_map/ppermute | solution.py:185
  44.3 12.4 %collective-permute-done.7.refs_6_ = bf16[96,3072]{1,0:T(8,128)(2,1)S(1)} collective-permute-done((bf16[96,3072]{1,0:T(8,128)(2,1)S(1)}, bf16[96,3072]{1,0:T(8,128)(2,1)S(1)}, u32[]{:S(2)}, u32[]{:S(2)}) %collective-permute-start.7) | collective-permute-done | bytes 589856 | tf_op jit(solution)/shard_map/ppermute | solution.py:185
  56.7 3.0 %collective-permute-start.8 = (bf16[96,3072]{1,0:T(8,128)(2,1)S(1)}, bf16[96,3072]{1,0:T(8,128)(2,1)S(1)}, u32[]{:S(2)}, u32[]{:S(2)}) collective-permute-start(bf16[96,3072]{1,0:T(8,128)(2,1)S(1)} %collective-permute-done.7.refs_6_), channel_id=1, source_target_pairs={{0,8},{1,9},{2,10},{3,11},{8,0},{9,1},{10,2},{11,3},{4,12},{5,13},... | collective-permute-start | bytes 1769480 | tf_op jit(solution)/shard_map/ppermute | solution.py:185
  59.6 2.7 %collective-permute-start.19 = (bf16[96,3072]{1,0:T(8,128)(2,1)}, bf16[96,3072]{1,0:T(8,128)(2,1)}, u32[]{:S(2)}, u32[]{:S(2)}) collective-permute-start(bf16[96,3072]{1,0:T(8,128)(2,1)} %collective-permute-done.15.refs_16_), channel_id=1, source_target_pairs={{0,192},{1,193},{2,194},{3,195},{8,200},{9,201},{10,202},{11,203},... | collective-permute-start | bytes 1769480 | tf_op jit(solution)/shard_map/ppermute | solution.py:185
  63.6 12.5 %collective-permute-done.16.refs_18_ = bf16[96,3072]{1,0:T(8,128)(2,1)} collective-permute-done((bf16[96,3072]{1,0:T(8,128)(2,1)}, bf16[96,3072]{1,0:T(8,128)(2,1)}, u32[]{:S(2)}, u32[]{:S(2)}) %collective-permute-start.16) | collective-permute-done | bytes 589856 | tf_op jit(solution)/shard_map/ppermute | solution.py:185
  76.1 0.9 collective-permute-start.12
  78.6 0.8 collective-permute-done.13.refs_13_
  79.8 1.3 collective-permute-done.11.refs_9_
  81.1 1.0 collective-permute-start.27
  83.3 0.8 all-to-all-done.in_ref
  84.1 11.5 %attend.1 = bf16[8,2,128,384]{3,2,1,0:T(8,128)(2,1)} custom-call(bf16[8,6,128,384]{3,2,1,0:T(8,128)(2,1)} %all-to-all-done.in_ref), custom_call_target="tpu_custom_call" | custom-call | flops 4831838208 | bytes 6291456 | tf_op jit(solution)/shard_map/attend/pallas_call | solution.py:102
  95.8 1.0 copy-done.19
  96.8 4.8 %all-to-all-start.1 = ((bf16[8,2,128,384]{3,2,1,0:T(8,128)(2,1)}), bf16[8,2,128,384]{3,2,1,0:T(8,128)(2,1)S(1)}, u32[]{:S(2)}, u32[]{:S(2)}) async-start(bf16[8,2,128,384]{3,2,1,0:T(8,128)(2,1)} %attend.1), calls=%async_computation.1 | async-start | bytes 3145728 | tf_op jit(solution)/shard_map/all_to_all | solution.py:237
  101.8 2.5 %collective-permute-start.29 = (bf16[96,3072]{1,0:T(8,128)(2,1)}, bf16[96,3072]{1,0:T(8,128)(2,1)}, u32[]{:S(2)}, u32[]{:S(2)}) collective-permute-start(bf16[96,3072]{1,0:T(8,128)(2,1)} %copy-done.19), channel_id=1, source_target_pairs={{0,192},{1,193},{2,194},{3,195},{8,200},{9,201},{10,202},{11,203},... | collective-permute-start | bytes 1769480 | tf_op jit(solution)/shard_map/ppermute | solution.py:185
  104.3 12.1 %collective-permute-done.25.refs_26_ = bf16[96,3072]{1,0:T(8,128)(2,1)S(1)} collective-permute-done((bf16[96,3072]{1,0:T(8,128)(2,1)}, bf16[96,3072]{1,0:T(8,128)(2,1)S(1)}, u32[]{:S(2)}, u32[]{:S(2)}) %collective-permute-start.25) | collective-permute-done | bytes 589856 | tf_op jit(solution)/shard_map/ppermute | solution.py:185
  116.4 2.4 %collective-permute-start.26 = (bf16[96,3072]{1,0:T(8,128)(2,1)S(1)}, bf16[96,3072]{1,0:T(8,128)(2,1)}, u32[]{:S(2)}, u32[]{:S(2)}) collective-permute-start(bf16[96,3072]{1,0:T(8,128)(2,1)S(1)} %collective-permute-done.25.refs_26_), channel_id=1, source_target_pairs={{0,8},{1,9},{2,10},{3,11},{8,0},{9,1},{10,2},{11,3},{4,12},{5,13},... | collective-permute-start | bytes 1769480 | tf_op jit(solution)/shard_map/ppermute | solution.py:185
  120.4 0.9 collective-permute-done.26.refs_27_
  121.4 1.0 collective-permute-done.28.refs_29_
  123.3 0.8 collective-permute-done.30.refs_31_
  124.2 1.2 copy-done
  125.3 10.4 %project.1 = (bf16[1,128,3072]{2,1,0:T(8,128)(2,1)}, bf16[1,128,3072]{2,1,0:T(8,128)(2,1)}) custom-call(s32[32]{0:T(128)} %stack.131.place_ref, bf16[96,3072]{1,0:T(8,128)(2,1)} %refs_0_.3, bf16[96,3072]{1,0:T(8,128)(2,1)} %copy-done.12, bf16[96,3072]{1,0:T(8,128)(2,1)} %copy-done.4, bf16[96,3072]{1,0:T(8,128)(2,1)} %copy-done.10, ...), custom_call_target="tpu_custom_call" | custom-call | flops 4831838208 | bytes 18874368 | tf_op jit(solution)/shard_map/project/pallas_call | solution.py:160
  (80 shorter events, 7.8 us)
Async XLA Ops:
  0.6 19.2 %collective-permute-start = (bf16[96,3072]{1,0:T(8,128)(2,1)}, bf16[96,3072]{1,0:T(8,128)(2,1)S(1)}, u32[]{:S(2)}, u32[]{:S(2)}) collective-permute-start(bf16[96,3072]{1,0:T(8,128)(2,1)} %refs_0_.3), channel_id=1, source_target_pairs={{0,48},{1,49},{2,50},{3,51},{8,56},{9,57},{10,58},{11,59},{4,20},{... | collective-permute-start | bytes 1769480 | tf_op jit(solution)/shard_map/ppermute | solution.py:185
  7.6 14.5 %collective-permute-start.5 = (bf16[96,3072]{1,0:T(8,128)(2,1)}, bf16[96,3072]{1,0:T(8,128)(2,1)S(1)}, u32[]{:S(2)}, u32[]{:S(2)}) collective-permute-start(bf16[96,3072]{1,0:T(8,128)(2,1)} %refs_0_.3), channel_id=1, source_target_pairs={{0,192},{1,193},{2,194},{3,195},{8,200},{9,201},{10,202},{11,203},... | collective-permute-start | bytes 1769480 | tf_op jit(solution)/shard_map/ppermute | solution.py:185
  10.0 15.0 %collective-permute-start.1 = (bf16[96,3072]{1,0:T(8,128)(2,1)}, bf16[96,3072]{1,0:T(8,128)(2,1)S(1)}, u32[]{:S(2)}, u32[]{:S(2)}) collective-permute-start(bf16[96,3072]{1,0:T(8,128)(2,1)} %refs_0_.3), channel_id=1, source_target_pairs={{0,64},{1,65},{2,66},{3,67},{8,72},{9,73},{10,74},{11,75},{4,68},{... | collective-permute-start | bytes 1769480 | tf_op jit(solution)/shard_map/ppermute | solution.py:185
  25.0 59.0 %all-to-all-start = ((bf16[8,6,128,384]{3,2,1,0:T(8,128)(2,1)}), bf16[8,6,128,384]{3,2,1,0:T(8,128)(2,1)}, u32[]{:S(2)}, u32[]{:S(2)}) async-start(bf16[8,6,128,384]{3,2,1,0:T(8,128)(2,1)} %pack.1), calls=%async_computation | async-start | bytes 9437184 | tf_op jit(solution)/shard_map/all_to_all | solution.py:209
  29.7 12.8 %collective-permute-start.9 = (bf16[96,3072]{1,0:T(8,128)(2,1)S(1)}, bf16[96,3072]{1,0:T(8,128)(2,1)S(1)}, u32[]{:S(2)}, u32[]{:S(2)}) collective-permute-start(bf16[96,3072]{1,0:T(8,128)(2,1)S(1)} %collective-permute-done.refs_8_), channel_id=1, source_target_pairs={{0,192},{1,193},{2,194},{3,195},{8,200},{9,201},{10,202},{11,203},... | collective-permute-start | bytes 1769480 | tf_op jit(solution)/shard_map/ppermute | solution.py:185
  30.0 14.3 %collective-permute-start.2 = (bf16[96,3072]{1,0:T(8,128)(2,1)S(1)}, bf16[96,3072]{1,0:T(8,128)(2,1)S(1)}, u32[]{:S(2)}, u32[]{:S(2)}) collective-permute-start(bf16[96,3072]{1,0:T(8,128)(2,1)S(1)} %collective-permute-done.refs_8_), channel_id=1, source_target_pairs={{0,64},{1,65},{2,66},{3,67},{8,72},{9,73},{10,74},{11,75},{4,68},{... | collective-permute-start | bytes 1769480 | tf_op jit(solution)/shard_map/ppermute | solution.py:185
  31.2 25.5 %collective-permute-start.7 = (bf16[96,3072]{1,0:T(8,128)(2,1)S(1)}, bf16[96,3072]{1,0:T(8,128)(2,1)S(1)}, u32[]{:S(2)}, u32[]{:S(2)}) collective-permute-start(bf16[96,3072]{1,0:T(8,128)(2,1)S(1)} %collective-permute-done.1.refs_2_), channel_id=1, source_target_pairs={{0,64},{1,65},{2,66},{3,67},{8,72},{9,73},{10,74},{11,75},{4,68},{... | collective-permute-start | bytes 1769480 | tf_op jit(solution)/shard_map/ppermute | solution.py:185
  31.2 28.4 %collective-permute-start.15 = (bf16[96,3072]{1,0:T(8,128)(2,1)S(1)}, bf16[96,3072]{1,0:T(8,128)(2,1)}, u32[]{:S(2)}, u32[]{:S(2)}) collective-permute-start(bf16[96,3072]{1,0:T(8,128)(2,1)S(1)} %copy-done.1), channel_id=1, source_target_pairs={{0,52},{1,53},{2,54},{3,55},{8,60},{9,61},{10,62},{11,63},{4,16},{... | collective-permute-start | bytes 1769480 | tf_op jit(solution)/shard_map/ppermute | solution.py:185
  32.5 29.8 %collective-permute-start.23 = (bf16[96,3072]{1,0:T(8,128)(2,1)S(1)}, bf16[96,3072]{1,0:T(8,128)(2,1)}, u32[]{:S(2)}, u32[]{:S(2)}) collective-permute-start(bf16[96,3072]{1,0:T(8,128)(2,1)S(1)} %collective-permute-done.refs_8_), channel_id=1, source_target_pairs={{0,52},{1,53},{2,54},{3,55},{8,60},{9,61},{10,62},{11,63},{4,16},{... | collective-permute-start | bytes 1769480 | tf_op jit(solution)/shard_map/ppermute | solution.py:185
  42.5 20.5 %collective-permute-start.10 = (bf16[96,3072]{1,0:T(8,128)(2,1)S(1)}, bf16[96,3072]{1,0:T(8,128)(2,1)S(1)}, u32[]{:S(2)}, u32[]{:S(2)}) collective-permute-start(bf16[96,3072]{1,0:T(8,128)(2,1)S(1)} %collective-permute-done.9.refs_12_), channel_id=1, source_target_pairs={{0,192},{1,193},{2,194},{3,195},{8,200},{9,201},{10,202},{11,203},... | collective-permute-start | bytes 1769480 | tf_op jit(solution)/shard_map/ppermute | solution.py:185
  56.7 6.4 %collective-permute-start.8 = (bf16[96,3072]{1,0:T(8,128)(2,1)S(1)}, bf16[96,3072]{1,0:T(8,128)(2,1)S(1)}, u32[]{:S(2)}, u32[]{:S(2)}) collective-permute-start(bf16[96,3072]{1,0:T(8,128)(2,1)S(1)} %collective-permute-done.7.refs_6_), channel_id=1, source_target_pairs={{0,8},{1,9},{2,10},{3,11},{8,0},{9,1},{10,2},{11,3},{4,12},{5,13},... | collective-permute-start | bytes 1769480 | tf_op jit(solution)/shard_map/ppermute | solution.py:185
  59.6 16.4 %collective-permute-start.16 = (bf16[96,3072]{1,0:T(8,128)(2,1)}, bf16[96,3072]{1,0:T(8,128)(2,1)}, u32[]{:S(2)}, u32[]{:S(2)}) collective-permute-start(bf16[96,3072]{1,0:T(8,128)(2,1)} %collective-permute-done.15.refs_16_), channel_id=1, source_target_pairs={{0,64},{1,65},{2,66},{3,67},{8,72},{9,73},{10,74},{11,75},{4,68},{... | collective-permute-start | bytes 1769480 | tf_op jit(solution)/shard_map/ppermute | solution.py:185
  59.6 17.3 %collective-permute-start.19 = (bf16[96,3072]{1,0:T(8,128)(2,1)}, bf16[96,3072]{1,0:T(8,128)(2,1)}, u32[]{:S(2)}, u32[]{:S(2)}) collective-permute-start(bf16[96,3072]{1,0:T(8,128)(2,1)} %collective-permute-done.15.refs_16_), channel_id=1, source_target_pairs={{0,192},{1,193},{2,194},{3,195},{8,200},{9,201},{10,202},{11,203},... | collective-permute-start | bytes 1769480 | tf_op jit(solution)/shard_map/ppermute | solution.py:185
  62.3 14.6 %collective-permute-start.4 = (bf16[96,3072]{1,0:T(8,128)(2,1)S(1)}, bf16[96,3072]{1,0:T(8,128)(2,1)S(1)}, u32[]{:S(2)}, u32[]{:S(2)}) collective-permute-start(bf16[96,3072]{1,0:T(8,128)(2,1)S(1)} %collective-permute-done.1.refs_2_), channel_id=1, source_target_pairs={{0,8},{1,9},{2,10},{3,11},{8,0},{9,1},{10,2},{11,3},{4,12},{5,13},... | collective-permute-start | bytes 1769480 | tf_op jit(solution)/shard_map/ppermute | solution.py:185
  63.0 14.7 %collective-permute-start.6 = (bf16[96,3072]{1,0:T(8,128)(2,1)S(1)}, bf16[96,3072]{1,0:T(8,128)(2,1)S(1)}, u32[]{:S(2)}, u32[]{:S(2)}) collective-permute-start(bf16[96,3072]{1,0:T(8,128)(2,1)S(1)} %collective-permute-done.5.refs_4_), channel_id=1, source_target_pairs={{0,8},{1,9},{2,10},{3,11},{8,0},{9,1},{10,2},{11,3},{4,12},{5,13},... | collective-permute-start | bytes 1769480 | tf_op jit(solution)/shard_map/ppermute | solution.py:185
  63.1 14.7 %collective-permute-start.3 = (bf16[96,3072]{1,0:T(8,128)(2,1)S(1)}, bf16[96,3072]{1,0:T(8,128)(2,1)S(1)}, u32[]{:S(2)}, u32[]{:S(2)}) collective-permute-start(bf16[96,3072]{1,0:T(8,128)(2,1)S(1)} %copy-done.1), channel_id=1, source_target_pairs={{0,8},{1,9},{2,10},{3,11},{8,0},{9,1},{10,2},{11,3},{4,12},{5,13},... | collective-permute-start | bytes 1769480 | tf_op jit(solution)/shard_map/ppermute | solution.py:185
  76.1 2.5 %collective-permute-start.12 = (bf16[96,3072]{1,0:T(8,128)(2,1)S(1)}, bf16[96,3072]{1,0:T(8,128)(2,1)S(1)}, u32[]{:S(2)}, u32[]{:S(2)}) collective-permute-start(bf16[96,3072]{1,0:T(8,128)(2,1)S(1)} %collective-permute-done.2.refs_10_), channel_id=1, source_target_pairs={{0,8},{1,9},{2,10},{3,11},{8,0},{9,1},{10,2},{11,3},{4,12},{5,13},... | collective-permute-start | bytes 1769480 | tf_op jit(solution)/shard_map/ppermute | solution.py:185
  77.0 4.1 %collective-permute-start.11 = (bf16[96,3072]{1,0:T(8,128)(2,1)S(1)}, bf16[96,3072]{1,0:T(8,128)(2,1)S(1)}, u32[]{:S(2)}, u32[]{:S(2)}) collective-permute-start(bf16[96,3072]{1,0:T(8,128)(2,1)S(1)} %collective-permute-done.refs_8_), channel_id=1, source_target_pairs={{0,8},{1,9},{2,10},{3,11},{8,0},{9,1},{10,2},{11,3},{4,12},{5,13},... | collective-permute-start | bytes 1769480 | tf_op jit(solution)/shard_map/ppermute | solution.py:185
  77.7 5.1 %collective-permute-start.14 = (bf16[96,3072]{1,0:T(8,128)(2,1)S(1)}, bf16[96,3072]{1,0:T(8,128)(2,1)S(1)}, u32[]{:S(2)}, u32[]{:S(2)}) collective-permute-start(bf16[96,3072]{1,0:T(8,128)(2,1)S(1)} %collective-permute-done.10.refs_14_), channel_id=1, source_target_pairs={{0,8},{1,9},{2,10},{3,11},{8,0},{9,1},{10,2},{11,3},{4,12},{5,13},... | collective-permute-start | bytes 1769480 | tf_op jit(solution)/shard_map/ppermute | solution.py:185
  77.8 17.8 %collective-permute-start.20 = (bf16[96,3072]{1,0:T(8,128)(2,1)}, bf16[96,3072]{1,0:T(8,128)(2,1)S(1)}, u32[]{:S(2)}, u32[]{:S(2)}) collective-permute-start(bf16[96,3072]{1,0:T(8,128)(2,1)} %collective-permute-done.19.refs_20_), channel_id=1, source_target_pairs={{0,8},{1,9},{2,10},{3,11},{8,0},{9,1},{10,2},{11,3},{4,12},{5,13},... | collective-permute-start | bytes 1769480 | tf_op jit(solution)/shard_map/ppermute | solution.py:185
  78.6 17.1 %collective-permute-start.21 = (bf16[96,3072]{1,0:T(8,128)(2,1)}, bf16[96,3072]{1,0:T(8,128)(2,1)S(1)}, u32[]{:S(2)}, u32[]{:S(2)}) collective-permute-start(bf16[96,3072]{1,0:T(8,128)(2,1)} %collective-permute-done.16.refs_18_), channel_id=1, source_target_pairs={{0,64},{1,65},{2,66},{3,67},{8,72},{9,73},{10,74},{11,75},{4,68},{... | collective-permute-start | bytes 1769480 | tf_op jit(solution)/shard_map/ppermute | solution.py:185
  79.4 16.3 %collective-permute-start.17 = (bf16[96,3072]{1,0:T(8,128)(2,1)}, bf16[96,3072]{1,0:T(8,128)(2,1)}, u32[]{:S(2)}, u32[]{:S(2)}) collective-permute-start(bf16[96,3072]{1,0:T(8,128)(2,1)} %collective-permute-done.15.refs_16_), channel_id=1, source_target_pairs={{0,8},{1,9},{2,10},{3,11},{8,0},{9,1},{10,2},{11,3},{4,12},{5,13},... | collective-permute-start | bytes 1769480 | tf_op jit(solution)/shard_map/ppermute | solution.py:185
  81.1 14.8 %collective-permute-start.27 = (bf16[96,3072]{1,0:T(8,128)(2,1)}, bf16[96,3072]{1,0:T(8,128)(2,1)S(1)}, u32[]{:S(2)}, u32[]{:S(2)}) collective-permute-start(bf16[96,3072]{1,0:T(8,128)(2,1)} %collective-permute-done.23.refs_24_), channel_id=1, source_target_pairs={{0,192},{1,193},{2,194},{3,195},{8,200},{9,201},{10,202},{11,203},... | collective-permute-start | bytes 1769480 | tf_op jit(solution)/shard_map/ppermute | solution.py:185
  82.8 13.0 %collective-permute-start.18 = (bf16[96,3072]{1,0:T(8,128)(2,1)}, bf16[96,3072]{1,0:T(8,128)(2,1)}, u32[]{:S(2)}, u32[]{:S(2)}) collective-permute-start(bf16[96,3072]{1,0:T(8,128)(2,1)} %collective-permute-done.16.refs_18_), channel_id=1, source_target_pairs={{0,8},{1,9},{2,10},{3,11},{8,0},{9,1},{10,2},{11,3},{4,12},{5,13},... | collective-permute-start | bytes 1769480 | tf_op jit(solution)/shard_map/ppermute | solution.py:185
  96.8 27.3 %all-to-all-start.1 = ((bf16[8,2,128,384]{3,2,1,0:T(8,128)(2,1)}), bf16[8,2,128,384]{3,2,1,0:T(8,128)(2,1)S(1)}, u32[]{:S(2)}, u32[]{:S(2)}) async-start(bf16[8,2,128,384]{3,2,1,0:T(8,128)(2,1)} %attend.1), calls=%async_computation.1 | async-start | bytes 3145728 | tf_op jit(solution)/shard_map/all_to_all | solution.py:237
  101.6 14.8 %collective-permute-start.25 = (bf16[96,3072]{1,0:T(8,128)(2,1)}, bf16[96,3072]{1,0:T(8,128)(2,1)S(1)}, u32[]{:S(2)}, u32[]{:S(2)}) collective-permute-start(bf16[96,3072]{1,0:T(8,128)(2,1)} %collective-permute-done.23.refs_24_), channel_id=1, source_target_pairs={{0,64},{1,65},{2,66},{3,67},{8,72},{9,73},{10,74},{11,75},{4,68},{... | collective-permute-start | bytes 1769480 | tf_op jit(solution)/shard_map/ppermute | solution.py:185
  101.8 17.5 %collective-permute-start.29 = (bf16[96,3072]{1,0:T(8,128)(2,1)}, bf16[96,3072]{1,0:T(8,128)(2,1)}, u32[]{:S(2)}, u32[]{:S(2)}) collective-permute-start(bf16[96,3072]{1,0:T(8,128)(2,1)} %copy-done.19), channel_id=1, source_target_pairs={{0,192},{1,193},{2,194},{3,195},{8,200},{9,201},{10,202},{11,203},... | collective-permute-start | bytes 1769480 | tf_op jit(solution)/shard_map/ppermute | solution.py:185
  116.4 5.0 %collective-permute-start.26 = (bf16[96,3072]{1,0:T(8,128)(2,1)S(1)}, bf16[96,3072]{1,0:T(8,128)(2,1)}, u32[]{:S(2)}, u32[]{:S(2)}) collective-permute-start(bf16[96,3072]{1,0:T(8,128)(2,1)S(1)} %collective-permute-done.25.refs_26_), channel_id=1, source_target_pairs={{0,8},{1,9},{2,10},{3,11},{8,0},{9,1},{10,2},{11,3},{4,12},{5,13},... | collective-permute-start | bytes 1769480 | tf_op jit(solution)/shard_map/ppermute | solution.py:185
  118.8 3.5 %collective-permute-start.28 = (bf16[96,3072]{1,0:T(8,128)(2,1)}, bf16[96,3072]{1,0:T(8,128)(2,1)}, u32[]{:S(2)}, u32[]{:S(2)}) collective-permute-start(bf16[96,3072]{1,0:T(8,128)(2,1)} %copy-done.19), channel_id=1, source_target_pairs={{0,8},{1,9},{2,10},{3,11},{8,0},{9,1},{10,2},{11,3},{4,12},{5,13},... | collective-permute-start | bytes 1769480 | tf_op jit(solution)/shard_map/ppermute | solution.py:185
  118.8 4.3 %collective-permute-start.22 = (bf16[96,3072]{1,0:T(8,128)(2,1)S(1)}, bf16[96,3072]{1,0:T(8,128)(2,1)}, u32[]{:S(2)}, u32[]{:S(2)}) collective-permute-start(bf16[96,3072]{1,0:T(8,128)(2,1)S(1)} %collective-permute-done.21.refs_22_), channel_id=1, source_target_pairs={{0,8},{1,9},{2,10},{3,11},{8,0},{9,1},{10,2},{11,3},{4,12},{5,13},... | collective-permute-start | bytes 1769480 | tf_op jit(solution)/shard_map/ppermute | solution.py:185
  119.3 4.0 %collective-permute-start.24 = (bf16[96,3072]{1,0:T(8,128)(2,1)}, bf16[96,3072]{1,0:T(8,128)(2,1)}, u32[]{:S(2)}, u32[]{:S(2)}) collective-permute-start(bf16[96,3072]{1,0:T(8,128)(2,1)} %collective-permute-done.23.refs_24_), channel_id=1, source_target_pairs={{0,8},{1,9},{2,10},{3,11},{8,0},{9,1},{10,2},{11,3},{4,12},{5,13},... | collective-permute-start | bytes 1769480 | tf_op jit(solution)/shard_map/ppermute | solution.py:185
  119.3 4.8 %collective-permute-start.30 = (bf16[96,3072]{1,0:T(8,128)(2,1)}, bf16[96,3072]{1,0:T(8,128)(2,1)}, u32[]{:S(2)}, u32[]{:S(2)}) collective-permute-start(bf16[96,3072]{1,0:T(8,128)(2,1)} %collective-permute-done.29.refs_30_), channel_id=1, source_target_pairs={{0,8},{1,9},{2,10},{3,11},{8,0},{9,1},{10,2},{11,3},{4,12},{5,13},... | collective-permute-start | bytes 1769480 | tf_op jit(solution)/shard_map/ppermute | solution.py:185
  (22 other events, 413.6 us)

commit v4 on v3

--- a/solution.py
+++ b/solution.py
@@ -119,10 +119,18 @@
 
 
 def project_kernel(place_ref, *refs):
-    x_ref, scale_ref, tan_ref, gated_ref, out_tan_ref, all_ref, held_ref, sem = refs[-8:]
-    weights = refs[:-8]
+    x_ref, scale_ref, tan_ref, gated_ref, out_tan_ref, all_ref, held_ref, x_sem, sem = refs[-9:]
+    weights = refs[:-9]
     blocks, depth, _ = held_ref.shape
     height = depth // place_ref.shape[0]
+    pieces, _, rows, width = x_ref.shape
+    for piece in range(pieces):
+        for which in range(2):
+            pltpu.make_async_copy(
+                x_ref.at[piece, which],
+                all_ref.at[pl.ds(which * rows, rows), pl.ds(piece * width, width)],
+                x_sem,
+            ).start()
     for n in range(blocks):
         at = 0
         for weight in weights:
@@ -134,11 +142,7 @@
                     sem.at[n],
                 ).start()
                 at += 1
-    pieces, _, rows, width = x_ref.shape
-    for piece in range(pieces):
-        columns = slice(piece * width, (piece + 1) * width)
-        all_ref[:rows, columns] = x_ref[piece, 0]
-        all_ref[rows:, columns] = x_ref[piece, 1]
+    pltpu.make_async_copy(all_ref, all_ref, x_sem).wait()
     for n in range(blocks):
         pltpu.make_async_copy(held_ref.at[n], held_ref.at[n], sem.at[n]).wait()
         projected = jnp.dot(all_ref[...], held_ref[n], preferred_element_type=jnp.float32)
@@ -160,13 +164,14 @@
     return pl.pallas_call(
         project_kernel,
         in_specs=[pl.BlockSpec(memory_space=pltpu.SMEM)]
-        + [pl.BlockSpec(memory_space=pl.ANY)] * len(weights)
-        + [in_vmem] * 3,
+        + [pl.BlockSpec(memory_space=pl.ANY)] * (len(weights) + 1)
+        + [in_vmem] * 2,
         out_specs=[in_vmem] * 2,
         out_shape=[out, out],
         scratch_shapes=[
             pltpu.VMEM((2 * rows, depth), jnp.bfloat16),
             pltpu.VMEM((columns // BLOCK, depth, BLOCK), jnp.bfloat16),
+            pltpu.SemaphoreType.DMA,
             pltpu.SemaphoreType.DMA((columns // BLOCK,)),
         ],
         compiler_params=pltpu.CompilerParams(vmem_limit_bytes=60 * MIB),
@@ -220,24 +225,32 @@
     before[3] = send(z[3], NEXT_X, before[2])
     far[3] = send(later[3], LAST_X, later[2])
 
-    weights, swapped, places = [], {}, []
+    late = [send(block, OTHER_CORE, far[2]) for block in (far[2], z[3], later[3])]
+    swapped = {(2, 2): late[0], (3, 0): late[1], (3, 1): late[2]}
+    weights, places = [], []
     for at, pairs in enumerate((0, -toward, toward, 2)):
         for block, steps in ((z[at], 0), (before[at], -1), (later[at], 1), (far[at], 2)):
             place = (x + steps) % 4 * 8 + (z_pair + pairs) % 4 * 2
-            after = [before[1], far[1], before[2], far[2]][at]
-            swapped[at, steps] = send(block, OTHER_CORE, after)
+            after = [[before[1]], [far[1]], [before[2]], [far[2]]][at]
+            if (at, steps) == (3, -1) or (at, steps) == (3, 2):
+                after = late
+            if (at, steps) not in swapped:
+                swapped[at, steps] = send(block, OTHER_CORE, *after)
             weights += [block, swapped[at, steps]]
             places += [place + core, place + 1 - core]
 
     early = [swapped[at, steps] for at in (0, 1) for steps in (0, -1, 1, 2)]
     during = [swapped[2, steps] for steps in (0, -1, 1)]
-    received = lax.optimization_barrier((received, z[3], before[2], later[2], *early))[0]
+    places = jnp.stack(places).astype(jnp.int32)
+    received, places = lax.optimization_barrier(
+        (received, places, z[3], before[2], later[2], *early)
+    )[:2]
     results = attend(received)
     results = lax.optimization_barrier((results, far[2], later[3], *during))[0]
     results = lax.all_to_all(results, "seq", 0, 0, tiled=True)
 
     gated, tangent = project(
-        weights, jnp.stack(places).astype(jnp.int32), results, gate_scale, gate_tangent
+        weights, places, results, gate_scale, gate_tangent
     )
     return (gated, tangent)
 

time: 136 us -> 140 us (1.029)
  Pallas kernels: 27.1 us -> 31.6 us
  waiting for transfers between devices: 63.2 us -> 61.6 us
    pallas_call x1, Pallas kernels: 10.4 us -> 14.9 us  [project(): pl.pallas_call(project_kernel, in_specs=[pl.BlockSpec(memory_space=pltpu....]
    ppermute x31, waiting for transfers between devices: 62.4 us -> 60.8 us  [send(): return lax.ppermute(value, AXES, moves_of)]
    unnamed x42 -> x54, local copies, waits for them, and re-layouts: 2.22 us -> 3.16 us
  transfers between devices with their start and end apart: 33 -> 33, of which waited for: 18 -> 13; matrix products, arithmetic and copies ran while one was open for 0% -> 0% of each run, Pallas kernels for 12% -> 12%
where the time goes in v4:
time: 140 us
  waiting for transfers between devices  61.6 us (44%)
  starting transfers between devices  41.5 us (30%)
  Pallas kernels  31.6 us (23%)
  local copies, waits for them, and re-layouts  3.81 us (3%)
    ppermute x31, waiting for transfers between devices, send(): return lax.ppermute(value, AXES, moves_of)  60.8 us
    ppermute x31, starting transfers between devices, send(): return lax.ppermute(value, AXES, moves_of)  32.8 us
    pallas_call x1, Pallas kernels, project(): pl.pallas_call(project_kernel, in_specs=[pl.BlockSpec(memory_space=pltpu....  14.9 us
    pallas_call x1, Pallas kernels, attend(): pl.pallas_call(attend_kernel, grid=(heads,), in_specs=[pl.BlockSpec((piec...  11.6 us
    pallas_call x1, Pallas kernels, pack(): pl.pallas_call(pack_kernel, grid=(rows // block,), in_specs=[pl.BlockSpec...  5.12 us
    all_to_all x1, starting transfers between devices, on_device(): received = lax.all_to_all(sent, 'seq', 0, 0, tiled=True)  4.6 us
    all_to_all x1, starting transfers between devices, on_device(): results = lax.all_to_all(results, 'seq', 0, 0, tiled=True)  4.16 us
    unnamed x54, local copies, waits for them, and re-layouts  3.16 us
  transfers between devices with their start and end apart: 33, of which 13 were waited for; matrix products, arithmetic and copies ran while one was open for 0% of the time, Pallas kernels for 12%

profile of v4, /device:TPU:1, one launch (start us, length us, event | category | flops | bytes accessed | tf_op | source)
XLA Modules:
  0.0 139.8 jit_solution(8745265511810687500)
XLA Ops:
  0.6 6.9 %collective-permute-start = (bf16[96,3072]{1,0:T(8,128)(2,1)}, bf16[96,3072]{1,0:T(8,128)(2,1)S(1)}, u32[]{:S(2)}, u32[]{:S(2)}) collective-permute-start(bf16[96,3072]{1,0:T(8,128)(2,1)} %refs_0_.3), channel_id=1, source_target_pairs={{0,48},{1,49},{2,50},{3,51},{8,56},{9,57},{10,58},{11,59},{4,20},{... | collective-permute-start | bytes 1769480 | tf_op jit(solution)/shard_map/ppermute | solution.py:190
  7.6 2.5 %collective-permute-start.2 = (bf16[96,3072]{1,0:T(8,128)(2,1)}, bf16[96,3072]{1,0:T(8,128)(2,1)S(1)}, u32[]{:S(2)}, u32[]{:S(2)}) collective-permute-start(bf16[96,3072]{1,0:T(8,128)(2,1)} %refs_0_.3), channel_id=1, source_target_pairs={{0,192},{1,193},{2,194},{3,195},{8,200},{9,201},{10,202},{11,203},... | collective-permute-start | bytes 1769480 | tf_op jit(solution)/shard_map/ppermute | solution.py:190
  10.0 5.1 %pack.1 = bf16[8,6,128,384]{3,2,1,0:T(8,128)(2,1)} custom-call(bf16[1,128,3072]{2,1,0:T(8,128)(2,1)} %refs_0_.2, bf16[1,128,3072]{2,1,0:T(8,128)(2,1)} %refs_1_.1, bf16[1,128,3072]{2,1,0:T(8,128)(2,1)} %refs_2_.1, bf16[1,128,3072]{2,1,0:T(8,128)(2,1)} %refs_3_.1, bf16[1,128,3072]{2,1,0:T(8,128)(2,1)} %refs_4_.1, bf16[1,128,3072]{2,1,0:T(8,128)(2,1)} %refs_5_.1), custom_call_target="tpu_custom_call" | custom-call | bytes 9437184 | tf_op jit(solution)/shard_map/pack/pallas_call | solution.py:48
  15.2 4.7 %collective-permute-done.refs_8_ = bf16[96,3072]{1,0:T(8,128)(2,1)S(1)} collective-permute-done((bf16[96,3072]{1,0:T(8,128)(2,1)}, bf16[96,3072]{1,0:T(8,128)(2,1)S(1)}, u32[]{:S(2)}, u32[]{:S(2)}) %collective-permute-start) | collective-permute-done | bytes 589856 | tf_op jit(solution)/shard_map/ppermute | solution.py:190
  19.9 2.2 %collective-permute-done.2.refs_4_ = bf16[96,3072]{1,0:T(8,128)(2,1)S(1)} collective-permute-done((bf16[96,3072]{1,0:T(8,128)(2,1)}, bf16[96,3072]{1,0:T(8,128)(2,1)S(1)}, u32[]{:S(2)}, u32[]{:S(2)}) %collective-permute-start.2) | collective-permute-done | bytes 589856 | tf_op jit(solution)/shard_map/ppermute | solution.py:190
  22.0 3.0 %collective-permute-done.1.refs_2_ = bf16[96,3072]{1,0:T(8,128)(2,1)S(1)} collective-permute-done((bf16[96,3072]{1,0:T(8,128)(2,1)}, bf16[96,3072]{1,0:T(8,128)(2,1)S(1)}, u32[]{:S(2)}, u32[]{:S(2)}) %collective-permute-start.1) | collective-permute-done | bytes 589856 | tf_op jit(solution)/shard_map/ppermute | solution.py:190
  25.0 4.6 %all-to-all-start = ((bf16[8,6,128,384]{3,2,1,0:T(8,128)(2,1)}), bf16[8,6,128,384]{3,2,1,0:T(8,128)(2,1)}, u32[]{:S(2)}, u32[]{:S(2)}) async-start(bf16[8,6,128,384]{3,2,1,0:T(8,128)(2,1)} %pack.1), calls=%async_computation | async-start | bytes 9437184 | tf_op jit(solution)/shard_map/all_to_all | solution.py:214
  30.0 1.2 collective-permute-start.9
  31.2 1.3 collective-permute-start.4
  32.5 1.4 %collective-permute-start.3 = (bf16[96,3072]{1,0:T(8,128)(2,1)S(1)}, bf16[96,3072]{1,0:T(8,128)(2,1)}, u32[]{:S(2)}, u32[]{:S(2)}) collective-permute-start(bf16[96,3072]{1,0:T(8,128)(2,1)S(1)} %collective-permute-done.refs_8_), channel_id=1, source_target_pairs={{0,52},{1,53},{2,54},{3,55},{8,60},{9,61},{10,62},{11,63},{4,16},{... | collective-permute-start | bytes 1769480 | tf_op jit(solution)/shard_map/ppermute | solution.py:190
  33.9 8.6 %collective-permute-done.7.refs_12_ = bf16[96,3072]{1,0:T(8,128)(2,1)S(1)} collective-permute-done((bf16[96,3072]{1,0:T(8,128)(2,1)S(1)}, bf16[96,3072]{1,0:T(8,128)(2,1)S(1)}, u32[]{:S(2)}, u32[]{:S(2)}) %collective-permute-start.7) | collective-permute-done | bytes 589856 | tf_op jit(solution)/shard_map/ppermute | solution.py:190
  42.5 1.8 %collective-permute-start.14 = (bf16[96,3072]{1,0:T(8,128)(2,1)S(1)}, bf16[96,3072]{1,0:T(8,128)(2,1)S(1)}, u32[]{:S(2)}, u32[]{:S(2)}) collective-permute-start(bf16[96,3072]{1,0:T(8,128)(2,1)S(1)} %collective-permute-done.7.refs_12_), channel_id=1, source_target_pairs={{0,192},{1,193},{2,194},{3,195},{8,200},{9,201},{10,202},{11,203},... | collective-permute-start | bytes 1769480 | tf_op jit(solution)/shard_map/ppermute | solution.py:190
  44.3 12.4 %collective-permute-done.5.refs_6_ = bf16[96,3072]{1,0:T(8,128)(2,1)S(1)} collective-permute-done((bf16[96,3072]{1,0:T(8,128)(2,1)S(1)}, bf16[96,3072]{1,0:T(8,128)(2,1)S(1)}, u32[]{:S(2)}, u32[]{:S(2)}) %collective-permute-start.5) | collective-permute-done | bytes 589856 | tf_op jit(solution)/shard_map/ppermute | solution.py:190
  56.7 3.0 %collective-permute-start.13 = (bf16[96,3072]{1,0:T(8,128)(2,1)S(1)}, bf16[96,3072]{1,0:T(8,128)(2,1)S(1)}, u32[]{:S(2)}, u32[]{:S(2)}) collective-permute-start(bf16[96,3072]{1,0:T(8,128)(2,1)S(1)} %collective-permute-done.5.refs_6_), channel_id=1, source_target_pairs={{0,8},{1,9},{2,10},{3,11},{8,0},{9,1},{10,2},{11,3},{4,12},{5,13},... | collective-permute-start | bytes 1769480 | tf_op jit(solution)/shard_map/ppermute | solution.py:190
  59.7 2.7 %collective-permute-start.8 = (bf16[96,3072]{1,0:T(8,128)(2,1)}, bf16[96,3072]{1,0:T(8,128)(2,1)}, u32[]{:S(2)}, u32[]{:S(2)}) collective-permute-start(bf16[96,3072]{1,0:T(8,128)(2,1)} %collective-permute-done.4.refs_16_), channel_id=1, source_target_pairs={{0,192},{1,193},{2,194},{3,195},{8,200},{9,201},{10,202},{11,203},... | collective-permute-start | bytes 1769480 | tf_op jit(solution)/shard_map/ppermute | solution.py:190
  62.4 1.5 %collective-permute-start.12 = (bf16[96,3072]{1,0:T(8,128)(2,1)S(1)}, bf16[96,3072]{1,0:T(8,128)(2,1)S(1)}, u32[]{:S(2)}, u32[]{:S(2)}) collective-permute-start(bf16[96,3072]{1,0:T(8,128)(2,1)S(1)} %collective-permute-done.2.refs_4_), channel_id=1, source_target_pairs={{0,8},{1,9},{2,10},{3,11},{8,0},{9,1},{10,2},{11,3},{4,12},{5,13},... | collective-permute-start | bytes 1769480 | tf_op jit(solution)/shard_map/ppermute | solution.py:190
  64.5 11.3 %collective-permute-done.6.refs_18_ = bf16[96,3072]{1,0:T(8,128)(2,1)} collective-permute-done((bf16[96,3072]{1,0:T(8,128)(2,1)}, bf16[96,3072]{1,0:T(8,128)(2,1)}, u32[]{:S(2)}, u32[]{:S(2)}) %collective-permute-start.6) | collective-permute-done | bytes 589856 | tf_op jit(solution)/shard_map/ppermute | solution.py:190
  75.7 1.3 collective-permute-start.17
  77.8 0.8 collective-permute-done.17.refs_13_
  79.0 1.3 collective-permute-done.15.refs_9_
  80.3 1.0 collective-permute-start.26
  83.3 0.8 all-to-all-done.in_ref
  84.1 11.6 %attend.1 = bf16[8,2,128,384]{3,2,1,0:T(8,128)(2,1)} custom-call(bf16[8,6,128,384]{3,2,1,0:T(8,128)(2,1)} %all-to-all-done.in_ref), custom_call_target="tpu_custom_call" | custom-call | flops 4831838208 | bytes 6291456 | tf_op jit(solution)/shard_map/attend/pallas_call | solution.py:102
  96.8 4.2 %all-to-all-start.1 = ((bf16[8,2,128,384]{3,2,1,0:T(8,128)(2,1)}), bf16[8,2,128,384]{3,2,1,0:T(8,128)(2,1)S(1)}, u32[]{:S(2)}, u32[]{:S(2)}) async-start(bf16[8,2,128,384]{3,2,1,0:T(8,128)(2,1)} %attend.1), calls=%async_computation.1 | async-start | bytes 3145728 | tf_op jit(solution)/shard_map/all_to_all | solution.py:250
  101.7 2.2 %collective-permute-start.29 = (bf16[96,3072]{1,0:T(8,128)(2,1)S(1)}, bf16[96,3072]{1,0:T(8,128)(2,1)S(1)}, u32[]{:S(2)}, u32[]{:S(2)}) collective-permute-start(bf16[96,3072]{1,0:T(8,128)(2,1)S(1)} %collective-permute-done.26.refs_28_), channel_id=1, source_target_pairs={{0,192},{1,193},{2,194},{3,195},{8,200},{9,201},{10,202},{11,203},... | collective-permute-start | bytes 1769480 | tf_op jit(solution)/shard_map/ppermute | solution.py:190
  104.6 11.6 %collective-permute-done.29.refs_30_ = bf16[96,3072]{1,0:T(8,128)(2,1)S(1)} collective-permute-done((bf16[96,3072]{1,0:T(8,128)(2,1)S(1)}, bf16[96,3072]{1,0:T(8,128)(2,1)S(1)}, u32[]{:S(2)}, u32[]{:S(2)}) %collective-permute-start.29) | collective-permute-done | bytes 589856 | tf_op jit(solution)/shard_map/ppermute | solution.py:190
  116.2 1.3 collective-permute-start.30
  117.5 3.4 %collective-permute-done.25.refs_26_ = bf16[96,3072]{1,0:T(8,128)(2,1)S(1)} collective-permute-done((bf16[96,3072]{1,0:T(8,128)(2,1)}, bf16[96,3072]{1,0:T(8,128)(2,1)S(1)}, u32[]{:S(2)}, u32[]{:S(2)}) %collective-permute-start.25) | collective-permute-done | bytes 589856 | tf_op jit(solution)/shard_map/ppermute | solution.py:190
  121.8 0.9 copy-done.26
  122.7 0.8 collective-permute-done.28.refs_27_
  123.5 1.2 copy-done
  124.7 14.9 %project.1 = (bf16[1,128,3072]{2,1,0:T(8,128)(2,1)}, bf16[1,128,3072]{2,1,0:T(8,128)(2,1)}) custom-call(s32[32]{0:T(128)} %stack.131.place_ref, bf16[96,3072]{1,0:T(8,128)(2,1)} %refs_0_.3, bf16[96,3072]{1,0:T(8,128)(2,1)} %copy-done.12, bf16[96,3072]{1,0:T(8,128)(2,1)} %copy-done.4, bf16[96,3072]{1,0:T(8,128)(2,1)} %copy-done.10, ...), custom_call_target="tpu_custom_call" | custom-call | flops 4831838208 | bytes 18874368 | tf_op jit(solution)/shard_map/project/pallas_call | solution.py:164
  (92 shorter events, 7.3 us)
Async XLA Ops:
  0.6 19.2 %collective-permute-start = (bf16[96,3072]{1,0:T(8,128)(2,1)}, bf16[96,3072]{1,0:T(8,128)(2,1)S(1)}, u32[]{:S(2)}, u32[]{:S(2)}) collective-permute-start(bf16[96,3072]{1,0:T(8,128)(2,1)} %refs_0_.3), channel_id=1, source_target_pairs={{0,48},{1,49},{2,50},{3,51},{8,56},{9,57},{10,58},{11,59},{4,20},{... | collective-permute-start | bytes 1769480 | tf_op jit(solution)/shard_map/ppermute | solution.py:190
  7.6 14.5 %collective-permute-start.2 = (bf16[96,3072]{1,0:T(8,128)(2,1)}, bf16[96,3072]{1,0:T(8,128)(2,1)S(1)}, u32[]{:S(2)}, u32[]{:S(2)}) collective-permute-start(bf16[96,3072]{1,0:T(8,128)(2,1)} %refs_0_.3), channel_id=1, source_target_pairs={{0,192},{1,193},{2,194},{3,195},{8,200},{9,201},{10,202},{11,203},... | collective-permute-start | bytes 1769480 | tf_op jit(solution)/shard_map/ppermute | solution.py:190
  10.0 15.0 %collective-permute-start.1 = (bf16[96,3072]{1,0:T(8,128)(2,1)}, bf16[96,3072]{1,0:T(8,128)(2,1)S(1)}, u32[]{:S(2)}, u32[]{:S(2)}) collective-permute-start(bf16[96,3072]{1,0:T(8,128)(2,1)} %refs_0_.3), channel_id=1, source_target_pairs={{0,64},{1,65},{2,66},{3,67},{8,72},{9,73},{10,74},{11,75},{4,68},{... | collective-permute-start | bytes 1769480 | tf_op jit(solution)/shard_map/ppermute | solution.py:190
  25.0 59.1 %all-to-all-start = ((bf16[8,6,128,384]{3,2,1,0:T(8,128)(2,1)}), bf16[8,6,128,384]{3,2,1,0:T(8,128)(2,1)}, u32[]{:S(2)}, u32[]{:S(2)}) async-start(bf16[8,6,128,384]{3,2,1,0:T(8,128)(2,1)} %pack.1), calls=%async_computation | async-start | bytes 9437184 | tf_op jit(solution)/shard_map/all_to_all | solution.py:214
  29.7 12.8 %collective-permute-start.7 = (bf16[96,3072]{1,0:T(8,128)(2,1)S(1)}, bf16[96,3072]{1,0:T(8,128)(2,1)S(1)}, u32[]{:S(2)}, u32[]{:S(2)}) collective-permute-start(bf16[96,3072]{1,0:T(8,128)(2,1)S(1)} %collective-permute-done.refs_8_), channel_id=1, source_target_pairs={{0,192},{1,193},{2,194},{3,195},{8,200},{9,201},{10,202},{11,203},... | collective-permute-start | bytes 1769480 | tf_op jit(solution)/shard_map/ppermute | solution.py:190
  30.0 14.3 %collective-permute-start.9 = (bf16[96,3072]{1,0:T(8,128)(2,1)S(1)}, bf16[96,3072]{1,0:T(8,128)(2,1)S(1)}, u32[]{:S(2)}, u32[]{:S(2)}) collective-permute-start(bf16[96,3072]{1,0:T(8,128)(2,1)S(1)} %collective-permute-done.refs_8_), channel_id=1, source_target_pairs={{0,64},{1,65},{2,66},{3,67},{8,72},{9,73},{10,74},{11,75},{4,68},{... | collective-permute-start | bytes 1769480 | tf_op jit(solution)/shard_map/ppermute | solution.py:190
  31.2 25.5 %collective-permute-start.5 = (bf16[96,3072]{1,0:T(8,128)(2,1)S(1)}, bf16[96,3072]{1,0:T(8,128)(2,1)S(1)}, u32[]{:S(2)}, u32[]{:S(2)}) collective-permute-start(bf16[96,3072]{1,0:T(8,128)(2,1)S(1)} %collective-permute-done.1.refs_2_), channel_id=1, source_target_pairs={{0,64},{1,65},{2,66},{3,67},{8,72},{9,73},{10,74},{11,75},{4,68},{... | collective-permute-start | bytes 1769480 | tf_op jit(solution)/shard_map/ppermute | solution.py:190
  31.2 28.5 %collective-permute-start.4 = (bf16[96,3072]{1,0:T(8,128)(2,1)S(1)}, bf16[96,3072]{1,0:T(8,128)(2,1)}, u32[]{:S(2)}, u32[]{:S(2)}) collective-permute-start(bf16[96,3072]{1,0:T(8,128)(2,1)S(1)} %copy-done.1), channel_id=1, source_target_pairs={{0,52},{1,53},{2,54},{3,55},{8,60},{9,61},{10,62},{11,63},{4,16},{... | collective-permute-start | bytes 1769480 | tf_op jit(solution)/shard_map/ppermute | solution.py:190
  32.5 27.2 %collective-permute-start.3 = (bf16[96,3072]{1,0:T(8,128)(2,1)S(1)}, bf16[96,3072]{1,0:T(8,128)(2,1)}, u32[]{:S(2)}, u32[]{:S(2)}) collective-permute-start(bf16[96,3072]{1,0:T(8,128)(2,1)S(1)} %collective-permute-done.refs_8_), channel_id=1, source_target_pairs={{0,52},{1,53},{2,54},{3,55},{8,60},{9,61},{10,62},{11,63},{4,16},{... | collective-permute-start | bytes 1769480 | tf_op jit(solution)/shard_map/ppermute | solution.py:190
  42.5 19.9 %collective-permute-start.14 = (bf16[96,3072]{1,0:T(8,128)(2,1)S(1)}, bf16[96,3072]{1,0:T(8,128)(2,1)S(1)}, u32[]{:S(2)}, u32[]{:S(2)}) collective-permute-start(bf16[96,3072]{1,0:T(8,128)(2,1)S(1)} %collective-permute-done.7.refs_12_), channel_id=1, source_target_pairs={{0,192},{1,193},{2,194},{3,195},{8,200},{9,201},{10,202},{11,203},... | collective-permute-start | bytes 1769480 | tf_op jit(solution)/shard_map/ppermute | solution.py:190
  56.7 7.3 %collective-permute-start.13 = (bf16[96,3072]{1,0:T(8,128)(2,1)S(1)}, bf16[96,3072]{1,0:T(8,128)(2,1)S(1)}, u32[]{:S(2)}, u32[]{:S(2)}) collective-permute-start(bf16[96,3072]{1,0:T(8,128)(2,1)S(1)} %collective-permute-done.5.refs_6_), channel_id=1, source_target_pairs={{0,8},{1,9},{2,10},{3,11},{8,0},{9,1},{10,2},{11,3},{4,12},{5,13},... | collective-permute-start | bytes 1769480 | tf_op jit(solution)/shard_map/ppermute | solution.py:190
  59.6 4.4 %collective-permute-start.11 = (bf16[96,3072]{1,0:T(8,128)(2,1)S(1)}, bf16[96,3072]{1,0:T(8,128)(2,1)S(1)}, u32[]{:S(2)}, u32[]{:S(2)}) collective-permute-start(bf16[96,3072]{1,0:T(8,128)(2,1)S(1)} %collective-permute-done.1.refs_2_), channel_id=1, source_target_pairs={{0,8},{1,9},{2,10},{3,11},{8,0},{9,1},{10,2},{11,3},{4,12},{5,13},... | collective-permute-start | bytes 1769480 | tf_op jit(solution)/shard_map/ppermute | solution.py:190
  59.7 16.0 %collective-permute-start.6 = (bf16[96,3072]{1,0:T(8,128)(2,1)}, bf16[96,3072]{1,0:T(8,128)(2,1)}, u32[]{:S(2)}, u32[]{:S(2)}) collective-permute-start(bf16[96,3072]{1,0:T(8,128)(2,1)} %collective-permute-done.4.refs_16_), channel_id=1, source_target_pairs={{0,64},{1,65},{2,66},{3,67},{8,72},{9,73},{10,74},{11,75},{4,68},{... | collective-permute-start | bytes 1769480 | tf_op jit(solution)/shard_map/ppermute | solution.py:190
  59.7 17.3 %collective-permute-start.8 = (bf16[96,3072]{1,0:T(8,128)(2,1)}, bf16[96,3072]{1,0:T(8,128)(2,1)}, u32[]{:S(2)}, u32[]{:S(2)}) collective-permute-start(bf16[96,3072]{1,0:T(8,128)(2,1)} %collective-permute-done.4.refs_16_), channel_id=1, source_target_pairs={{0,192},{1,193},{2,194},{3,195},{8,200},{9,201},{10,202},{11,203},... | collective-permute-start | bytes 1769480 | tf_op jit(solution)/shard_map/ppermute | solution.py:190
  62.4 14.9 %collective-permute-start.12 = (bf16[96,3072]{1,0:T(8,128)(2,1)S(1)}, bf16[96,3072]{1,0:T(8,128)(2,1)S(1)}, u32[]{:S(2)}, u32[]{:S(2)}) collective-permute-start(bf16[96,3072]{1,0:T(8,128)(2,1)S(1)} %collective-permute-done.2.refs_4_), channel_id=1, source_target_pairs={{0,8},{1,9},{2,10},{3,11},{8,0},{9,1},{10,2},{11,3},{4,12},{5,13},... | collective-permute-start | bytes 1769480 | tf_op jit(solution)/shard_map/ppermute | solution.py:190
  64.0 13.6 %collective-permute-start.10 = (bf16[96,3072]{1,0:T(8,128)(2,1)S(1)}, bf16[96,3072]{1,0:T(8,128)(2,1)S(1)}, u32[]{:S(2)}, u32[]{:S(2)}) collective-permute-start(bf16[96,3072]{1,0:T(8,128)(2,1)S(1)} %copy-done.1), channel_id=1, source_target_pairs={{0,8},{1,9},{2,10},{3,11},{8,0},{9,1},{10,2},{11,3},{4,12},{5,13},... | collective-permute-start | bytes 1769480 | tf_op jit(solution)/shard_map/ppermute | solution.py:190
  64.1 13.7 %collective-permute-start.16 = (bf16[96,3072]{1,0:T(8,128)(2,1)S(1)}, bf16[96,3072]{1,0:T(8,128)(2,1)S(1)}, u32[]{:S(2)}, u32[]{:S(2)}) collective-permute-start(bf16[96,3072]{1,0:T(8,128)(2,1)S(1)} %collective-permute-done.9.refs_10_), channel_id=1, source_target_pairs={{0,8},{1,9},{2,10},{3,11},{8,0},{9,1},{10,2},{11,3},{4,12},{5,13},... | collective-permute-start | bytes 1769480 | tf_op jit(solution)/shard_map/ppermute | solution.py:190
  75.7 2.9 %collective-permute-start.17 = (bf16[96,3072]{1,0:T(8,128)(2,1)S(1)}, bf16[96,3072]{1,0:T(8,128)(2,1)S(1)}, u32[]{:S(2)}, u32[]{:S(2)}) collective-permute-start(bf16[96,3072]{1,0:T(8,128)(2,1)S(1)} %collective-permute-done.7.refs_12_), channel_id=1, source_target_pairs={{0,8},{1,9},{2,10},{3,11},{8,0},{9,1},{10,2},{11,3},{4,12},{5,13},... | collective-permute-start | bytes 1769480 | tf_op jit(solution)/shard_map/ppermute | solution.py:190
  77.0 3.3 %collective-permute-start.15 = (bf16[96,3072]{1,0:T(8,128)(2,1)S(1)}, bf16[96,3072]{1,0:T(8,128)(2,1)S(1)}, u32[]{:S(2)}, u32[]{:S(2)}) collective-permute-start(bf16[96,3072]{1,0:T(8,128)(2,1)S(1)} %collective-permute-done.refs_8_), channel_id=1, source_target_pairs={{0,8},{1,9},{2,10},{3,11},{8,0},{9,1},{10,2},{11,3},{4,12},{5,13},... | collective-permute-start | bytes 1769480 | tf_op jit(solution)/shard_map/ppermute | solution.py:190
  77.3 4.7 %collective-permute-start.18 = (bf16[96,3072]{1,0:T(8,128)(2,1)S(1)}, bf16[96,3072]{1,0:T(8,128)(2,1)S(1)}, u32[]{:S(2)}, u32[]{:S(2)}) collective-permute-start(bf16[96,3072]{1,0:T(8,128)(2,1)S(1)} %collective-permute-done.14.refs_14_), channel_id=1, source_target_pairs={{0,8},{1,9},{2,10},{3,11},{8,0},{9,1},{10,2},{11,3},{4,12},{5,13},... | collective-permute-start | bytes 1769480 | tf_op jit(solution)/shard_map/ppermute | solution.py:190
  77.5 18.1 %collective-permute-start.21 = (bf16[96,3072]{1,0:T(8,128)(2,1)}, bf16[96,3072]{1,0:T(8,128)(2,1)S(1)}, u32[]{:S(2)}, u32[]{:S(2)}) collective-permute-start(bf16[96,3072]{1,0:T(8,128)(2,1)} %collective-permute-done.8.refs_20_), channel_id=1, source_target_pairs={{0,8},{1,9},{2,10},{3,11},{8,0},{9,1},{10,2},{11,3},{4,12},{5,13},... | collective-permute-start | bytes 1769480 | tf_op jit(solution)/shard_map/ppermute | solution.py:190
  77.8 17.9 %collective-permute-start.22 = (bf16[96,3072]{1,0:T(8,128)(2,1)}, bf16[96,3072]{1,0:T(8,128)(2,1)S(1)}, u32[]{:S(2)}, u32[]{:S(2)}) collective-permute-start(bf16[96,3072]{1,0:T(8,128)(2,1)} %collective-permute-done.6.refs_18_), channel_id=1, source_target_pairs={{0,64},{1,65},{2,66},{3,67},{8,72},{9,73},{10,74},{11,75},{4,68},{... | collective-permute-start | bytes 1769480 | tf_op jit(solution)/shard_map/ppermute | solution.py:190
  78.6 17.1 %collective-permute-start.19 = (bf16[96,3072]{1,0:T(8,128)(2,1)}, bf16[96,3072]{1,0:T(8,128)(2,1)S(1)}, u32[]{:S(2)}, u32[]{:S(2)}) collective-permute-start(bf16[96,3072]{1,0:T(8,128)(2,1)} %collective-permute-done.4.refs_16_), channel_id=1, source_target_pairs={{0,8},{1,9},{2,10},{3,11},{8,0},{9,1},{10,2},{11,3},{4,12},{5,13},... | collective-permute-start | bytes 1769480 | tf_op jit(solution)/shard_map/ppermute | solution.py:190
  80.3 15.4 %collective-permute-start.26 = (bf16[96,3072]{1,0:T(8,128)(2,1)}, bf16[96,3072]{1,0:T(8,128)(2,1)S(1)}, u32[]{:S(2)}, u32[]{:S(2)}) collective-permute-start(bf16[96,3072]{1,0:T(8,128)(2,1)} %collective-permute-done.3.refs_24_), channel_id=1, source_target_pairs={{0,192},{1,193},{2,194},{3,195},{8,200},{9,201},{10,202},{11,203},... | collective-permute-start | bytes 1769480 | tf_op jit(solution)/shard_map/ppermute | solution.py:190
  82.0 13.7 %collective-permute-start.20 = (bf16[96,3072]{1,0:T(8,128)(2,1)}, bf16[96,3072]{1,0:T(8,128)(2,1)}, u32[]{:S(2)}, u32[]{:S(2)}) collective-permute-start(bf16[96,3072]{1,0:T(8,128)(2,1)} %collective-permute-done.6.refs_18_), channel_id=1, source_target_pairs={{0,8},{1,9},{2,10},{3,11},{8,0},{9,1},{10,2},{11,3},{4,12},{5,13},... | collective-permute-start | bytes 1769480 | tf_op jit(solution)/shard_map/ppermute | solution.py:190
  96.8 26.7 %all-to-all-start.1 = ((bf16[8,2,128,384]{3,2,1,0:T(8,128)(2,1)}), bf16[8,2,128,384]{3,2,1,0:T(8,128)(2,1)S(1)}, u32[]{:S(2)}, u32[]{:S(2)}) async-start(bf16[8,2,128,384]{3,2,1,0:T(8,128)(2,1)} %attend.1), calls=%async_computation.1 | async-start | bytes 3145728 | tf_op jit(solution)/shard_map/all_to_all | solution.py:250
  100.9 3.7 %collective-permute-start.27 = (bf16[96,3072]{1,0:T(8,128)(2,1)S(1)}, bf16[96,3072]{1,0:T(8,128)(2,1)S(1)}, u32[]{:S(2)}, u32[]{:S(2)}) collective-permute-start(bf16[96,3072]{1,0:T(8,128)(2,1)S(1)} %collective-permute-done.26.refs_28_), channel_id=1, source_target_pairs={{0,8},{1,9},{2,10},{3,11},{8,0},{9,1},{10,2},{11,3},{4,12},{5,13},... | collective-permute-start | bytes 1769480 | tf_op jit(solution)/shard_map/ppermute | solution.py:190
  101.6 3.0 %collective-permute-start.24 = (bf16[96,3072]{1,0:T(8,128)(2,1)}, bf16[96,3072]{1,0:T(8,128)(2,1)S(1)}, u32[]{:S(2)}, u32[]{:S(2)}) collective-permute-start(bf16[96,3072]{1,0:T(8,128)(2,1)} %collective-permute-done.3.refs_24_), channel_id=1, source_target_pairs={{0,8},{1,9},{2,10},{3,11},{8,0},{9,1},{10,2},{11,3},{4,12},{5,13},... | collective-permute-start | bytes 1769480 | tf_op jit(solution)/shard_map/ppermute | solution.py:190
  101.7 14.5 %collective-permute-start.29 = (bf16[96,3072]{1,0:T(8,128)(2,1)S(1)}, bf16[96,3072]{1,0:T(8,128)(2,1)S(1)}, u32[]{:S(2)}, u32[]{:S(2)}) collective-permute-start(bf16[96,3072]{1,0:T(8,128)(2,1)S(1)} %collective-permute-done.26.refs_28_), channel_id=1, source_target_pairs={{0,192},{1,193},{2,194},{3,195},{8,200},{9,201},{10,202},{11,203},... | collective-permute-start | bytes 1769480 | tf_op jit(solution)/shard_map/ppermute | solution.py:190
  103.9 12.3 %collective-permute-start.23 = (bf16[96,3072]{1,0:T(8,128)(2,1)}, bf16[96,3072]{1,0:T(8,128)(2,1)S(1)}, u32[]{:S(2)}, u32[]{:S(2)}) collective-permute-start(bf16[96,3072]{1,0:T(8,128)(2,1)} %copy-done.18), channel_id=1, source_target_pairs={{0,8},{1,9},{2,10},{3,11},{8,0},{9,1},{10,2},{11,3},{4,12},{5,13},... | collective-permute-start | bytes 1769480 | tf_op jit(solution)/shard_map/ppermute | solution.py:190
  104.6 16.4 %collective-permute-start.25 = (bf16[96,3072]{1,0:T(8,128)(2,1)}, bf16[96,3072]{1,0:T(8,128)(2,1)S(1)}, u32[]{:S(2)}, u32[]{:S(2)}) collective-permute-start(bf16[96,3072]{1,0:T(8,128)(2,1)} %collective-permute-done.3.refs_24_), channel_id=1, source_target_pairs={{0,64},{1,65},{2,66},{3,67},{8,72},{9,73},{10,74},{11,75},{4,68},{... | collective-permute-start | bytes 1769480 | tf_op jit(solution)/shard_map/ppermute | solution.py:190
  116.2 5.6 %collective-permute-start.30 = (bf16[96,3072]{1,0:T(8,128)(2,1)S(1)}, bf16[96,3072]{1,0:T(8,128)(2,1)S(1)}, u32[]{:S(2)}, u32[]{:S(2)}) collective-permute-start(bf16[96,3072]{1,0:T(8,128)(2,1)S(1)} %collective-permute-done.29.refs_30_), channel_id=1, source_target_pairs={{0,8},{1,9},{2,10},{3,11},{8,0},{9,1},{10,2},{11,3},{4,12},{5,13},... | collective-permute-start | bytes 1769480 | tf_op jit(solution)/shard_map/ppermute | solution.py:190
  (28 other events, 462.7 us)

commit v5 on v3

--- a/solution.py
+++ b/solution.py
@@ -123,7 +123,8 @@
     weights = refs[:-8]
     blocks, depth, _ = held_ref.shape
     height = depth // place_ref.shape[0]
-    for n in range(blocks):
+
+    def fetch(n):
         at = 0
         for weight in weights:
             for first in range(0, weight.shape[0], height):
@@ -134,13 +135,18 @@
                     sem.at[n],
                 ).start()
                 at += 1
+
+    fetch(0)
     pieces, _, rows, width = x_ref.shape
     for piece in range(pieces):
         columns = slice(piece * width, (piece + 1) * width)
         all_ref[:rows, columns] = x_ref[piece, 0]
         all_ref[rows:, columns] = x_ref[piece, 1]
+    fetch(1)
     for n in range(blocks):
         pltpu.make_async_copy(held_ref.at[n], held_ref.at[n], sem.at[n]).wait()
+        if n + 2 < blocks:
+            fetch(n + 2)
         projected = jnp.dot(all_ref[...], held_ref[n], preferred_element_type=jnp.float32)
         primal, tangent = projected[:rows], projected[rows:]
         columns = slice(n * BLOCK, (n + 1) * BLOCK)
@@ -220,24 +226,32 @@
     before[3] = send(z[3], NEXT_X, before[2])
     far[3] = send(later[3], LAST_X, later[2])
 
-    weights, swapped, places = [], {}, []
+    late = [send(block, OTHER_CORE, far[2]) for block in (far[2], z[3], later[3])]
+    swapped = {(2, 2): late[0], (3, 0): late[1], (3, 1): late[2]}
+    weights, places = [], []
     for at, pairs in enumerate((0, -toward, toward, 2)):
         for block, steps in ((z[at], 0), (before[at], -1), (later[at], 1), (far[at], 2)):
             place = (x + steps) % 4 * 8 + (z_pair + pairs) % 4 * 2
-            after = [before[1], far[1], before[2], far[2]][at]
-            swapped[at, steps] = send(block, OTHER_CORE, after)
+            after = [[before[1]], [far[1]], [before[2]], [far[2]]][at]
+            if (at, steps) == (3, -1) or (at, steps) == (3, 2):
+                after = late
+            if (at, steps) not in swapped:
+                swapped[at, steps] = send(block, OTHER_CORE, *after)
             weights += [block, swapped[at, steps]]
             places += [place + core, place + 1 - core]
 
     early = [swapped[at, steps] for at in (0, 1) for steps in (0, -1, 1, 2)]
     during = [swapped[2, steps] for steps in (0, -1, 1)]
-    received = lax.optimization_barrier((received, z[3], before[2], later[2], *early))[0]
+    places = jnp.stack(places).astype(jnp.int32)
+    received, places = lax.optimization_barrier(
+        (received, places, z[3], before[2], later[2], *early)
+    )[:2]
     results = attend(received)
     results = lax.optimization_barrier((results, far[2], later[3], *during))[0]
     results = lax.all_to_all(results, "seq", 0, 0, tiled=True)
 
     gated, tangent = project(
-        weights, jnp.stack(places).astype(jnp.int32), results, gate_scale, gate_tangent
+        weights, places, results, gate_scale, gate_tangent
     )
     return (gated, tangent)
 

time: 136 us -> 136 us (level)
  waiting for transfers between devices: 63.2 us -> 61.6 us
    ppermute x31, waiting for transfers between devices: 62.4 us -> 60.8 us  [send(): return lax.ppermute(value, AXES, moves_of)]
    unnamed x42 -> x54, local copies, waits for them, and re-layouts: 2.22 us -> 3.16 us
  transfers between devices with their start and end apart: 33 -> 33, of which waited for: 18 -> 13; matrix products, arithmetic and copies ran while one was open for 0% -> 0% of each run, Pallas kernels for 12% -> 12%
where the time goes in v5:
time: 136 us
  waiting for transfers between devices  61.6 us (45%)
  starting transfers between devices  41.5 us (31%)
  Pallas kernels  27.4 us (20%)
  local copies, waits for them, and re-layouts  3.81 us (3%)
    ppermute x31, waiting for transfers between devices, send(): return lax.ppermute(value, AXES, moves_of)  60.8 us
    ppermute x31, starting transfers between devices, send(): return lax.ppermute(value, AXES, moves_of)  32.8 us
    pallas_call x1, Pallas kernels, attend(): pl.pallas_call(attend_kernel, grid=(heads,), in_specs=[pl.BlockSpec((piec...  11.6 us
    pallas_call x1, Pallas kernels, project(): pl.pallas_call(project_kernel, in_specs=[pl.BlockSpec(memory_space=pltpu....  10.8 us
    pallas_call x1, Pallas kernels, pack(): pl.pallas_call(pack_kernel, grid=(rows // block,), in_specs=[pl.BlockSpec...  5.12 us
    all_to_all x1, starting transfers between devices, on_device(): received = lax.all_to_all(sent, 'seq', 0, 0, tiled=True)  4.6 us
    all_to_all x1, starting transfers between devices, on_device(): results = lax.all_to_all(results, 'seq', 0, 0, tiled=True)  4.16 us
    unnamed x54, local copies, waits for them, and re-layouts  3.16 us
  transfers between devices with their start and end apart: 33, of which 13 were waited for; matrix products, arithmetic and copies ran while one was open for 0% of the time, Pallas kernels for 12%

profile of v5, /device:TPU:1, one launch (start us, length us, event | category | flops | bytes accessed | tf_op | source)
XLA Modules:
  0.0 135.6 jit_solution(9632843774512050288)
XLA Ops:
  0.6 6.9 %collective-permute-start = (bf16[96,3072]{1,0:T(8,128)(2,1)}, bf16[96,3072]{1,0:T(8,128)(2,1)S(1)}, u32[]{:S(2)}, u32[]{:S(2)}) collective-permute-start(bf16[96,3072]{1,0:T(8,128)(2,1)} %refs_0_.3), channel_id=1, source_target_pairs={{0,48},{1,49},{2,50},{3,51},{8,56},{9,57},{10,58},{11,59},{4,20},{... | collective-permute-start | bytes 1769480 | tf_op jit(solution)/shard_map/ppermute | solution.py:191
  7.6 2.5 %collective-permute-start.2 = (bf16[96,3072]{1,0:T(8,128)(2,1)}, bf16[96,3072]{1,0:T(8,128)(2,1)S(1)}, u32[]{:S(2)}, u32[]{:S(2)}) collective-permute-start(bf16[96,3072]{1,0:T(8,128)(2,1)} %refs_0_.3), channel_id=1, source_target_pairs={{0,192},{1,193},{2,194},{3,195},{8,200},{9,201},{10,202},{11,203},... | collective-permute-start | bytes 1769480 | tf_op jit(solution)/shard_map/ppermute | solution.py:191
  10.0 5.1 %pack.1 = bf16[8,6,128,384]{3,2,1,0:T(8,128)(2,1)} custom-call(bf16[1,128,3072]{2,1,0:T(8,128)(2,1)} %refs_0_.2, bf16[1,128,3072]{2,1,0:T(8,128)(2,1)} %refs_1_.1, bf16[1,128,3072]{2,1,0:T(8,128)(2,1)} %refs_2_.1, bf16[1,128,3072]{2,1,0:T(8,128)(2,1)} %refs_3_.1, bf16[1,128,3072]{2,1,0:T(8,128)(2,1)} %refs_4_.1, bf16[1,128,3072]{2,1,0:T(8,128)(2,1)} %refs_5_.1), custom_call_target="tpu_custom_call" | custom-call | bytes 9437184 | tf_op jit(solution)/shard_map/pack/pallas_call | solution.py:48
  15.2 4.7 %collective-permute-done.refs_8_ = bf16[96,3072]{1,0:T(8,128)(2,1)S(1)} collective-permute-done((bf16[96,3072]{1,0:T(8,128)(2,1)}, bf16[96,3072]{1,0:T(8,128)(2,1)S(1)}, u32[]{:S(2)}, u32[]{:S(2)}) %collective-permute-start) | collective-permute-done | bytes 589856 | tf_op jit(solution)/shard_map/ppermute | solution.py:191
  19.9 2.2 %collective-permute-done.2.refs_4_ = bf16[96,3072]{1,0:T(8,128)(2,1)S(1)} collective-permute-done((bf16[96,3072]{1,0:T(8,128)(2,1)}, bf16[96,3072]{1,0:T(8,128)(2,1)S(1)}, u32[]{:S(2)}, u32[]{:S(2)}) %collective-permute-start.2) | collective-permute-done | bytes 589856 | tf_op jit(solution)/shard_map/ppermute | solution.py:191
  22.0 3.0 %collective-permute-done.1.refs_2_ = bf16[96,3072]{1,0:T(8,128)(2,1)S(1)} collective-permute-done((bf16[96,3072]{1,0:T(8,128)(2,1)}, bf16[96,3072]{1,0:T(8,128)(2,1)S(1)}, u32[]{:S(2)}, u32[]{:S(2)}) %collective-permute-start.1) | collective-permute-done | bytes 589856 | tf_op jit(solution)/shard_map/ppermute | solution.py:191
  25.0 4.6 %all-to-all-start = ((bf16[8,6,128,384]{3,2,1,0:T(8,128)(2,1)}), bf16[8,6,128,384]{3,2,1,0:T(8,128)(2,1)}, u32[]{:S(2)}, u32[]{:S(2)}) async-start(bf16[8,6,128,384]{3,2,1,0:T(8,128)(2,1)} %pack.1), calls=%async_computation | async-start | bytes 9437184 | tf_op jit(solution)/shard_map/all_to_all | solution.py:215
  30.0 1.2 collective-permute-start.9
  31.2 1.3 collective-permute-start.4
  32.5 1.4 %collective-permute-start.3 = (bf16[96,3072]{1,0:T(8,128)(2,1)S(1)}, bf16[96,3072]{1,0:T(8,128)(2,1)}, u32[]{:S(2)}, u32[]{:S(2)}) collective-permute-start(bf16[96,3072]{1,0:T(8,128)(2,1)S(1)} %collective-permute-done.refs_8_), channel_id=1, source_target_pairs={{0,52},{1,53},{2,54},{3,55},{8,60},{9,61},{10,62},{11,63},{4,16},{... | collective-permute-start | bytes 1769480 | tf_op jit(solution)/shard_map/ppermute | solution.py:191
  33.9 8.6 %collective-permute-done.7.refs_12_ = bf16[96,3072]{1,0:T(8,128)(2,1)S(1)} collective-permute-done((bf16[96,3072]{1,0:T(8,128)(2,1)S(1)}, bf16[96,3072]{1,0:T(8,128)(2,1)S(1)}, u32[]{:S(2)}, u32[]{:S(2)}) %collective-permute-start.7) | collective-permute-done | bytes 589856 | tf_op jit(solution)/shard_map/ppermute | solution.py:191
  42.5 1.8 %collective-permute-start.14 = (bf16[96,3072]{1,0:T(8,128)(2,1)S(1)}, bf16[96,3072]{1,0:T(8,128)(2,1)S(1)}, u32[]{:S(2)}, u32[]{:S(2)}) collective-permute-start(bf16[96,3072]{1,0:T(8,128)(2,1)S(1)} %collective-permute-done.7.refs_12_), channel_id=1, source_target_pairs={{0,192},{1,193},{2,194},{3,195},{8,200},{9,201},{10,202},{11,203},... | collective-permute-start | bytes 1769480 | tf_op jit(solution)/shard_map/ppermute | solution.py:191
  44.3 12.4 %collective-permute-done.5.refs_6_ = bf16[96,3072]{1,0:T(8,128)(2,1)S(1)} collective-permute-done((bf16[96,3072]{1,0:T(8,128)(2,1)S(1)}, bf16[96,3072]{1,0:T(8,128)(2,1)S(1)}, u32[]{:S(2)}, u32[]{:S(2)}) %collective-permute-start.5) | collective-permute-done | bytes 589856 | tf_op jit(solution)/shard_map/ppermute | solution.py:191
  56.7 3.0 %collective-permute-start.13 = (bf16[96,3072]{1,0:T(8,128)(2,1)S(1)}, bf16[96,3072]{1,0:T(8,128)(2,1)S(1)}, u32[]{:S(2)}, u32[]{:S(2)}) collective-permute-start(bf16[96,3072]{1,0:T(8,128)(2,1)S(1)} %collective-permute-done.5.refs_6_), channel_id=1, source_target_pairs={{0,8},{1,9},{2,10},{3,11},{8,0},{9,1},{10,2},{11,3},{4,12},{5,13},... | collective-permute-start | bytes 1769480 | tf_op jit(solution)/shard_map/ppermute | solution.py:191
  59.7 2.7 %collective-permute-start.8 = (bf16[96,3072]{1,0:T(8,128)(2,1)}, bf16[96,3072]{1,0:T(8,128)(2,1)}, u32[]{:S(2)}, u32[]{:S(2)}) collective-permute-start(bf16[96,3072]{1,0:T(8,128)(2,1)} %collective-permute-done.4.refs_16_), channel_id=1, source_target_pairs={{0,192},{1,193},{2,194},{3,195},{8,200},{9,201},{10,202},{11,203},... | collective-permute-start | bytes 1769480 | tf_op jit(solution)/shard_map/ppermute | solution.py:191
  62.4 1.5 %collective-permute-start.12 = (bf16[96,3072]{1,0:T(8,128)(2,1)S(1)}, bf16[96,3072]{1,0:T(8,128)(2,1)S(1)}, u32[]{:S(2)}, u32[]{:S(2)}) collective-permute-start(bf16[96,3072]{1,0:T(8,128)(2,1)S(1)} %collective-permute-done.2.refs_4_), channel_id=1, source_target_pairs={{0,8},{1,9},{2,10},{3,11},{8,0},{9,1},{10,2},{11,3},{4,12},{5,13},... | collective-permute-start | bytes 1769480 | tf_op jit(solution)/shard_map/ppermute | solution.py:191
  64.5 11.3 %collective-permute-done.6.refs_18_ = bf16[96,3072]{1,0:T(8,128)(2,1)} collective-permute-done((bf16[96,3072]{1,0:T(8,128)(2,1)}, bf16[96,3072]{1,0:T(8,128)(2,1)}, u32[]{:S(2)}, u32[]{:S(2)}) %collective-permute-start.6) | collective-permute-done | bytes 589856 | tf_op jit(solution)/shard_map/ppermute | solution.py:191
  75.7 1.3 collective-permute-start.17
  77.8 0.8 collective-permute-done.17.refs_13_
  79.0 1.3 collective-permute-done.15.refs_9_
  80.3 1.0 collective-permute-start.26
  83.3 0.8 all-to-all-done.in_ref
  84.1 11.6 %attend.1 = bf16[8,2,128,384]{3,2,1,0:T(8,128)(2,1)} custom-call(bf16[8,6,128,384]{3,2,1,0:T(8,128)(2,1)} %all-to-all-done.in_ref), custom_call_target="tpu_custom_call" | custom-call | flops 4831838208 | bytes 6291456 | tf_op jit(solution)/shard_map/attend/pallas_call | solution.py:102
  96.8 4.2 %all-to-all-start.1 = ((bf16[8,2,128,384]{3,2,1,0:T(8,128)(2,1)}), bf16[8,2,128,384]{3,2,1,0:T(8,128)(2,1)S(1)}, u32[]{:S(2)}, u32[]{:S(2)}) async-start(bf16[8,2,128,384]{3,2,1,0:T(8,128)(2,1)} %attend.1), calls=%async_computation.1 | async-start | bytes 3145728 | tf_op jit(solution)/shard_map/all_to_all | solution.py:251
  101.7 2.2 %collective-permute-start.29 = (bf16[96,3072]{1,0:T(8,128)(2,1)S(1)}, bf16[96,3072]{1,0:T(8,128)(2,1)S(1)}, u32[]{:S(2)}, u32[]{:S(2)}) collective-permute-start(bf16[96,3072]{1,0:T(8,128)(2,1)S(1)} %collective-permute-done.26.refs_28_), channel_id=1, source_target_pairs={{0,192},{1,193},{2,194},{3,195},{8,200},{9,201},{10,202},{11,203},... | collective-permute-start | bytes 1769480 | tf_op jit(solution)/shard_map/ppermute | solution.py:191
  104.6 11.6 %collective-permute-done.29.refs_30_ = bf16[96,3072]{1,0:T(8,128)(2,1)S(1)} collective-permute-done((bf16[96,3072]{1,0:T(8,128)(2,1)S(1)}, bf16[96,3072]{1,0:T(8,128)(2,1)S(1)}, u32[]{:S(2)}, u32[]{:S(2)}) %collective-permute-start.29) | collective-permute-done | bytes 589856 | tf_op jit(solution)/shard_map/ppermute | solution.py:191
  116.2 1.3 collective-permute-start.30
  117.5 3.4 %collective-permute-done.25.refs_26_ = bf16[96,3072]{1,0:T(8,128)(2,1)S(1)} collective-permute-done((bf16[96,3072]{1,0:T(8,128)(2,1)}, bf16[96,3072]{1,0:T(8,128)(2,1)S(1)}, u32[]{:S(2)}, u32[]{:S(2)}) %collective-permute-start.25) | collective-permute-done | bytes 589856 | tf_op jit(solution)/shard_map/ppermute | solution.py:191
  121.8 0.9 copy-done.26
  122.7 0.8 collective-permute-done.28.refs_27_
  123.5 1.2 copy-done
  124.7 10.8 %project.1 = (bf16[1,128,3072]{2,1,0:T(8,128)(2,1)}, bf16[1,128,3072]{2,1,0:T(8,128)(2,1)}) custom-call(s32[32]{0:T(128)} %stack.131.place_ref, bf16[96,3072]{1,0:T(8,128)(2,1)} %refs_0_.3, bf16[96,3072]{1,0:T(8,128)(2,1)} %copy-done.12, bf16[96,3072]{1,0:T(8,128)(2,1)} %copy-done.4, bf16[96,3072]{1,0:T(8,128)(2,1)} %copy-done.10, ...), custom_call_target="tpu_custom_call" | custom-call | flops 4831838208 | bytes 18874368 | tf_op jit(solution)/shard_map/project/pallas_call | solution.py:166
  (92 shorter events, 7.3 us)
Async XLA Ops:
  0.6 19.2 %collective-permute-start = (bf16[96,3072]{1,0:T(8,128)(2,1)}, bf16[96,3072]{1,0:T(8,128)(2,1)S(1)}, u32[]{:S(2)}, u32[]{:S(2)}) collective-permute-start(bf16[96,3072]{1,0:T(8,128)(2,1)} %refs_0_.3), channel_id=1, source_target_pairs={{0,48},{1,49},{2,50},{3,51},{8,56},{9,57},{10,58},{11,59},{4,20},{... | collective-permute-start | bytes 1769480 | tf_op jit(solution)/shard_map/ppermute | solution.py:191
  7.6 14.5 %collective-permute-start.2 = (bf16[96,3072]{1,0:T(8,128)(2,1)}, bf16[96,3072]{1,0:T(8,128)(2,1)S(1)}, u32[]{:S(2)}, u32[]{:S(2)}) collective-permute-start(bf16[96,3072]{1,0:T(8,128)(2,1)} %refs_0_.3), channel_id=1, source_target_pairs={{0,192},{1,193},{2,194},{3,195},{8,200},{9,201},{10,202},{11,203},... | collective-permute-start | bytes 1769480 | tf_op jit(solution)/shard_map/ppermute | solution.py:191
  10.0 15.0 %collective-permute-start.1 = (bf16[96,3072]{1,0:T(8,128)(2,1)}, bf16[96,3072]{1,0:T(8,128)(2,1)S(1)}, u32[]{:S(2)}, u32[]{:S(2)}) collective-permute-start(bf16[96,3072]{1,0:T(8,128)(2,1)} %refs_0_.3), channel_id=1, source_target_pairs={{0,64},{1,65},{2,66},{3,67},{8,72},{9,73},{10,74},{11,75},{4,68},{... | collective-permute-start | bytes 1769480 | tf_op jit(solution)/shard_map/ppermute | solution.py:191
  25.0 59.1 %all-to-all-start = ((bf16[8,6,128,384]{3,2,1,0:T(8,128)(2,1)}), bf16[8,6,128,384]{3,2,1,0:T(8,128)(2,1)}, u32[]{:S(2)}, u32[]{:S(2)}) async-start(bf16[8,6,128,384]{3,2,1,0:T(8,128)(2,1)} %pack.1), calls=%async_computation | async-start | bytes 9437184 | tf_op jit(solution)/shard_map/all_to_all | solution.py:215
  29.7 12.8 %collective-permute-start.7 = (bf16[96,3072]{1,0:T(8,128)(2,1)S(1)}, bf16[96,3072]{1,0:T(8,128)(2,1)S(1)}, u32[]{:S(2)}, u32[]{:S(2)}) collective-permute-start(bf16[96,3072]{1,0:T(8,128)(2,1)S(1)} %collective-permute-done.refs_8_), channel_id=1, source_target_pairs={{0,192},{1,193},{2,194},{3,195},{8,200},{9,201},{10,202},{11,203},... | collective-permute-start | bytes 1769480 | tf_op jit(solution)/shard_map/ppermute | solution.py:191
  30.0 14.3 %collective-permute-start.9 = (bf16[96,3072]{1,0:T(8,128)(2,1)S(1)}, bf16[96,3072]{1,0:T(8,128)(2,1)S(1)}, u32[]{:S(2)}, u32[]{:S(2)}) collective-permute-start(bf16[96,3072]{1,0:T(8,128)(2,1)S(1)} %collective-permute-done.refs_8_), channel_id=1, source_target_pairs={{0,64},{1,65},{2,66},{3,67},{8,72},{9,73},{10,74},{11,75},{4,68},{... | collective-permute-start | bytes 1769480 | tf_op jit(solution)/shard_map/ppermute | solution.py:191
  31.2 25.5 %collective-permute-start.5 = (bf16[96,3072]{1,0:T(8,128)(2,1)S(1)}, bf16[96,3072]{1,0:T(8,128)(2,1)S(1)}, u32[]{:S(2)}, u32[]{:S(2)}) collective-permute-start(bf16[96,3072]{1,0:T(8,128)(2,1)S(1)} %collective-permute-done.1.refs_2_), channel_id=1, source_target_pairs={{0,64},{1,65},{2,66},{3,67},{8,72},{9,73},{10,74},{11,75},{4,68},{... | collective-permute-start | bytes 1769480 | tf_op jit(solution)/shard_map/ppermute | solution.py:191
  31.2 28.5 %collective-permute-start.4 = (bf16[96,3072]{1,0:T(8,128)(2,1)S(1)}, bf16[96,3072]{1,0:T(8,128)(2,1)}, u32[]{:S(2)}, u32[]{:S(2)}) collective-permute-start(bf16[96,3072]{1,0:T(8,128)(2,1)S(1)} %copy-done.1), channel_id=1, source_target_pairs={{0,52},{1,53},{2,54},{3,55},{8,60},{9,61},{10,62},{11,63},{4,16},{... | collective-permute-start | bytes 1769480 | tf_op jit(solution)/shard_map/ppermute | solution.py:191
  32.5 27.2 %collective-permute-start.3 = (bf16[96,3072]{1,0:T(8,128)(2,1)S(1)}, bf16[96,3072]{1,0:T(8,128)(2,1)}, u32[]{:S(2)}, u32[]{:S(2)}) collective-permute-start(bf16[96,3072]{1,0:T(8,128)(2,1)S(1)} %collective-permute-done.refs_8_), channel_id=1, source_target_pairs={{0,52},{1,53},{2,54},{3,55},{8,60},{9,61},{10,62},{11,63},{4,16},{... | collective-permute-start | bytes 1769480 | tf_op jit(solution)/shard_map/ppermute | solution.py:191
  42.5 19.9 %collective-permute-start.14 = (bf16[96,3072]{1,0:T(8,128)(2,1)S(1)}, bf16[96,3072]{1,0:T(8,128)(2,1)S(1)}, u32[]{:S(2)}, u32[]{:S(2)}) collective-permute-start(bf16[96,3072]{1,0:T(8,128)(2,1)S(1)} %collective-permute-done.7.refs_12_), channel_id=1, source_target_pairs={{0,192},{1,193},{2,194},{3,195},{8,200},{9,201},{10,202},{11,203},... | collective-permute-start | bytes 1769480 | tf_op jit(solution)/shard_map/ppermute | solution.py:191
  56.7 7.3 %collective-permute-start.13 = (bf16[96,3072]{1,0:T(8,128)(2,1)S(1)}, bf16[96,3072]{1,0:T(8,128)(2,1)S(1)}, u32[]{:S(2)}, u32[]{:S(2)}) collective-permute-start(bf16[96,3072]{1,0:T(8,128)(2,1)S(1)} %collective-permute-done.5.refs_6_), channel_id=1, source_target_pairs={{0,8},{1,9},{2,10},{3,11},{8,0},{9,1},{10,2},{11,3},{4,12},{5,13},... | collective-permute-start | bytes 1769480 | tf_op jit(solution)/shard_map/ppermute | solution.py:191
  59.6 4.4 %collective-permute-start.11 = (bf16[96,3072]{1,0:T(8,128)(2,1)S(1)}, bf16[96,3072]{1,0:T(8,128)(2,1)S(1)}, u32[]{:S(2)}, u32[]{:S(2)}) collective-permute-start(bf16[96,3072]{1,0:T(8,128)(2,1)S(1)} %collective-permute-done.1.refs_2_), channel_id=1, source_target_pairs={{0,8},{1,9},{2,10},{3,11},{8,0},{9,1},{10,2},{11,3},{4,12},{5,13},... | collective-permute-start | bytes 1769480 | tf_op jit(solution)/shard_map/ppermute | solution.py:191
  59.7 16.0 %collective-permute-start.6 = (bf16[96,3072]{1,0:T(8,128)(2,1)}, bf16[96,3072]{1,0:T(8,128)(2,1)}, u32[]{:S(2)}, u32[]{:S(2)}) collective-permute-start(bf16[96,3072]{1,0:T(8,128)(2,1)} %collective-permute-done.4.refs_16_), channel_id=1, source_target_pairs={{0,64},{1,65},{2,66},{3,67},{8,72},{9,73},{10,74},{11,75},{4,68},{... | collective-permute-start | bytes 1769480 | tf_op jit(solution)/shard_map/ppermute | solution.py:191
  59.7 17.3 %collective-permute-start.8 = (bf16[96,3072]{1,0:T(8,128)(2,1)}, bf16[96,3072]{1,0:T(8,128)(2,1)}, u32[]{:S(2)}, u32[]{:S(2)}) collective-permute-start(bf16[96,3072]{1,0:T(8,128)(2,1)} %collective-permute-done.4.refs_16_), channel_id=1, source_target_pairs={{0,192},{1,193},{2,194},{3,195},{8,200},{9,201},{10,202},{11,203},... | collective-permute-start | bytes 1769480 | tf_op jit(solution)/shard_map/ppermute | solution.py:191
  62.4 14.9 %collective-permute-start.12 = (bf16[96,3072]{1,0:T(8,128)(2,1)S(1)}, bf16[96,3072]{1,0:T(8,128)(2,1)S(1)}, u32[]{:S(2)}, u32[]{:S(2)}) collective-permute-start(bf16[96,3072]{1,0:T(8,128)(2,1)S(1)} %collective-permute-done.2.refs_4_), channel_id=1, source_target_pairs={{0,8},{1,9},{2,10},{3,11},{8,0},{9,1},{10,2},{11,3},{4,12},{5,13},... | collective-permute-start | bytes 1769480 | tf_op jit(solution)/shard_map/ppermute | solution.py:191
  64.0 13.6 %collective-permute-start.10 = (bf16[96,3072]{1,0:T(8,128)(2,1)S(1)}, bf16[96,3072]{1,0:T(8,128)(2,1)S(1)}, u32[]{:S(2)}, u32[]{:S(2)}) collective-permute-start(bf16[96,3072]{1,0:T(8,128)(2,1)S(1)} %copy-done.1), channel_id=1, source_target_pairs={{0,8},{1,9},{2,10},{3,11},{8,0},{9,1},{10,2},{11,3},{4,12},{5,13},... | collective-permute-start | bytes 1769480 | tf_op jit(solution)/shard_map/ppermute | solution.py:191
  64.1 13.7 %collective-permute-start.16 = (bf16[96,3072]{1,0:T(8,128)(2,1)S(1)}, bf16[96,3072]{1,0:T(8,128)(2,1)S(1)}, u32[]{:S(2)}, u32[]{:S(2)}) collective-permute-start(bf16[96,3072]{1,0:T(8,128)(2,1)S(1)} %collective-permute-done.9.refs_10_), channel_id=1, source_target_pairs={{0,8},{1,9},{2,10},{3,11},{8,0},{9,1},{10,2},{11,3},{4,12},{5,13},... | collective-permute-start | bytes 1769480 | tf_op jit(solution)/shard_map/ppermute | solution.py:191
  75.7 2.9 %collective-permute-start.17 = (bf16[96,3072]{1,0:T(8,128)(2,1)S(1)}, bf16[96,3072]{1,0:T(8,128)(2,1)S(1)}, u32[]{:S(2)}, u32[]{:S(2)}) collective-permute-start(bf16[96,3072]{1,0:T(8,128)(2,1)S(1)} %collective-permute-done.7.refs_12_), channel_id=1, source_target_pairs={{0,8},{1,9},{2,10},{3,11},{8,0},{9,1},{10,2},{11,3},{4,12},{5,13},... | collective-permute-start | bytes 1769480 | tf_op jit(solution)/shard_map/ppermute | solution.py:191
  77.0 3.3 %collective-permute-start.15 = (bf16[96,3072]{1,0:T(8,128)(2,1)S(1)}, bf16[96,3072]{1,0:T(8,128)(2,1)S(1)}, u32[]{:S(2)}, u32[]{:S(2)}) collective-permute-start(bf16[96,3072]{1,0:T(8,128)(2,1)S(1)} %collective-permute-done.refs_8_), channel_id=1, source_target_pairs={{0,8},{1,9},{2,10},{3,11},{8,0},{9,1},{10,2},{11,3},{4,12},{5,13},... | collective-permute-start | bytes 1769480 | tf_op jit(solution)/shard_map/ppermute | solution.py:191
  77.3 4.7 %collective-permute-start.18 = (bf16[96,3072]{1,0:T(8,128)(2,1)S(1)}, bf16[96,3072]{1,0:T(8,128)(2,1)S(1)}, u32[]{:S(2)}, u32[]{:S(2)}) collective-permute-start(bf16[96,3072]{1,0:T(8,128)(2,1)S(1)} %collective-permute-done.14.refs_14_), channel_id=1, source_target_pairs={{0,8},{1,9},{2,10},{3,11},{8,0},{9,1},{10,2},{11,3},{4,12},{5,13},... | collective-permute-start | bytes 1769480 | tf_op jit(solution)/shard_map/ppermute | solution.py:191
  77.5 18.1 %collective-permute-start.21 = (bf16[96,3072]{1,0:T(8,128)(2,1)}, bf16[96,3072]{1,0:T(8,128)(2,1)S(1)}, u32[]{:S(2)}, u32[]{:S(2)}) collective-permute-start(bf16[96,3072]{1,0:T(8,128)(2,1)} %collective-permute-done.8.refs_20_), channel_id=1, source_target_pairs={{0,8},{1,9},{2,10},{3,11},{8,0},{9,1},{10,2},{11,3},{4,12},{5,13},... | collective-permute-start | bytes 1769480 | tf_op jit(solution)/shard_map/ppermute | solution.py:191
  77.8 17.9 %collective-permute-start.22 = (bf16[96,3072]{1,0:T(8,128)(2,1)}, bf16[96,3072]{1,0:T(8,128)(2,1)S(1)}, u32[]{:S(2)}, u32[]{:S(2)}) collective-permute-start(bf16[96,3072]{1,0:T(8,128)(2,1)} %collective-permute-done.6.refs_18_), channel_id=1, source_target_pairs={{0,64},{1,65},{2,66},{3,67},{8,72},{9,73},{10,74},{11,75},{4,68},{... | collective-permute-start | bytes 1769480 | tf_op jit(solution)/shard_map/ppermute | solution.py:191
  78.6 17.1 %collective-permute-start.19 = (bf16[96,3072]{1,0:T(8,128)(2,1)}, bf16[96,3072]{1,0:T(8,128)(2,1)S(1)}, u32[]{:S(2)}, u32[]{:S(2)}) collective-permute-start(bf16[96,3072]{1,0:T(8,128)(2,1)} %collective-permute-done.4.refs_16_), channel_id=1, source_target_pairs={{0,8},{1,9},{2,10},{3,11},{8,0},{9,1},{10,2},{11,3},{4,12},{5,13},... | collective-permute-start | bytes 1769480 | tf_op jit(solution)/shard_map/ppermute | solution.py:191
  80.3 15.4 %collective-permute-start.26 = (bf16[96,3072]{1,0:T(8,128)(2,1)}, bf16[96,3072]{1,0:T(8,128)(2,1)S(1)}, u32[]{:S(2)}, u32[]{:S(2)}) collective-permute-start(bf16[96,3072]{1,0:T(8,128)(2,1)} %collective-permute-done.3.refs_24_), channel_id=1, source_target_pairs={{0,192},{1,193},{2,194},{3,195},{8,200},{9,201},{10,202},{11,203},... | collective-permute-start | bytes 1769480 | tf_op jit(solution)/shard_map/ppermute | solution.py:191
  82.0 13.7 %collective-permute-start.20 = (bf16[96,3072]{1,0:T(8,128)(2,1)}, bf16[96,3072]{1,0:T(8,128)(2,1)}, u32[]{:S(2)}, u32[]{:S(2)}) collective-permute-start(bf16[96,3072]{1,0:T(8,128)(2,1)} %collective-permute-done.6.refs_18_), channel_id=1, source_target_pairs={{0,8},{1,9},{2,10},{3,11},{8,0},{9,1},{10,2},{11,3},{4,12},{5,13},... | collective-permute-start | bytes 1769480 | tf_op jit(solution)/shard_map/ppermute | solution.py:191
  96.8 26.7 %all-to-all-start.1 = ((bf16[8,2,128,384]{3,2,1,0:T(8,128)(2,1)}), bf16[8,2,128,384]{3,2,1,0:T(8,128)(2,1)S(1)}, u32[]{:S(2)}, u32[]{:S(2)}) async-start(bf16[8,2,128,384]{3,2,1,0:T(8,128)(2,1)} %attend.1), calls=%async_computation.1 | async-start | bytes 3145728 | tf_op jit(solution)/shard_map/all_to_all | solution.py:251
  100.9 3.7 %collective-permute-start.27 = (bf16[96,3072]{1,0:T(8,128)(2,1)S(1)}, bf16[96,3072]{1,0:T(8,128)(2,1)S(1)}, u32[]{:S(2)}, u32[]{:S(2)}) collective-permute-start(bf16[96,3072]{1,0:T(8,128)(2,1)S(1)} %collective-permute-done.26.refs_28_), channel_id=1, source_target_pairs={{0,8},{1,9},{2,10},{3,11},{8,0},{9,1},{10,2},{11,3},{4,12},{5,13},... | collective-permute-start | bytes 1769480 | tf_op jit(solution)/shard_map/ppermute | solution.py:191
  101.6 3.0 %collective-permute-start.24 = (bf16[96,3072]{1,0:T(8,128)(2,1)}, bf16[96,3072]{1,0:T(8,128)(2,1)S(1)}, u32[]{:S(2)}, u32[]{:S(2)}) collective-permute-start(bf16[96,3072]{1,0:T(8,128)(2,1)} %collective-permute-done.3.refs_24_), channel_id=1, source_target_pairs={{0,8},{1,9},{2,10},{3,11},{8,0},{9,1},{10,2},{11,3},{4,12},{5,13},... | collective-permute-start | bytes 1769480 | tf_op jit(solution)/shard_map/ppermute | solution.py:191
  101.7 14.5 %collective-permute-start.29 = (bf16[96,3072]{1,0:T(8,128)(2,1)S(1)}, bf16[96,3072]{1,0:T(8,128)(2,1)S(1)}, u32[]{:S(2)}, u32[]{:S(2)}) collective-permute-start(bf16[96,3072]{1,0:T(8,128)(2,1)S(1)} %collective-permute-done.26.refs_28_), channel_id=1, source_target_pairs={{0,192},{1,193},{2,194},{3,195},{8,200},{9,201},{10,202},{11,203},... | collective-permute-start | bytes 1769480 | tf_op jit(solution)/shard_map/ppermute | solution.py:191
  103.9 12.3 %collective-permute-start.23 = (bf16[96,3072]{1,0:T(8,128)(2,1)}, bf16[96,3072]{1,0:T(8,128)(2,1)S(1)}, u32[]{:S(2)}, u32[]{:S(2)}) collective-permute-start(bf16[96,3072]{1,0:T(8,128)(2,1)} %copy-done.18), channel_id=1, source_target_pairs={{0,8},{1,9},{2,10},{3,11},{8,0},{9,1},{10,2},{11,3},{4,12},{5,13},... | collective-permute-start | bytes 1769480 | tf_op jit(solution)/shard_map/ppermute | solution.py:191
  104.6 16.4 %collective-permute-start.25 = (bf16[96,3072]{1,0:T(8,128)(2,1)}, bf16[96,3072]{1,0:T(8,128)(2,1)S(1)}, u32[]{:S(2)}, u32[]{:S(2)}) collective-permute-start(bf16[96,3072]{1,0:T(8,128)(2,1)} %collective-permute-done.3.refs_24_), channel_id=1, source_target_pairs={{0,64},{1,65},{2,66},{3,67},{8,72},{9,73},{10,74},{11,75},{4,68},{... | collective-permute-start | bytes 1769480 | tf_op jit(solution)/shard_map/ppermute | solution.py:191
  116.2 5.6 %collective-permute-start.30 = (bf16[96,3072]{1,0:T(8,128)(2,1)S(1)}, bf16[96,3072]{1,0:T(8,128)(2,1)S(1)}, u32[]{:S(2)}, u32[]{:S(2)}) collective-permute-start(bf16[96,3072]{1,0:T(8,128)(2,1)S(1)} %collective-permute-done.29.refs_30_), channel_id=1, source_target_pairs={{0,8},{1,9},{2,10},{3,11},{8,0},{9,1},{10,2},{11,3},{4,12},{5,13},... | collective-permute-start | bytes 1769480 | tf_op jit(solution)/shard_map/ppermute | solution.py:191
  (28 other events, 462.7 us)
